TPU v7x, 32 devices: a whole 2x2x4 slice. The times are simulated.
32 devices in a mesh: replica: 16 (over z, y, x), shard: 2 (over core).
Axes of the slice: x: 2, y: 2, z: 4, core: 2. Of those that a mesh axis runs over, the one named last changes fastest.
Arguments:
- inputs: bfloat16 [6304, 512], P(('replica', 'shard')), may hold values from -6 to 6
- norm1_gain: bfloat16 [512], P('shard'), may hold values from 0.5 to 1.5
- norm1_bias: bfloat16 [512], P('shard'), may hold values from -1.25 to 1.25
- qkv_weight: bfloat16 [512, 1536], P('shard'), may hold values from -0.25 to 0.25
- query_bias: bfloat16 [512], P('shard'), may hold values from -1.25 to 1.25
- value_bias: bfloat16 [512], P('shard'), may hold values from -1.25 to 1.25
- out_weight: bfloat16 [512, 512], P('shard'), may hold values from -0.5 to 0.5
- out_bias: bfloat16 [512], P('shard'), may hold values from -1.25 to 1.25
- norm2_gain: bfloat16 [512], P('shard'), may hold values from 0.5 to 1.5
- norm2_bias: bfloat16 [512], P('shard'), may hold values from -1.25 to 1.25
- router_weight: bfloat16 [512, 4], P('shard'), may hold values from -0.125 to 0.125
- noise: float32 [6304, 4], P(('replica', 'shard')), may hold values from -1.75 to 1.75
- expert_in: bfloat16 [4, 512, 2048], P('shard'), may hold values from -0.25 to 0.25
- expert_in_bias: bfloat16 [4, 2048], P('shard'), may hold values from -0.625 to 0.625
- expert_out: bfloat16 [4, 2048, 512], P('shard'), may hold values from -0.5 to 0.5
- expert_out_bias: bfloat16 [4, 512], P('shard'), may hold values from -1.25 to 1.25
- routes: int32 [6304, 2], P(('replica', 'shard')), may hold values from 0 to 3, all different within a row
- priority: int32 [32, 394], P(('replica', 'shard')), may hold values from 0 to 393, each once within a row
- cotangent: bfloat16 [6304, 512], P(('replica', 'shard')), may hold values from -6 to 6
Outputs:
- output: bfloat16 [6304, 512], P(('replica', 'shard'))
- input_grad: float32 [6304, 512], P(('replica', 'shard'))
- grad_norm1_gain: float32 [512], P('shard')
- grad_norm1_bias: float32 [512], P('shard')
- grad_qkv_weight: float32 [512, 1536], P('shard')
- grad_query_bias: float32 [512], P('shard')
- grad_value_bias: float32 [512], P('shard')
- grad_out_weight: float32 [512, 512], P('shard')
- grad_out_bias: float32 [512], P('shard')
- grad_norm2_gain: float32 [512], P('shard')
- grad_norm2_bias: float32 [512], P('shard')
- grad_router_weight: float32 [512, 4], P('shard')
- grad_expert_in: float32 [4, 512, 2048], P('shard')
- grad_expert_in_bias: float32 [4, 2048], P('shard')
- grad_expert_out: float32 [4, 2048, 512], P('shard')
- grad_expert_out_bias: float32 [4, 512], P('shard')
Inputs may be any that keep to these rules, and one draw needn't show every extreme that they name: `routes`: each token names two different experts; every expert is named by some token. `priority`: each row is a permutation; it ranks the pairs of the tokens of the device of that row, pair 2 t + k being token t's k-th route.
All inputs are finite; a program needn't handle non-finite values.
Results may differ from a plain program's by a relative error of at most 0.017.
Values may be sent and summed in bfloat16 or wider, within the bound.
A program may use at most 192 MiB of HBM per device.

v0:
```python
import jax
import jax.numpy as jnp
from jax import lax
from jax.sharding import PartitionSpec as P

HEAD_DIM = 64
PATCHES = 197


LN_EPS = 1e-06


def entering(x, axis, combine, identity):
    peers, position = (lax.axis_size(axis), lax.axis_index(axis))
    everything = lax.all_gather(x, axis)
    start = jnp.broadcast_to(jnp.asarray(identity, x.dtype), x.shape)

    def turn(k, before):
        reached = k < position
        new = combine(before, everything[k])
        return jnp.where(reached, new, before)

    return lax.fori_loop(0, peers, turn, start)


def to_half(values):
    return values.astype(jnp.bfloat16)


def layer_norm(values, gain_vector, bias_vector):
    centered = values - jnp.mean(values, axis=-1, keepdims=True)
    spread = lax.rsqrt(jnp.mean(centered * centered, axis=-1, keepdims=True) + LN_EPS)
    return centered * spread * gain_vector + bias_vector


def kept_gates(pair_expert, ranks, offsets, capacity, expert_count):
    same = pair_expert[:, None] == pair_expert[None, :]
    earlier = ranks[None, :] < ranks[:, None]
    before = jnp.sum(jnp.where(same & earlier, 1, 0).astype(jnp.int32), axis=1)
    onehot = pair_expert[:, None] == jnp.arange(expert_count, dtype=jnp.int32)[None, :]
    first_slot = jnp.sum(jnp.where(onehot, offsets[None, :], 0).astype(jnp.int32), axis=1)
    keep = before + first_slot < capacity
    picked = jnp.where(onehot & keep[:, None], 1.0, 0.0).astype(jnp.float32)
    return jnp.sum(picked.reshape(-1, 2, expert_count), axis=1)


def add_counts(earlier, later):
    return earlier + later


def expert_apply(rows_half, gate_column, weight_in, bias_in, weight_out, bias_out):
    pre_act = jnp.dot(rows_half, weight_in, preferred_element_type=jnp.float32) + bias_in.astype(
        jnp.float32
    )
    hidden = to_half(jax.nn.gelu(pre_act))
    result = jnp.dot(hidden, weight_out, preferred_element_type=jnp.float32) + bias_out.astype(
        jnp.float32
    )
    return gate_column * result


def expert_back(rows_half, gate_column, upstream, weight_in, bias_in, weight_out, bias_out):
    pre_act = jnp.dot(rows_half, weight_in, preferred_element_type=jnp.float32) + bias_in.astype(
        jnp.float32
    )
    activated, gelu_back = jax.vjp(jax.nn.gelu, pre_act)
    hidden = to_half(activated)
    result = jnp.dot(hidden, weight_out, preferred_element_type=jnp.float32) + bias_out.astype(
        jnp.float32
    )
    d_result = to_half(gate_column * upstream)
    d_gate = jnp.sum(upstream * result, axis=1)
    grad_out = jnp.einsum("th,td->hd", hidden, d_result, preferred_element_type=jnp.float32)
    grad_out_bias = jnp.sum(d_result.astype(jnp.float32), axis=0)
    d_hidden = jnp.einsum("td,hd->th", d_result, weight_out, preferred_element_type=jnp.float32)
    d_pre = to_half(gelu_back(d_hidden)[0])
    grad_in = jnp.einsum("td,th->dh", rows_half, d_pre, preferred_element_type=jnp.float32)
    grad_in_bias = jnp.sum(d_pre.astype(jnp.float32), axis=0)
    d_rows = jnp.einsum("th,dh->td", d_pre, weight_in, preferred_element_type=jnp.float32)
    return (d_rows, d_gate, grad_in, grad_in_bias, grad_out, grad_out_bias)


def on_device(
    inputs,
    norm1_gain,
    norm1_bias,
    qkv_weight,
    query_bias,
    value_bias,
    out_weight,
    out_bias,
    norm2_gain,
    norm2_bias,
    router_weight,
    noise,
    expert_in,
    expert_in_bias,
    expert_out,
    expert_out_bias,
    routes,
    priority,
    cotangent,
):
    dense = (
        lax.all_gather(norm1_gain, "shard", axis=0, tiled=True),
        lax.all_gather(norm1_bias, "shard", axis=0, tiled=True),
        lax.all_gather(qkv_weight, "shard", axis=0, tiled=True),
        lax.all_gather(query_bias, "shard", axis=0, tiled=True),
        lax.all_gather(value_bias, "shard", axis=0, tiled=True),
        lax.all_gather(out_weight, "shard", axis=0, tiled=True),
        lax.all_gather(out_bias, "shard", axis=0, tiled=True),
        lax.all_gather(norm2_gain, "shard", axis=0, tiled=True),
        lax.all_gather(norm2_bias, "shard", axis=0, tiled=True),
        lax.all_gather(router_weight, "shard", axis=0, tiled=True),
    )
    (
        gain_one,
        bias_one,
        weight_qkv,
        bias_query,
        bias_value,
        weight_proj,
        bias_proj,
        gain_two,
        bias_two,
        weight_route,
    ) = dense
    width = inputs.shape[1]
    tok_count = inputs.shape[0]
    images = tok_count // PATCHES
    heads = width // HEAD_DIM
    expert_count = weight_route.shape[1]
    score_scale = HEAD_DIM ** (-0.5)
    pair_expert = routes.reshape(-1)
    onehot_pairs = (
        pair_expert[:, None] == jnp.arange(expert_count, dtype=jnp.int32)[None, :]
    ).astype(jnp.int32)
    expert_load = jnp.sum(onehot_pairs, axis=0)
    offsets = entering(expert_load, ("replica", "shard"), add_counts, jnp.zeros_like(expert_load))
    capacity = 2 * tok_count * lax.axis_size("replica") * lax.axis_size("shard") // expert_count
    chosen = kept_gates(pair_expert, priority.reshape(-1), offsets, capacity, expert_count)
    residual_in = inputs.astype(jnp.float32)
    normed_one, norm_one_back = jax.vjp(
        layer_norm, residual_in, gain_one.astype(jnp.float32), bias_one.astype(jnp.float32)
    )
    normed_one_half = to_half(normed_one)
    qkv_bias = jnp.concatenate([bias_query, jnp.zeros_like(bias_query), bias_value]).astype(
        jnp.float32
    )
    mixed = to_half(
        jnp.dot(normed_one_half, weight_qkv, preferred_element_type=jnp.float32) + qkv_bias
    )
    shaped = mixed.reshape(images, PATCHES, 3, heads, HEAD_DIM)
    query, keys, values = (shaped[:, :, 0], shaped[:, :, 1], shaped[:, :, 2])
    scores = (
        jnp.einsum("bqhd,bkhd->bhqk", query, keys, preferred_element_type=jnp.float32) * score_scale
    )
    row_max = jnp.max(scores, axis=-1, keepdims=True)
    log_total = row_max + jnp.log(jnp.sum(jnp.exp(scores - row_max), axis=-1, keepdims=True))
    context = jnp.einsum(
        "bhqk,bkhd->bqhd",
        to_half(jnp.exp(scores - log_total)),
        values,
        preferred_element_type=jnp.float32,
    )
    context_half = to_half(context.reshape(tok_count, width))
    branch = jnp.dot(
        context_half, weight_proj, preferred_element_type=jnp.float32
    ) + bias_proj.astype(jnp.float32)
    middle = residual_in + branch
    normed_two, norm_two_back = jax.vjp(
        layer_norm, middle, gain_two.astype(jnp.float32), bias_two.astype(jnp.float32)
    )
    normed_two_half = to_half(normed_two)
    logits = jnp.dot(normed_two_half, weight_route, preferred_element_type=jnp.float32) + noise
    route_probs = jax.nn.softmax(logits, axis=-1)
    gate_weights = route_probs * chosen
    upstream = cotangent.astype(jnp.float32)
    running = jnp.zeros((tok_count, width), jnp.float32)
    portion = (
        lax.all_gather(expert_in, "shard", axis=0, tiled=True),
        lax.all_gather(expert_in_bias, "shard", axis=0, tiled=True),
        lax.all_gather(expert_out, "shard", axis=0, tiled=True),
        lax.all_gather(expert_out_bias, "shard", axis=0, tiled=True),
    )
    for local_index in range(portion[0].shape[0]):
        column = lax.dynamic_slice_in_dim(gate_weights, local_index, 1, 1)
        running = running + expert_apply(
            normed_two_half,
            column,
            portion[0][local_index],
            portion[1][local_index],
            portion[2][local_index],
            portion[3][local_index],
        )
    gathered = (
        lax.all_gather(expert_in, "shard", axis=0, tiled=True),
        lax.all_gather(expert_in_bias, "shard", axis=0, tiled=True),
        lax.all_gather(expert_out, "shard", axis=0, tiled=True),
        lax.all_gather(expert_out_bias, "shard", axis=0, tiled=True),
    )
    d_normed = jnp.zeros((tok_count, width), jnp.float32)
    gate_columns = []
    collected = ([], [], [], [])
    for expert_index in range(gathered[0].shape[0]):
        pieces = expert_back(
            normed_two_half,
            gate_weights[:, expert_index : expert_index + 1],
            upstream,
            gathered[0][expert_index],
            gathered[1][expert_index],
            gathered[2][expert_index],
            gathered[3][expert_index],
        )
        d_normed = d_normed + pieces[0]
        gate_columns.append(pieces[1])
        for member in range(4):
            collected[member].append(pieces[member + 2])
    d_gates = jnp.stack(gate_columns, axis=1)
    expert_grads = (
        lax.psum_scatter(
            jnp.stack(collected[0], axis=0).astype(jnp.bfloat16),
            "shard",
            scatter_dimension=0,
            tiled=True,
        ).astype(jnp.float32),
        lax.psum_scatter(
            jnp.stack(collected[1], axis=0).astype(jnp.bfloat16),
            "shard",
            scatter_dimension=0,
            tiled=True,
        ).astype(jnp.float32),
        lax.psum_scatter(
            jnp.stack(collected[2], axis=0).astype(jnp.bfloat16),
            "shard",
            scatter_dimension=0,
            tiled=True,
        ).astype(jnp.float32),
        lax.psum_scatter(
            jnp.stack(collected[3], axis=0).astype(jnp.bfloat16),
            "shard",
            scatter_dimension=0,
            tiled=True,
        ).astype(jnp.float32),
    )
    output = to_half(middle + running)
    d_probs = d_gates * chosen
    d_logits = to_half(
        route_probs * (d_probs - jnp.sum(route_probs * d_probs, axis=-1, keepdims=True))
    )
    grad_route = jnp.einsum(
        "td,te->de", normed_two_half, d_logits, preferred_element_type=jnp.float32
    )
    d_normed = d_normed + jnp.einsum(
        "te,de->td", d_logits, weight_route, preferred_element_type=jnp.float32
    )
    d_middle, grad_gain_two, grad_bias_two = norm_two_back(d_normed)
    d_middle = d_middle + upstream
    d_branch = to_half(d_middle)
    grad_proj = jnp.einsum("tc,td->cd", context_half, d_branch, preferred_element_type=jnp.float32)
    grad_proj_bias = jnp.sum(d_branch.astype(jnp.float32), axis=0)
    d_context = to_half(
        jnp.einsum("td,cd->tc", d_branch, weight_proj, preferred_element_type=jnp.float32)
    )
    d_context = d_context.reshape(images, PATCHES, heads, HEAD_DIM)
    scores = (
        jnp.einsum("bqhd,bkhd->bhqk", query, keys, preferred_element_type=jnp.float32) * score_scale
    )
    attn_probs = jnp.exp(scores - log_total)
    d_attn = jnp.einsum("bqhd,bkhd->bhqk", d_context, values, preferred_element_type=jnp.float32)
    d_values = jnp.einsum(
        "bhqk,bqhd->bkhd", to_half(attn_probs), d_context, preferred_element_type=jnp.float32
    )
    d_scores = to_half(attn_probs * (d_attn - jnp.sum(attn_probs * d_attn, axis=-1, keepdims=True)))
    d_query = (
        jnp.einsum("bhqk,bkhd->bqhd", d_scores, keys, preferred_element_type=jnp.float32)
        * score_scale
    )
    d_keys = (
        jnp.einsum("bhqk,bqhd->bkhd", d_scores, query, preferred_element_type=jnp.float32)
        * score_scale
    )
    d_mixed = to_half(jnp.stack([d_query, d_keys, d_values], axis=2).reshape(tok_count, 3 * width))
    grad_qkv = jnp.einsum("td,tf->df", normed_one_half, d_mixed, preferred_element_type=jnp.float32)
    mixed_sums = jnp.sum(d_mixed.astype(jnp.float32), axis=0)
    grad_query = mixed_sums[:width]
    grad_value = mixed_sums[2 * width :]
    d_normed_one = jnp.einsum("tf,df->td", d_mixed, weight_qkv, preferred_element_type=jnp.float32)
    d_input, grad_gain_one, grad_bias_one = norm_one_back(d_normed_one)
    input_grad = d_input + d_middle
    dense_grads = (
        lax.psum_scatter(
            grad_gain_one.astype(jnp.bfloat16), "shard", scatter_dimension=0, tiled=True
        ).astype(jnp.float32),
        lax.psum_scatter(
            grad_bias_one.astype(jnp.bfloat16), "shard", scatter_dimension=0, tiled=True
        ).astype(jnp.float32),
        lax.psum_scatter(
            grad_qkv.astype(jnp.bfloat16), "shard", scatter_dimension=0, tiled=True
        ).astype(jnp.float32),
        lax.psum_scatter(
            grad_query.astype(jnp.bfloat16), "shard", scatter_dimension=0, tiled=True
        ).astype(jnp.float32),
        lax.psum_scatter(
            grad_value.astype(jnp.bfloat16), "shard", scatter_dimension=0, tiled=True
        ).astype(jnp.float32),
        lax.psum_scatter(
            grad_proj.astype(jnp.bfloat16), "shard", scatter_dimension=0, tiled=True
        ).astype(jnp.float32),
        lax.psum_scatter(
            grad_proj_bias.astype(jnp.bfloat16), "shard", scatter_dimension=0, tiled=True
        ).astype(jnp.float32),
        lax.psum_scatter(
            grad_gain_two.astype(jnp.bfloat16), "shard", scatter_dimension=0, tiled=True
        ).astype(jnp.float32),
        lax.psum_scatter(
            grad_bias_two.astype(jnp.bfloat16), "shard", scatter_dimension=0, tiled=True
        ).astype(jnp.float32),
        lax.psum_scatter(
            grad_route.astype(jnp.bfloat16), "shard", scatter_dimension=0, tiled=True
        ).astype(jnp.float32),
    )
    summed = lax.psum(
        (
            dense_grads[0],
            dense_grads[1],
            dense_grads[2],
            dense_grads[3],
            dense_grads[4],
            dense_grads[5],
            dense_grads[6],
            dense_grads[7],
            dense_grads[8],
            dense_grads[9],
            expert_grads[0],
            expert_grads[1],
            expert_grads[2],
            expert_grads[3],
        ),
        "replica",
    )
    return (
        output,
        input_grad,
        summed[0],
        summed[1],
        summed[2],
        summed[3],
        summed[4],
        summed[5],
        summed[6],
        summed[7],
        summed[8],
        summed[9],
        summed[10],
        summed[11],
        summed[12],
        summed[13],
    )


def solution(mesh):
    return jax.shard_map(
        on_device,
        mesh=mesh,
        in_specs=(
            P(("replica", "shard"), None),
            P("shard"),
            P("shard"),
            P("shard", None),
            P("shard"),
            P("shard"),
            P("shard", None),
            P("shard"),
            P("shard"),
            P("shard"),
            P("shard", None),
            P(("replica", "shard"), None),
            P("shard", None, None),
            P("shard", None),
            P("shard", None, None),
            P("shard", None),
            P(("replica", "shard"), None),
            P(("replica", "shard"), None),
            P(("replica", "shard"), None),
        ),
        out_specs=(
            P(("replica", "shard"), None),
            P(("replica", "shard"), None),
            P("shard"),
            P("shard"),
            P("shard", None),
            P("shard"),
            P("shard"),
            P("shard", None),
            P("shard"),
            P("shard"),
            P("shard"),
            P("shard", None),
            P("shard", None, None),
            P("shard", None),
            P("shard", None, None),
            P("shard", None),
        ),
        check_vma=False,
    )
```

profile of v0, /device:TPU:0, one launch (start us, length us, event | category | flops | bytes accessed | tf_op | source)
XLA Modules:
  0.0 980.8 jit_solution(1298103572640503789)
XLA Ops:
  10.3 42.0 %all-reduce = s32[128]{0:T(128)S(1)} all-reduce(s32[128]{0:T(128)S(1)} %dynamic-update-slice), channel_id=2, replica_groups=mesh['replica'=16,'shard'=2] {'replica','shard'}, use_global_device_ids=true, to_apply=%add | all-reduce | flops 128 | bytes 1024
  61.0 1.8 all-gather.5
  68.7 1.8 all-gather.8
  73.4 2.3 all_gather.57
  77.0 2.0 fusion.8
  83.5 3.4 convolution_add_fusion.1
  86.9 3.4 convolution_add_fusion.2
  90.2 3.4 convolution_add_fusion.3
  93.6 3.4 convolution_add_fusion.4
  97.0 3.0 fusion.52
  100.0 3.2 fusion.55
  108.6 4.5 fusion.115
  113.1 4.1 fusion.116
  117.2 2.2 fusion.117
  119.4 2.1 fusion.118
  136.3 1.9 convolution_convert_fusion.8
  138.6 2.5 fusion.7
  144.9 3.9 pad_maximum_fusion.1
  153.8 3.9 pad_maximum_fusion
  160.6 2.2 fusion.105
  163.2 3.6 all-reduce.11
  169.0 6.0 reduce-scatter.14.cloned.1.call-done
  175.0 21.0 %reduce-scatter.12.cloned.1.call-done = bf16[2,512,2048]{2,1,0:T(8,128)(2,1)} async-done(((bf16[4,512,2048]{2,1,0:T(8,128)(2,1)}), bf16[2,512,2048]{2,1,0:T(8,128)(2,1)}) %reduce-scatter.12.cloned.1.call-update) | async-done | bytes 4194320 | tf_op jit(solution)/shard_map/reduce_scatter | solution.py:221
  196.1 777.9 %all-reduce.13 = (f32[256]{0:T(256)}, f32[256]{0:T(256)}, f32[256,1536]{1,0:T(8,128)}, f32[256]{0:T(256)}, f32[256]{0:T(256)}, /*index=5*/f32[256,512]{1,0:T(8,1...) all-reduce(f32[256]{0:T(256)S(1)} %dynamic-slice_convert_fusion.8, ...), channel_id=1, replica_groups=mesh['replica'=16,'shard'=2] {'replica'}, use_global_device_ids=true, to_apply=%region_26.27 | all-reduce | flops 4726528 | bytes 28372992 | tf_op jit(solution)/shard_map/psum | solution.py:323
  (335 shorter events, 59.4 us)
Async XLA Ops:
  7.2 69.8 %all-gather.14.cloned.1.call-start = ((), (), s32[]{:S(2)}) async-start(), calls=%async_computation.5 | async-start | bytes 2359296 | tf_op jit(solution)/shard_map/all_gather | solution.py:107
  7.9 75.5 %all-gather.16.cloned.1.call-start = ((), (), s32[]{:S(2)}) async-start(), calls=%async_computation.6 | async-start | bytes 12582912 | tf_op jit(solution)/shard_map/all_gather | solution.py:181
  8.7 45.0 %copy-start.69 = (bf16[256]{0:T(256)(128)(2,1)S(1)}, bf16[256]{0:T(256)(128)(2,1)}, u32[]{:S(2)}) copy-start(bf16[256]{0:T(256)(128)(2,1)} %param.22) | copy-start | bytes 1540
  8.7 46.8 %copy-start.70 = (bf16[256]{0:T(256)(128)(2,1)S(1)}, bf16[256]{0:T(256)(128)(2,1)}, u32[]{:S(2)}) copy-start(bf16[256]{0:T(256)(128)(2,1)} %param.23) | copy-start | bytes 1540
  8.7 48.6 %copy-start.71 = (bf16[256]{0:T(256)(128)(2,1)S(1)}, bf16[256]{0:T(256)(128)(2,1)}, u32[]{:S(2)}) copy-start(bf16[256]{0:T(256)(128)(2,1)} %param.25) | copy-start | bytes 1540
  8.7 50.4 %copy-start.72 = (bf16[256]{0:T(256)(128)(2,1)S(1)}, bf16[256]{0:T(256)(128)(2,1)}, u32[]{:S(2)}) copy-start(bf16[256]{0:T(256)(128)(2,1)} %param.26) | copy-start | bytes 1540
  8.7 52.2 %copy-start.73 = (bf16[256]{0:T(256)(128)(2,1)S(1)}, bf16[256]{0:T(256)(128)(2,1)}, u32[]{:S(2)}) copy-start(bf16[256]{0:T(256)(128)(2,1)} %param.28) | copy-start | bytes 1540
  8.7 54.0 %copy-start.74 = (bf16[256]{0:T(256)(128)(2,1)S(1)}, bf16[256]{0:T(256)(128)(2,1)}, u32[]{:S(2)}) copy-start(bf16[256]{0:T(256)(128)(2,1)} %param.29) | copy-start | bytes 1540
  8.7 55.8 %copy-start.75 = (bf16[256]{0:T(256)(128)(2,1)S(1)}, bf16[256]{0:T(256)(128)(2,1)}, u32[]{:S(2)}) copy-start(bf16[256]{0:T(256)(128)(2,1)} %param.30) | copy-start | bytes 1540
  8.7 58.2 %copy-start.60 = (bf16[2,512]{1,0:T(2,128)(2,1)S(1)}, bf16[2,512]{1,0:T(2,128)(2,1)}, u32[]{:S(2)}) copy-start(bf16[2,512]{1,0:T(2,128)(2,1)} %param.36) | copy-start | bytes 6148
  8.8 60.0 %copy-start.45 = (bf16[2,2048]{1,0:T(2,128)(2,1)S(1)}, bf16[2,2048]{1,0:T(2,128)(2,1)}, u32[]{:S(2)}) copy-start(bf16[2,2048]{1,0:T(2,128)(2,1)} %param.34) | copy-start | bytes 24580
  8.8 61.9 %copy-start.47 = (s32[1,394]{1,0:T(1,128)S(1)}, s32[1,394]{1,0:T(1,128)}, u32[]{:S(2)}) copy-start(s32[1,394]{1,0:T(1,128)} %param.38) | copy-start | bytes 4732
  8.8 62.5 %copy-start.61 = (bf16[256,4]{0,1:T(4,128)(2,1)S(1)}, bf16[256,4]{0,1:T(4,128)(2,1)}, u32[]{:S(2)}) copy-start(bf16[256,4]{0,1:T(4,128)(2,1)} %param.31) | copy-start | bytes 6148
  8.8 64.3 %copy-start = (bf16[197,512]{1,0:T(8,128)(2,1)S(1)}, bf16[197,512]{1,0:T(8,128)(2,1)}, u32[]{:S(2)}) copy-start(bf16[197,512]{1,0:T(8,128)(2,1)} %param.21) | copy-start | bytes 605188
  8.8 64.6 %copy-start.28 = (bf16[256,512]{1,0:T(8,128)(2,1)S(1)}, bf16[256,512]{1,0:T(8,128)(2,1)}, u32[]{:S(2)}) copy-start(bf16[256,512]{1,0:T(8,128)(2,1)} %param.27) | copy-start | bytes 786436
  8.8 88.1 %all-gather.18.cloned.1.call-start = ((), (), s32[]{:S(2)}) async-start(), calls=%async_computation.7 | async-start | bytes 12582912 | tf_op jit(solution)/shard_map/all_gather | solution.py:183
  9.5 158.5 %reduce-scatter.16.cloned.1.call-start = ((), (), s32[]{:S(2)}) async-start(), calls=%async_computation.12 | async-start | bytes 196608
  57.3 21.7 %copy-start.48 = (f32[2,1,256]{2,1,0:T(1,128)}, f32[2,1,256]{2,1,0:T(1,128)S(1)}, u32[]{:S(2)}) copy-start(f32[2,1,256]{2,1,0:T(1,128)S(1)} %convert_element_type.330) | copy-start | bytes 6148
  64.6 17.3 %copy-start.32 = (f32[2,1,256]{2,1,0:T(1,128)}, f32[2,1,256]{2,1,0:T(1,128)S(1)}, u32[]{:S(2)}) copy-start(f32[2,1,256]{2,1,0:T(1,128)S(1)} %convert_element_type.332) | copy-start | bytes 6148
  108.4 60.7 %reduce-scatter.10.cloned.1.call-start = ((), (), s32[]{:S(2)}) async-start(), calls=%async_computation.9 | async-start | bytes 786432 | tf_op jit(solution)/shard_map/reduce_scatter | solution.py:307
  113.1 11.6 %copy-start.16 = (bf16[197,2048]{1,0:T(8,128)(2,1)}, bf16[197,2048]{1,0:T(8,128)(2,1)S(1)}, u32[]{:S(2)}) copy-start(bf16[197,2048]{1,0:T(8,128)(2,1)S(1)} %get-tuple-element.191) | copy-start | bytes 2420740
  133.1 35.9 %reduce-scatter.8.cloned.1.call-start = ((), (), s32[]{:S(2)}) async-start(), calls=%async_computation.8 | async-start | bytes 2359296 | tf_op jit(solution)/shard_map/reduce_scatter | solution.py:298
  138.3 36.7 %reduce-scatter.14.cloned.1.call-start = ((), (), s32[]{:S(2)}) async-start(), calls=%async_computation.11 | async-start | bytes 12582912 | tf_op jit(solution)/shard_map/reduce_scatter | solution.py:233
  148.8 47.3 %reduce-scatter.12.cloned.1.call-start = ((), (), s32[]{:S(2)}) async-start(), calls=%async_computation.10 | async-start | bytes 12582912 | tf_op jit(solution)/shard_map/reduce_scatter | solution.py:221
  (65 other events, 157.3 us)
Sparse Core Ops, SparseCore 0:
  9.6 12.4 all-gather.13
  23.6 21.0 all-gather.15
  46.3 21.0 all-gather.17
  108.5 7.3 reduce-scatter.15
  133.3 7.7 reduce-scatter.9
  143.8 10.2 reduce-scatter.7
  156.9 18.0 reduce-scatter.13
  178.0 18.0 reduce-scatter.11
where the time goes:
time: 985 us; the launch traced here: 981 us
  blocking collectives  844 us (86%)
  matrix products  60.5 us (6%)
  waiting for transfers between devices  29.2 us (3%)
  between operations  16.7 us (2%)
  other arithmetic  16 us (2%)
  local copies, waits for them, and re-layouts  13.3 us (1%)
    psum x1, blocking collectives, on_device(): lax.psum((dense_grads[0], dense_grads[1], dense_grads[2], dense_grads[3],...  778 us
    unnamed x2, blocking collectives  45.5 us
    reduce_scatter x1, waiting for transfers between devices, on_device(): lax.psum_scatter(jnp.stack(collected[0], axis=0).astype(jnp.bfloat16), 's...  21 us
  transfers between devices with their start and end apart: 8, of which 2 were waited for; matrix products, arithmetic and copies ran while one was open for 7% of the time, Pallas kernels for 0%

commit v1 on v0

v1 whole, which is shorter than its diff:
```python
import functools

import jax
import jax.numpy as jnp
from jax import lax
from jax.experimental import pallas as pl
from jax.experimental.pallas import tpu as pltpu
from jax.sharding import PartitionSpec as P

HEAD_DIM = 64
PATCHES = 197
LN_EPS = 1e-06
MESH = pl.DeviceIdType.MESH
NT = (((1,), (1,)), ((), ()))
GELU_K = 0.7978845608028654
GELU_A = 0.044715


def half(values):
    return values.astype(jnp.bfloat16)


def dot(a, b):
    return jnp.dot(a, b, preferred_element_type=jnp.float32)


def dot_nt(a, b):
    return lax.dot_general(a, b, NT, preferred_element_type=jnp.float32)


def gelu_parts(x):
    x2 = x * x
    q = 0.5 + 0.5 * jnp.tanh(x * (GELU_K + (GELU_K * GELU_A) * x2))
    h = x * q
    return h, q + (h * (1.0 - q)) * (2 * GELU_K + (6 * GELU_K * GELU_A) * x2)


def layer_norm(values, gain_vector, bias_vector):
    centered = values - jnp.mean(values, axis=-1, keepdims=True)
    spread = lax.rsqrt(jnp.mean(centered * centered, axis=-1, keepdims=True) + LN_EPS)
    return centered * spread * gain_vector + bias_vector


def kept_gates(pair_expert, ranks, offsets, capacity, expert_count):
    same = pair_expert[:, None] == pair_expert[None, :]
    earlier = ranks[None, :] < ranks[:, None]
    before = jnp.sum(jnp.where(same & earlier, 1, 0).astype(jnp.int32), axis=1)
    onehot = pair_expert[:, None] == jnp.arange(expert_count, dtype=jnp.int32)[None, :]
    first_slot = jnp.sum(jnp.where(onehot, offsets[None, :], 0).astype(jnp.int32), axis=1)
    keep = before + first_slot < capacity
    picked = jnp.where(onehot & keep[:, None], 1.0, 0.0).astype(jnp.float32)
    return jnp.sum(picked.reshape(-1, 2, expert_count), axis=1)


def place():
    r = lax.axis_index("replica")
    return r // 4, (r // 2) % 2, r % 2, lax.axis_index("shard")


def rep(z, y, x):
    return (z * 2 + y) * 2 + x


def gather_kernel(zs, a_ref, b_ref, a_all, b_all, own_sem, send_sem, recv_sem, core_send, core_recv):
    z, y, x, c = place()
    me = rep(z, y, x)
    up, down, xn, yn = rep(z + 1, y, x), rep(z - 1, y, x), rep(z, y, 1 - x), rep(z, 1 - y, x)
    bar = pltpu.get_barrier_semaphore()

    @pl.when(z < zs - 1)
    def _():
        pl.semaphore_signal(bar, inc=1, device_id=(up, c), device_id_type=MESH)

    @pl.when(z > 0)
    def _():
        pl.semaphore_signal(bar, inc=1, device_id=(down, c), device_id_type=MESH)

    for t in ((xn, c), (yn, c), (me, 1 - c)):
        pl.semaphore_signal(bar, inc=1, device_id=t, device_id_type=MESH)
    pl.semaphore_wait(bar, 3 + (z < zs - 1).astype(jnp.int32) + (z > 0).astype(jnp.int32))

    src = (a_ref, b_ref)
    dst = (a_all, b_all)

    def link(m, kind, block, target):
        ref = dst[m].at[block * 2 + c]
        return pltpu.make_async_remote_copy(
            src_ref=ref, dst_ref=ref, send_sem=send_sem.at[m, kind, block], recv_sem=recv_sem.at[m, block],
            device_id=(target, c), device_id_type=MESH)

    def across(m, block):
        ref = dst[m].at[block * 2 + c]
        return pltpu.make_async_remote_copy(
            src_ref=ref, dst_ref=ref, send_sem=core_send.at[m, block], recv_sem=core_recv.at[m, block],
            device_id=(me, 1 - c), device_id_type=MESH)

    def from_core(m, block):
        ref = dst[m].at[block * 2 + 1 - c]
        return pltpu.make_async_remote_copy(
            src_ref=ref, dst_ref=ref, send_sem=core_send.at[m, block], recv_sem=core_recv.at[m, block],
            device_id=(me, 1 - c), device_id_type=MESH)

    first = (xn, yn)
    second = (yn, xn)

    def column(m, zz):
        block = rep(zz, y, x)
        link(m, 2, block, first[m]).start()
        link(m, 3, block, second[m]).start()
        across(m, block).start()

    own = [pltpu.make_async_copy(src[m], dst[m].at[me * 2 + c], own_sem.at[m]) for m in range(2)]
    for m in range(2):
        own[m].start()
    for m in range(2):
        own[m].wait()
    for m in range(2):
        pl.when(z < zs - 1)(lambda m=m: link(m, 0, me, up).start())
        pl.when(z > 0)(lambda m=m: link(m, 1, me, down).start())
    for m in range(2):
        column(m, z)

    def arrived(m, block):
        link(m, 0, block, up).wait_recv()

    def side_column(m, zz):
        block = rep(zz, y, 1 - x) if m == 0 else rep(zz, 1 - y, x)
        arrived(m, block)
        link(m, 3, block, second[m]).start()
        across(m, block).start()

    def far(m, zz):
        blocks = (rep(zz, 1 - y, x), rep(zz, 1 - y, 1 - x)) if m == 0 else (rep(zz, y, 1 - x), rep(zz, 1 - y, 1 - x))
        for block in blocks:
            arrived(m, block)
            across(m, block).start()

    for k in range(1, zs):
        for m in range(2):
            @pl.when(z - k >= 0)
            def _(m=m, k=k):
                arrived(m, rep(z - k, y, x))
                pl.when(z < zs - 1)(lambda: link(m, 0, rep(z - k, y, x), up).start())
                column(m, z - k)

            @pl.when(z + k < zs)
            def _(m=m, k=k):
                arrived(m, rep(z + k, y, x))
                pl.when(z > 0)(lambda: link(m, 1, rep(z + k, y, x), down).start())
                column(m, z + k)

        for m in range(2):
            for s in (-1, 1):
                if k == 1 and s == 1:
                    continue
                d = s * (k - 1)
                pl.when((z + d >= 0) & (z + d < zs))(lambda m=m, d=d: side_column(m, z + d))
    for m in range(2):
        for d in (1 - zs, zs - 1):
            pl.when((z + d >= 0) & (z + d < zs))(lambda m=m, d=d: side_column(m, z + d))
    for zz in range(zs):
        for m in range(2):
            far(m, zz)
    for block in range(4 * zs):
        for m in range(2):
            from_core(m, block).wait_recv()
            across(m, block).wait_send()
    for zz in range(zs):
        for m in range(2):
            pl.when((z >= zz) & (z < zs - 1))(lambda m=m, zz=zz: link(m, 0, rep(zz, y, x), up).wait_send())
            pl.when((z <= zz) & (z > 0))(lambda m=m, zz=zz: link(m, 1, rep(zz, y, x), down).wait_send())
            link(m, 2, rep(zz, y, x), xn).wait_send()
            link(m, 3, rep(zz, y, x), xn).wait_send()
            side = rep(zz, y, 1 - x) if m == 0 else rep(zz, 1 - y, x)
            link(m, 3, side, xn).wait_send()


def gather_blocks(a, b, zs):
    rows, width = a.shape
    hbm = pl.BlockSpec(memory_space=pl.ANY)
    n = 4 * zs
    return pl.pallas_call(
        functools.partial(gather_kernel, zs),
        out_shape=(jax.ShapeDtypeStruct((2 * n, rows, width), a.dtype), jax.ShapeDtypeStruct((2 * n, rows, width), a.dtype)),
        in_specs=[hbm, hbm],
        out_specs=(hbm, hbm),
        scratch_shapes=[
            pltpu.SemaphoreType.DMA((2,)),
            pltpu.SemaphoreType.DMA((2, 4, n)),
            pltpu.SemaphoreType.DMA((2, n)),
            pltpu.SemaphoreType.DMA((2, n)),
            pltpu.SemaphoreType.DMA((2, n)),
        ],
        compiler_params=pltpu.CompilerParams(collective_id=0, has_side_effects=True),
        name="token_gather",
    )(a, b)


def slice_kernel(block, n_ref, c_ref, g_ref, wi_ref, wo_ref, b_ref, gin_ref, gout_ref,
                 acc_in, acc_out, st_in, st_out, own_sem, send_sem, recv_sem):
    z, y, x, c = place()
    zn = z + 1 - 2 * (z % 2)
    targets = (rep(z, y, 1 - x), rep(z, 1 - y, x), rep(zn, y, x))
    bar = pltpu.get_barrier_semaphore()
    for t in targets:
        pl.semaphore_signal(bar, inc=1, device_id=(t, c), device_id_type=MESH)
    pl.semaphore_wait(bar, 3)
    qx, qy = (x + z) % 2, (y + z) % 2
    mine = qx * 2 + qy
    quarters = ((1 - qx) * 2 + qy, qx * 2 + 1 - qy, (1 - qx) * 2 + 1 - qy)
    experts, hq, _ = wi_ref.shape
    total = n_ref.shape[0]

    def sends(e, kind):
        src = st_in.at[e] if kind == 0 else st_out.at[e]
        cols = pl.ds(pl.multiple_of(mine * hq, 128), hq)
        dst = gin_ref.at[e, :, cols] if kind == 0 else gout_ref.at[e, cols, :]
        out = [pltpu.make_async_remote_copy(
            src_ref=src, dst_ref=dst, send_sem=send_sem.at[e, kind, i], recv_sem=recv_sem.at[e, kind, i],
            device_id=(t, c), device_id_type=MESH) for i, t in enumerate(targets)]
        return out, pltpu.make_async_copy(src, dst, own_sem.at[e, kind])

    def receives(e, kind):
        src = st_in.at[e] if kind == 0 else st_out.at[e]
        out = []
        for i, t in enumerate(targets):
            cols = pl.ds(pl.multiple_of(quarters[i] * hq, 128), hq)
            dst = gin_ref.at[e, :, cols] if kind == 0 else gout_ref.at[e, cols, :]
            out.append(pltpu.make_async_remote_copy(
                src_ref=src, dst_ref=dst, send_sem=send_sem.at[e, kind, i], recv_sem=recv_sem.at[e, kind, i],
                device_id=(t, c), device_id_type=MESH))
        return out

    for e in range(experts):
        acc_in[...] = jnp.zeros_like(acc_in)
        acc_out[...] = jnp.zeros_like(acc_out)
        wi, wo, bias = wi_ref[e], wo_ref[e], b_ref[e]

        def body(i, _):
            ts = pl.ds(pl.multiple_of(i * block, block), block)
            n, co, g = n_ref[ts, :], c_ref[ts, :], g_ref[e:e + 1, ts]
            pre = dot_nt(wi, n) + bias
            dh = dot_nt(wo, co)
            h, slope = gelu_parts(pre)
            acc_out[...] += dot(half(h * g), co)
            acc_in[...] += dot(half(slope * (dh * g)), n)
            return 0

        lax.fori_loop(0, total // block, body, 0)
        st_in[e] = half(acc_in[...].T)
        st_out[e] = half(acc_out[...])
        for kind in range(2):
            out, own = sends(e, kind)
            for copy in out:
                copy.start()
            own.start()
    for e in range(experts):
        for kind in range(2):
            out, own = sends(e, kind)
            own.wait()
            for copy in out:
                copy.wait_send()
            for copy in receives(e, kind):
                copy.wait_recv()


def slice_grads(n_all, c_all, gates_t, wi, wo, bias, block):
    experts, hq, width = wi.shape
    vm = pl.BlockSpec(memory_space=pltpu.VMEM)
    hbm = pl.BlockSpec(memory_space=pl.ANY)
    return pl.pallas_call(
        functools.partial(slice_kernel, block),
        out_shape=(jax.ShapeDtypeStruct((experts, width, 4 * hq), jnp.bfloat16), jax.ShapeDtypeStruct((experts, 4 * hq, width), jnp.bfloat16)),
        in_specs=[vm] * 6,
        out_specs=(hbm, hbm),
        scratch_shapes=[
            pltpu.VMEM((hq, width), jnp.float32),
            pltpu.VMEM((hq, width), jnp.float32),
            pltpu.VMEM((experts, width, hq), jnp.bfloat16),
            pltpu.VMEM((experts, hq, width), jnp.bfloat16),
            pltpu.SemaphoreType.DMA((experts, 2)),
            pltpu.SemaphoreType.DMA((experts, 2, 3)),
            pltpu.SemaphoreType.DMA((experts, 2, 3)),
        ],
        compiler_params=pltpu.CompilerParams(collective_id=1, has_side_effects=True, vmem_limit_bytes=56 << 20),
        name="slice_grads",
    )(n_all, c_all, gates_t, wi, wo, bias)


def swap(v):
    return lax.ppermute(v, "shard", [(0, 1), (1, 0)])


def on_device(
    inputs, norm1_gain, norm1_bias, qkv_weight, query_bias, value_bias, out_weight, out_bias, norm2_gain, norm2_bias,
    router_weight, noise, expert_in, expert_in_bias, expert_out, expert_out_bias, routes, priority, cotangent,
):
    tok_count, width = inputs.shape
    replicas, cores = lax.axis_size("replica"), lax.axis_size("shard")
    shard = lax.axis_index("shard")
    images = tok_count // PATCHES
    heads = width // HEAD_DIM
    owned, _, hidden_count = expert_in.shape
    expert_count = owned * cores
    score_scale = HEAD_DIM ** (-0.5)
    f32 = jnp.float32

    vectors = (norm1_gain, norm1_bias, query_bias, value_bias, out_bias, norm2_gain, norm2_bias)
    packed = jnp.concatenate(
        [qkv_weight, out_weight, jnp.stack(vectors, axis=1), router_weight], axis=1)
    packed = lax.all_gather(packed, "shard", axis=0, tiled=True)
    weight_qkv = packed[:, :3 * width]
    weight_proj = packed[:, 3 * width:4 * width]
    small = packed[:, 4 * width:]
    gain_one, bias_one, bias_query, bias_value, bias_proj, gain_two, bias_two = [
        small[:, i].astype(f32) for i in range(len(vectors))]
    weight_route = small[:, len(vectors):]

    pair_expert = routes.reshape(-1)
    onehot_pairs = (pair_expert[:, None] == jnp.arange(expert_count, dtype=jnp.int32)[None, :]).astype(jnp.int32)
    load = jnp.sum(onehot_pairs, axis=0)
    loads = lax.all_gather(load, ("replica", "shard"))
    position = lax.axis_index("replica") * cores + shard
    ahead = jnp.arange(replicas * cores)[:, None] < position
    offsets = jnp.sum(jnp.where(ahead, loads, 0), axis=0)
    capacity = 2 * tok_count * replicas * cores // expert_count
    chosen = kept_gates(pair_expert, priority.reshape(-1), offsets, capacity, expert_count)

    residual_in = inputs.astype(f32)
    normed_one, norm_one_back = jax.vjp(layer_norm, residual_in, gain_one, bias_one)
    normed_one_half = half(normed_one)
    qkv_bias = jnp.concatenate([bias_query, jnp.zeros_like(bias_query), bias_value])
    mixed = half(dot(normed_one_half, weight_qkv) + qkv_bias)
    shaped = mixed.reshape(images, PATCHES, 3, heads, HEAD_DIM)
    query, keys, values = (shaped[:, :, 0], shaped[:, :, 1], shaped[:, :, 2])
    scores = jnp.einsum("bqhd,bkhd->bhqk", query, keys, preferred_element_type=f32) * score_scale
    row_max = jnp.max(scores, axis=-1, keepdims=True)
    log_total = row_max + jnp.log(jnp.sum(jnp.exp(scores - row_max), axis=-1, keepdims=True))
    context = jnp.einsum(
        "bhqk,bkhd->bqhd", half(jnp.exp(scores - log_total)), values, preferred_element_type=f32)
    context_half = half(context.reshape(tok_count, width))
    middle = residual_in + (dot(context_half, weight_proj) + bias_proj)
    normed_two, norm_two_back = jax.vjp(layer_norm, middle, gain_two, bias_two)
    normed_two_half = half(normed_two)
    logits = dot(normed_two_half, weight_route) + noise
    route_probs = jax.nn.softmax(logits, axis=-1)
    gate_weights = route_probs * chosen
    upstream = cotangent.astype(f32)

    rows = -(-tok_count // 16) * 16
    pad = ((0, rows - tok_count), (0, 0))
    special = replicas == 16 and cores == 2 and images == 1 and hidden_count % 512 == 0
    if special:
        gates_pad = jnp.pad(gate_weights, pad).T
        gates_all = lax.all_gather(gates_pad, ("replica", "shard"), axis=0)
        n_all, c_all = gather_blocks(jnp.pad(normed_two_half, pad), jnp.pad(cotangent, pad), 4)

    pair_n = jnp.concatenate([normed_two_half, swap(normed_two_half)], axis=0)
    pair_c = jnp.concatenate([cotangent, swap(cotangent)], axis=0)
    own_gates = lax.dynamic_slice_in_dim(gate_weights, shard * owned, owned, 1)
    other_gates = swap(lax.dynamic_slice_in_dim(gate_weights, (1 - shard) * owned, owned, 1))
    pair_g = jnp.concatenate([own_gates, other_gates], axis=0)
    pair_up = pair_c.astype(f32)
    running = jnp.zeros((2 * tok_count, width), f32)
    d_rows = jnp.zeros((2 * tok_count, width), f32)
    gate_columns, bias_in_grads, bias_out_grads, in_grads, out_grads = [], [], [], [], []
    for e in range(owned):
        gate = pair_g[:, e:e + 1]
        pre = dot(pair_n, expert_in[e]) + expert_in_bias[e].astype(f32)
        act, slope = gelu_parts(pre)
        hid = half(act)
        result = dot(hid, expert_out[e]) + expert_out_bias[e].astype(f32)
        running = running + gate * result
        gate_columns.append(jnp.sum(pair_up * result, axis=1))
        d_result = half(gate * pair_up)
        d_pre = half(slope * dot_nt(d_result, expert_out[e]))
        d_rows = d_rows + dot_nt(d_pre, expert_in[e])
        bias_in_grads.append(jnp.sum(d_pre.astype(f32), axis=0))
        bias_out_grads.append(jnp.sum(d_result.astype(f32), axis=0))
        if not special:
            in_grads.append(jnp.einsum("td,th->dh", pair_n, d_pre, preferred_element_type=f32))
            out_grads.append(jnp.einsum("th,td->hd", hid, d_result, preferred_element_type=f32))
    d_gate_part = jnp.stack(gate_columns, axis=1)
    running = running[:tok_count] + swap(running[tok_count:])
    d_normed = d_rows[:tok_count] + swap(d_rows[tok_count:])
    d_gate_other = swap(d_gate_part[tok_count:])
    d_gate_own = d_gate_part[:tok_count]
    d_gates = jnp.where(shard == 0, jnp.concatenate([d_gate_own, d_gate_other], axis=1),
                        jnp.concatenate([d_gate_other, d_gate_own], axis=1))

    if special:
        z, y, x, _ = place()
        quarter = hidden_count // 4
        start = (((x + z) % 2) * 2 + (y + z) % 2) * quarter
        wi = lax.dynamic_slice_in_dim(expert_in, start, quarter, 2).swapaxes(1, 2)
        wo = lax.dynamic_slice_in_dim(expert_out, start, quarter, 1)
        bias = lax.dynamic_slice_in_dim(expert_in_bias, start, quarter, 1).astype(f32)[:, :, None]
        gates_t = lax.dynamic_slice_in_dim(gates_all, shard * owned, owned, 1)
        gates_t = gates_t.transpose(1, 0, 2).reshape(owned, -1)
        grad_in, grad_out = slice_grads(
            n_all.reshape(-1, width), c_all.reshape(-1, width), gates_t, wi, wo, bias, 512)
    else:
        grad_in = lax.psum(half(jnp.stack(in_grads, axis=0)), "replica")
        grad_out = lax.psum(half(jnp.stack(out_grads, axis=0)), "replica")

    output = half(middle + running)
    d_probs = d_gates * chosen
    d_logits = half(route_probs * (d_probs - jnp.sum(route_probs * d_probs, axis=-1, keepdims=True)))
    grad_route = jnp.einsum("td,te->de", normed_two_half, d_logits, preferred_element_type=f32)
    d_normed = d_normed + dot_nt(d_logits, weight_route)
    d_middle, grad_gain_two, grad_bias_two = norm_two_back(d_normed)
    d_middle = d_middle + upstream
    d_branch = half(d_middle)
    grad_proj = jnp.einsum("tc,td->cd", context_half, d_branch, preferred_element_type=f32)
    grad_proj_bias = jnp.sum(d_branch.astype(f32), axis=0)
    d_context = half(dot_nt(d_branch, weight_proj)).reshape(images, PATCHES, heads, HEAD_DIM)
    attn_probs = jnp.exp(scores - log_total)
    d_attn = jnp.einsum("bqhd,bkhd->bhqk", d_context, values, preferred_element_type=f32)
    d_values = jnp.einsum("bhqk,bqhd->bkhd", half(attn_probs), d_context, preferred_element_type=f32)
    d_scores = half(attn_probs * (d_attn - jnp.sum(attn_probs * d_attn, axis=-1, keepdims=True)))
    d_query = jnp.einsum("bhqk,bkhd->bqhd", d_scores, keys, preferred_element_type=f32) * score_scale
    d_keys = jnp.einsum("bhqk,bqhd->bkhd", d_scores, query, preferred_element_type=f32) * score_scale
    d_mixed = half(jnp.stack([d_query, d_keys, d_values], axis=2).reshape(tok_count, 3 * width))
    grad_qkv = jnp.einsum("td,tf->df", normed_one_half, d_mixed, preferred_element_type=f32)
    mixed_sums = jnp.sum(d_mixed.astype(f32), axis=0)
    d_normed_one = dot_nt(d_mixed, weight_qkv)
    d_input, grad_gain_one, grad_bias_one = norm_one_back(d_normed_one)
    input_grad = d_input + d_middle

    columns = jnp.stack((grad_gain_one, grad_bias_one, mixed_sums[:width], mixed_sums[2 * width:], grad_proj_bias,
                         grad_gain_two, grad_bias_two), axis=1)
    dense = half(jnp.concatenate([grad_qkv, grad_proj, columns, grad_route], axis=1))
    mine = width // 2
    keep = lax.dynamic_slice_in_dim(dense, shard * mine, mine, 0)
    give = lax.dynamic_slice_in_dim(dense, (1 - shard) * mine, mine, 0)
    dense = keep.astype(f32) + swap(give).astype(f32)
    bias_row = jnp.concatenate(bias_in_grads + bias_out_grads)
    summed, bias_row = lax.psum((half(dense), bias_row), "replica")
    summed = summed.astype(f32)
    columns = [summed[:, 4 * width + i] for i in range(len(vectors))]
    grad_in_bias = bias_row[:owned * hidden_count].reshape(owned, hidden_count)
    grad_out_bias = bias_row[owned * hidden_count:].reshape(owned, width)
    return (
        output, input_grad, columns[0], columns[1], summed[:, :3 * width], columns[2], columns[3],
        summed[:, 3 * width:4 * width], columns[4], columns[5], columns[6], summed[:, 4 * width + len(vectors):],
        grad_in.astype(f32), grad_in_bias, grad_out.astype(f32), grad_out_bias,
    )


def solution(mesh):
    both, split = ("replica", "shard"), "shard"
    return jax.shard_map(
        on_device,
        mesh=mesh,
        in_specs=(
            P(both, None), P(split), P(split), P(split, None), P(split), P(split), P(split, None), P(split), P(split),
            P(split), P(split, None), P(both, None), P(split, None, None), P(split, None), P(split, None, None),
            P(split, None), P(both, None), P(both, None), P(both, None),
        ),
        out_specs=(
            P(both, None), P(both, None), P(split), P(split), P(split, None), P(split), P(split), P(split, None),
            P(split), P(split), P(split), P(split, None), P(split, None, None), P(split, None), P(split, None, None),
            P(split, None),
        ),
        check_vma=False,
    )
```

time: 985 us -> 440 us (0.45)
  blocking collectives: 844 us -> 158 us
  Pallas kernels: 0 us -> 157 us
  local copies, waits for them, and re-layouts: 13.3 us -> 49.2 us
  matrix products: 60.5 us -> 32 us
  waiting for transfers between devices: 29.2 us -> 1.43 us
    psum x1, blocking collectives: 778 us -> 75.7 us  [on_device(): summed, bias_row = lax.psum((half(dense), bias_row), 'replica')]
    pallas_call x0 -> x2, Pallas kernels: none -> 157 us  [the longest x1 80.6 us: gather_blocks(): pl.pallas_call(functools.partial(gather_kernel, zs), out_shape=(jax.Shape...]
    dot_general x37 -> x21, matrix products: 58.4 us -> 30 us  [the longest x7 14.3 us: dot_nt(): return lax.dot_general(a, b, NT, preferred_element_type=jnp.float32)]
    reduce_scatter x4 -> x0, waiting for transfers between devices: 27 us -> none  [the longest x1 21 us: on_device(): lax.psum_scatter(jnp.stack(collected[0], axis=0).astype(jnp.bfloat16), 's...]
    all_gather x11 -> x1, blocking collectives: 20.2 us -> 40.8 us  [on_device(): gates_all = lax.all_gather(gates_pad, ('replica', 'shard'), axis=0)]
    convert_element_type x14 -> x7, other arithmetic: 2.82 us -> 18.4 us  [the longest x1 6.81 us: on_device(): grad_in.astype(f32)]
    another operation x8 -> x15, local copies, waits for them, and re-layouts: 0.05 us -> 12 us  [the longest x7 5.74 us: on_device(): jnp.stack((grad_gain_one, grad_bias_one, mixed_sums[:width], mixed_sums[2...]
    unnamed x2 -> x1, blocking collectives: 45.5 us -> 41.5 us
  transfers between devices with their start and end apart: 8 -> 9, of which waited for: 2 -> 2; matrix products, arithmetic and copies ran while one was open for 7% -> 10% of each run, Pallas kernels for 0% -> 36%
where the time goes in v1:
time: 440 us; the launch traced here: 439 us
  blocking collectives  158 us (36%)
  Pallas kernels  157 us (36%)
  local copies, waits for them, and re-layouts  49.2 us (11%)
  matrix products  32 us (7%)
  other arithmetic  24.5 us (6%)
  between operations  14.7 us (3%)
    pallas_call x1, Pallas kernels, gather_blocks(): pl.pallas_call(functools.partial(gather_kernel, zs), out_shape=(jax.Shape...  80.6 us
    pallas_call x1, Pallas kernels, slice_grads(): pl.pallas_call(functools.partial(slice_kernel, block), out_shape=(jax.Sha...  76.6 us
    psum x1, blocking collectives, on_device(): summed, bias_row = lax.psum((half(dense), bias_row), 'replica')  75.7 us
    unnamed x1, blocking collectives  41.5 us
    all_gather x1, blocking collectives, on_device(): gates_all = lax.all_gather(gates_pad, ('replica', 'shard'), axis=0)  40.8 us
    dot_general x7, matrix products, dot_nt(): return lax.dot_general(a, b, NT, preferred_element_type=jnp.float32)  14.3 us
    dot_general x7, matrix products, dot(): return jnp.dot(a, b, preferred_element_type=jnp.float32)  12.2 us
  transfers between devices with their start and end apart: 9, of which 2 were waited for; matrix products, arithmetic and copies ran while one was open for 10% of the time, Pallas kernels for 36%

profile of v1, /device:TPU:0, one launch (start us, length us, event | category | flops | bytes accessed | tf_op | source)
XLA Modules:
  0.0 439.3 jit_solution(91510079465131204)
XLA Ops:
  13.6 3.1 concatenate.34
  17.9 41.5 %all-reduce.3 = s32[128]{0:T(128)S(1)} all-reduce(s32[128]{0:T(128)S(1)} %dynamic-update-slice), channel_id=2, replica_groups=mesh['replica'=16,'shard'=2] {'replica','shard'}, use_global_device_ids=true, to_apply=%add.3 | all-reduce | flops 128 | bytes 1024
  61.4 2.5 convert_reduce_fusion.6
  63.9 2.0 fusion.4
  74.5 3.5 convert_reduce_fusion
  81.3 3.7 convert_reduce_fusion.1
  88.1 3.9 convert_reduce_fusion.3
  95.4 2.3 multiply_reduce_fusion.1
  97.7 2.0 fusion.110
  101.6 2.0 convolution_convert_fusion.3
  109.5 1.9 convolution_convert_fusion
  115.9 3.8 concatenate.41
  120.8 2.3 copy.167
  123.2 2.3 constant_dynamic-slice_fusion
  126.1 2.3 copy.168
  128.4 2.5 add_convert_fusion
  132.7 2.3 copy.178
  134.9 2.3 constant_dynamic-slice_fusion.4.wo_ref
  137.9 40.8 %all-gather.2 = f32[32,4,208]{2,1,0:T(4,128)S(1)} all-gather(f32[1,4,208]{2,1,0:T(4,128)S(1)} %pad_bitcast_fusion), channel_id=3, replica_groups=mesh['replica'=16,'shard'=2] {'replica','shard'}, dimensions={0}, use_global_device_ids=true | all-gather | bytes 109824 | tf_op jit(solution)/shard_map/all_gather | solution.py:355
  179.5 80.6 %token_gather.1 = (bf16[32,208,512]{2,1,0:T(8,128)(2,1)}, bf16[32,208,512]{2,1,0:T(8,128)(2,1)}) custom-call(bf16[208,512]{1,0:T(8,128)(2,1)} %pad.11.a_ref, bf16[208,512]{1,0:T(8,128)(2,1)} %pad.12.b_ref), custom_call_target="tpu_custom_call" | custom-call | tf_op jit(solution)/shard_map/token_gather/pallas_call | solution.py:182
  260.1 76.6 %slice_grads.1 = (bf16[2,512,2048]{2,1,0:T(8,128)(2,1)}, bf16[2,2048,512]{2,1,0:T(8,128)(2,1)}) custom-call(bf16[6656,512]{1,0:T(8,128)(2,1)} %bitcast.116, bf16[6656,512]{1,0:T(8,128)(2,1)} %bitcast.117, f32[2,6656]{1,0:T(2,128)} %reshape.334.g_ref, bf16[2,512,512]{2,1,0:T(8,128)(2,1)} %bitcast.118, ...), custom_call_target="tpu_custom_call" | custom-call | tf_op jit(solution)/shard_map/slice_grads/pallas_call | solution.py:271
  336.7 6.8 %convert_element_type.250 = f32[2,512,2048]{2,1,0:T(8,128)} convert(bf16[2,512,2048]{2,1,0:T(8,128)(2,1)} %get-tuple-element.22) | non-fusion elementwise | flops 2097152 | bytes 12582912 | tf_op jit(solution)/shard_map/convert_element_type | solution.py:446
  343.5 4.6 %convert_element_type.255 = f32[2,2048,512]{2,1,0:T(8,128)} convert(bf16[2,2048,512]{2,1,0:T(8,128)(2,1)S(1)} %copy-done.3) | non-fusion elementwise | flops 2097152 | bytes 12582912 | tf_op jit(solution)/shard_map/convert_element_type | solution.py:446
  348.1 75.7 %psum.15 = f32[5120]{0:T(1024)S(1)} all-reduce(f32[5120]{0:T(1024)S(1)} %pad_maximum_fusion.4), channel_id=1, replica_groups=mesh['replica'=16,'shard'=2] {'replica'}, use_global_device_ids=true, to_apply=%region_32.33 | all-reduce | flops 5120 | bytes 40960 | tf_op jit(solution)/shard_map/psum | solution.py:438
  (172 shorter events, 53.5 us)
Async XLA Ops:
  7.2 9.6 %copy-start.7 = (bf16[197,512]{1,0:T(8,128)(2,1)S(1)}, bf16[197,512]{1,0:T(8,128)(2,1)}, u32[]{:S(2)}) copy-start(bf16[197,512]{1,0:T(8,128)(2,1)} %param.37) | copy-start | bytes 605188
  7.2 10.1 %copy-start.16 = (s32[197,2]{0,1:T(2,128)S(1)}, s32[197,2]{0,1:T(2,128)}, u32[]{:S(2)}) copy-start(s32[197,2]{0,1:T(2,128)} %param.35) | copy-start | bytes 4732
  7.2 52.5 %copy-start.17 = (s32[1,394]{1,0:T(1,128)S(1)}, s32[1,394]{1,0:T(1,128)}, u32[]{:S(2)}) copy-start(s32[1,394]{1,0:T(1,128)} %param.36) | copy-start | bytes 4732
  7.2 53.2 %copy-start.2 = (bf16[197,512]{1,0:T(8,128)(2,1)S(1)}, bf16[197,512]{1,0:T(8,128)(2,1)}, u32[]{:S(2)}) copy-start(bf16[197,512]{1,0:T(8,128)(2,1)} %param.19) | copy-start | bytes 605188
  7.2 53.5 %copy-start.15 = (bf16[2,2048]{1,0:T(2,128)(2,1)S(1)}, bf16[2,2048]{1,0:T(2,128)(2,1)}, u32[]{:S(2)}) copy-start(bf16[2,2048]{1,0:T(2,128)(2,1)} %param.32) | copy-start | bytes 24580
  7.2 54.1 %all-gather.5.cloned.1.call-start = ((), (), s32[]{:S(2)}) async-start(), calls=%async_computation | async-start | bytes 3342336 | tf_op jit(solution)/shard_map/all_gather | solution.py:311
  16.7 409.3 %all-reduce.6.cloned.1.call-start = ((), (), s32[]{:S(2)}) async-start(), calls=%async_computation.1 | async-start | bytes 2228224 | tf_op jit(solution)/shard_map/psum | solution.py:438
  16.8 56.7 %collective-permute-start.3 = (bf16[197,512]{1,0:T(8,128)(2,1)S(1)}, bf16[197,512]{1,0:T(8,128)(2,1)}, u32[]{:S(2)}, u32[]{:S(2)}) collective-permute-start(bf16[197,512]{1,0:T(8,128)(2,1)S(1)} %copy-done.7), channel_id=1, source_target_pairs={{0,1},{1,0},{2,3},{3,2},{4,5},{5,4},{6,7},{7,6},{8,9},{9,8},{10,11... | collective-permute-start | bytes 605192 | tf_op jit(solution)/shard_map/ppermute | solution.py:291
  61.4 12.1 %copy-start.19 = (f32[1,2048]{1,0:T(1,128)}, f32[1,2048]{1,0:T(1,128)S(1)}, u32[]{:S(2)}) copy-start(f32[1,2048]{1,0:T(1,128)S(1)} %get-tuple-element.138) | copy-start | bytes 24580
  66.6 4.9 %copy-start.18 = (bf16[2,512]{1,0:T(2,128)(2,1)S(1)}, bf16[2,512]{1,0:T(2,128)(2,1)}, u32[]{:S(2)}) copy-start(bf16[2,512]{1,0:T(2,128)(2,1)} %param.34) | copy-start | bytes 6148
  66.6 5.8 %copy-start.1 = (bf16[2,512,2048]{2,1,0:T(8,128)(2,1)S(1)}, bf16[2,512,2048]{2,1,0:T(8,128)(2,1)}, u32[]{:S(2)}) copy-start(bf16[2,512,2048]{2,1,0:T(8,128)(2,1)} %param.31) | copy-start | bytes 12582916
  67.3 5.1 %copy-start.10 = (bf16[8,64,197]{2,1,0:T(8,128)(2,1)}, bf16[8,64,197]{2,1,0:T(8,128)(2,1)S(1)}, u32[]{:S(2)}) copy-start(bf16[8,64,197]{2,1,0:T(8,128)(2,1)S(1)} %convolution_convert_fusion.2) | copy-start | bytes 605188
  69.6 2.8 collective-permute-start.1
  70.9 1.4 collective-permute-start
  87.8 7.6 %collective-permute-start.4 = (f32[197,512]{1,0:T(8,128)}, f32[197,512]{1,0:T(8,128)}, u32[]{:S(2)}, u32[]{:S(2)}) collective-permute-start(f32[197,512]{1,0:T(8,128)} %slice.218), channel_id=1, source_target_pairs={{0,1},{1,0},{2,3},{3,2},{4,5},{5,4},{6,7},{7,6},{8,9},{9,8},{10,11... | collective-permute-start | bytes 1210376 | tf_op jit(solution)/shard_map/ppermute | solution.py:291
  92.1 2.3 collective-permute-start.5
  94.1 3.6 collective-permute-start.2
  95.4 5.1 %copy-start.11 = (bf16[8,64,197]{2,1,0:T(8,128)(2,1)S(1)}, bf16[8,64,197]{2,1,0:T(8,128)(2,1)}, u32[]{:S(2)}) copy-start(bf16[8,64,197]{2,1,0:T(8,128)(2,1)} %copy-done.10) | copy-start | bytes 605188
  106.5 4.9 %copy-start.13 = (bf16[512,2059]{1,0:T(8,128)(2,1)S(1)}, bf16[512,2059]{1,0:T(8,128)(2,1)}, u32[]{:S(2)}) copy-start(bf16[512,2059]{1,0:T(8,128)(2,1)} %all-gather.5.cloned.1.call-done) | copy-start | bytes 6325252
  109.5 6.4 %copy-start.6 = (bf16[512,512]{1,0:T(8,128)(2,1)S(1)}, bf16[512,512]{1,0:T(8,128)(2,1)}, u32[]{:S(2)}) copy-start(bf16[512,512]{1,0:T(8,128)(2,1)} %convolution_convert_fusion.1) | copy-start | bytes 1572868
  123.0 3.0 collective-permute-start.6
  336.7 6.8 %copy-start.3 = (bf16[2,2048,512]{2,1,0:T(8,128)(2,1)S(1)}, bf16[2,2048,512]{2,1,0:T(8,128)(2,1)}, u32[]{:S(2)}) copy-start(bf16[2,2048,512]{2,1,0:T(8,128)(2,1)} %get-tuple-element.23) | copy-start | bytes 12582916
  343.5 81.6 %copy-start.5 = (f32[197,512]{1,0:T(8,128)S(1)}, f32[197,512]{1,0:T(8,128)}, u32[]{:S(2)}) copy-start(f32[197,512]{1,0:T(8,128)} %copy-done.4) | copy-start | bytes 1210372
  343.5 81.6 %copy-start.9 = (f32[197,512]{1,0:T(8,128)S(1)}, f32[197,512]{1,0:T(8,128)}, u32[]{:S(2)}) copy-start(f32[197,512]{1,0:T(8,128)} %copy-done.8) | copy-start | bytes 1210372
  (11 other events, 28.5 us)
Sparse Core Ops, SparseCore 0:
  16.8 13.4 all-gather.4
  131.0 116.6 all-reduce.5

commit v2 on v1

v2 whole, which is shorter than its diff:
```python
import functools
from types import SimpleNamespace

import jax
import jax.numpy as jnp
from jax import lax
from jax.experimental import pallas as pl
from jax.experimental.pallas import tpu as pltpu
from jax.sharding import PartitionSpec as P

HEAD_DIM = 64
PATCHES = 197
LN_EPS = 1e-06
MESH = pl.DeviceIdType.MESH
NT = (((1,), (1,)), ((), ()))
GELU_K = 0.7978845608028654
GELU_A = 0.044715
F32 = jnp.float32
BF16 = jnp.bfloat16
ROWS = 256
BLOCK = 208
STEP = 512


def half(values):
    return values.astype(BF16)


def dot(a, b):
    return jnp.dot(a, b, preferred_element_type=F32)


def dot_nt(a, b):
    return lax.dot_general(a, b, NT, preferred_element_type=F32)


def gelu_parts(x):
    x2 = x * x
    q = 0.5 + 0.5 * jnp.tanh(x * (GELU_K + (GELU_K * GELU_A) * x2))
    h = x * q
    return h, q + (h * (1.0 - q)) * (2 * GELU_K + (6 * GELU_K * GELU_A) * x2)


def iota(shape, dim):
    return lax.broadcasted_iota(jnp.int32, shape, dim)


def many(start, size, unit):
    return pl.ds(pl.multiple_of(start, unit), size)


def normalize(v):
    centered = v - jnp.mean(v, axis=-1, keepdims=True)
    spread = lax.rsqrt(jnp.mean(centered * centered, axis=-1, keepdims=True) + LN_EPS)
    return centered * spread, spread


def norm_back(d, xhat, spread, gain):
    dx = d * gain
    return spread * (dx - jnp.mean(dx, axis=-1, keepdims=True) - xhat * jnp.mean(dx * xhat, axis=-1, keepdims=True))


def column_sum(v):
    return jnp.sum(v, axis=0, keepdims=True)


def place():
    r = lax.axis_index("replica")
    return r // 4, (r // 2) % 2, r % 2, lax.axis_index("shard")


def rep(z, y, x):
    return (z * 2 + y) * 2 + x


def as_int(flag):
    return flag.astype(jnp.int32)


class Gather:
    def __init__(self, zs, x_first, rows, sems):
        self.zs, self.x_first, self.rows = zs, x_first, rows
        self.send, self.recv, self.core_send, self.core_recv = sems
        self.z, self.y, self.x, self.c = place()
        z, y, x = self.z, self.y, self.x
        self.me, self.up, self.down = rep(z, y, x), rep(z + 1, y, x), rep(z - 1, y, x)
        near = (rep(z, y, 1 - x), rep(z, 1 - y, x))
        self.first, self.second = near if x_first else near[::-1]

    def side(self, zz):
        return rep(zz, self.y, 1 - self.x) if self.x_first else rep(zz, 1 - self.y, self.x)

    def opposite(self, zz):
        return rep(zz, 1 - self.y, self.x) if self.x_first else rep(zz, self.y, 1 - self.x)

    def ref(self, block, core):
        return self.rows.at[many((block * 2 + core) * BLOCK, BLOCK, 16), :]

    def link(self, kind, block, target):
        ref = self.ref(block, self.c)
        return pltpu.make_async_remote_copy(
            src_ref=ref, dst_ref=ref, send_sem=self.send.at[kind, block], recv_sem=self.recv.at[block],
            device_id=(target, self.c), device_id_type=MESH)

    def across(self, block, core=None):
        ref = self.ref(block, self.c if core is None else core)
        return pltpu.make_async_remote_copy(
            src_ref=ref, dst_ref=ref, send_sem=self.core_send.at[block], recv_sem=self.core_recv.at[block],
            device_id=(self.me, 1 - self.c), device_id_type=MESH)

    def column(self, block):
        self.link(2, block, self.first).start()
        self.link(3, block, self.second).start()
        self.across(block).start()

    def arrived(self, block):
        self.link(0, block, self.up).wait_recv()

    def begin(self):
        pl.when(self.z < self.zs - 1)(lambda: self.link(0, self.me, self.up).start())
        pl.when(self.z > 0)(lambda: self.link(1, self.me, self.down).start())
        self.column(self.me)

    def turn(self, k):
        z, y, x = self.z, self.y, self.x

        @pl.when(z - k >= 0)
        def _():
            block = rep(z - k, y, x)
            self.arrived(block)
            pl.when(z < self.zs - 1)(lambda: self.link(0, block, self.up).start())
            self.column(block)

        @pl.when(z + k < self.zs)
        def _():
            block = rep(z + k, y, x)
            self.arrived(block)
            pl.when(z > 0)(lambda: self.link(1, block, self.down).start())
            self.column(block)

    def side_turn(self, k):
        for d in ((0,) if k == 0 else (-k, k)):
            @pl.when((self.z + d >= 0) & (self.z + d < self.zs))
            def _():
                block = self.side(self.z + d)
                self.arrived(block)
                self.link(3, block, self.second).start()
                self.across(block).start()

    def far(self, zz):
        for block in (self.opposite(zz), rep(zz, 1 - self.y, 1 - self.x)):
            self.arrived(block)
            self.across(block).start()

    def finish_partner(self):
        self.across(self.me, 1 - self.c).wait_recv()

    def finish(self):
        for block in range(4 * self.zs):
            pl.when(block != self.me)(lambda block=block: self.across(block, 1 - self.c).wait_recv())

    def drain(self):
        z, y, x = self.z, self.y, self.x
        for block in range(4 * self.zs):
            self.across(block).wait_send()
        for zz in range(self.zs):
            block = rep(zz, y, x)
            pl.when((z >= zz) & (z < self.zs - 1))(lambda block=block: self.link(0, block, self.up).wait_send())
            pl.when((z <= zz) & (z > 0))(lambda block=block: self.link(1, block, self.down).wait_send())
            self.link(2, block, self.first).wait_send()
            self.link(3, block, self.second).wait_send()
            self.link(3, self.side(zz), self.second).wait_send()


SCRATCH = (
    ("n_all", (None, 512), BF16), ("c_all", (None, 512), BF16), ("g_all", (8, None), F32),
    ("wqkv", (512, 1536), BF16), ("wproj", (512, 512), BF16), ("wroute", (512, 128), BF16), ("vec", (2, 8, 256), F32),
    ("win", (2, 512, 2048), BF16), ("wout", (2, 2048, 512), BF16),
    ("count_out", (6, 8, 128), F32), ("count_in", (4, 8, 128), F32),
    ("xs", (ROWS, 512), F32), ("noise", (ROWS, 128), F32), ("routes", (ROWS, 128), F32),
    ("xhat1", (ROWS, 512), F32), ("n1", (ROWS, 512), BF16), ("mixed", (ROWS, 1536), BF16),
    ("probs", (8, ROWS, ROWS), F32), ("ctx", (ROWS, 512), BF16), ("mid", (ROWS, 512), F32), ("xhat2", (ROWS, 512), F32),
    ("chosen", (ROWS, 128), F32), ("rprobs", (ROWS, 128), F32),
    ("res", (2 * BLOCK, 512), F32), ("running", (2 * BLOCK, 512), F32), ("drows", (2 * BLOCK, 512), F32),
    ("dgate", (2 * BLOCK, 128), F32), ("dres", (2 * BLOCK, 512), BF16), ("gcol", (2 * BLOCK, 128), F32),
    ("got_running", (BLOCK, 512), F32), ("got_drows", (BLOCK, 512), F32), ("got_dgate", (BLOCK, 128), F32),
    ("db", (ROWS, 512), BF16), ("dctx", (ROWS, 512), BF16), ("dmixed", (ROWS, 1536), BF16), ("dn", (ROWS, 512), F32),
    ("dense", (512, 2048), BF16), ("dense_in", (256, 2048), BF16), ("extra", (3, 16, 2048), F32),
    ("total", (272, 2048), BF16), ("final", (272, 2048), BF16), ("part_in", (4, 272, 512), BF16), ("z_out", (4, 272, 256), BF16), ("z_in", (4, 272, 256), BF16),
    ("acc_in", (512, 512), F32), ("acc_out", (512, 512), F32),
    ("st_in", (2, 512, 512), BF16), ("st_out", (2, 512, 512), BF16),
)
SEMS = (
    ("g_send", (2, 4, None)), ("g_recv", (2, None)), ("g_csend", (2, None)), ("g_crecv", (2, None)),
    ("load", (2,)), ("w_send", (4,)), ("w_recv", (4,)), ("count_send", (6,)), ("count_recv", (4,)),
    ("p_send", (3,)), ("p_recv", (3,)), ("d_send", (2,)), ("d_recv", (2,)),
    ("ar_send", (12,)), ("ar_recv", (12,)), ("s_own", (2, 2)), ("s_send", (2, 2, 3)), ("s_recv", (2, 2, 3)),
)
INPUTS = ("x", "cot", "noise_in", "routes_in", "prio", "vec_in", "wqkv_in", "wproj_in", "wroute_in", "win_in", "wout_in",
          "bin", "bout")
OUTPUTS = ("out", "igrad", "gin", "gout", "summed")


def remote(src, dst, send, recv, target):
    return pltpu.make_async_remote_copy(
        src_ref=src, dst_ref=dst, send_sem=send, recv_sem=recv, device_id=target, device_id_type=MESH)


def block_kernel(zs, *refs):
    names = INPUTS + OUTPUTS + tuple(n for n, _, _ in SCRATCH) + tuple(n for n, _ in SEMS)
    r = SimpleNamespace(**dict(zip(names, refs, strict=True)))
    z, y, x, c = place()
    me = rep(z, y, x)
    partner = (me, 1 - c)
    xn, yn = (rep(z, y, 1 - x), c), (rep(z, 1 - y, x), c)
    up, down = (rep(z + 1, y, x), c), (rep(z - 1, y, x), c)
    low_z, high_z = z > 0, z < zs - 1
    tokens = r.x.shape[0]
    devices = 8 * zs
    capacity = 2 * tokens * devices // 4

    bar = pltpu.get_barrier_semaphore()
    pl.when(high_z)(lambda: pl.semaphore_signal(bar, inc=1, device_id=up, device_id_type=MESH))
    pl.when(low_z)(lambda: pl.semaphore_signal(bar, inc=1, device_id=down, device_id_type=MESH))
    for t in (xn, yn, partner):
        pl.semaphore_signal(bar, inc=1, device_id=t, device_id_type=MESH)

    loads = [pltpu.make_async_copy(r.win_in, r.win, r.load.at[0]), pltpu.make_async_copy(r.wout_in, r.wout, r.load.at[1])]
    for copy in loads:
        copy.start()

    r.xs[...] = jnp.zeros_like(r.xs)
    r.xs[0:tokens, :] = r.cot[...].astype(F32)
    own_rows = many((me * 2 + c) * BLOCK, BLOCK, 16)
    r.c_all[own_rows, :] = half(r.xs[0:BLOCK, :])
    mine, other = many(c * 256, 256, 16), many((1 - c) * 256, 256, 16)
    r.wqkv[mine, :] = r.wqkv_in[...]
    r.wproj[mine, :] = r.wproj_in[...]
    r.wroute[mine, :] = r.wroute_in[...]
    r.vec[c] = r.vec_in[...]

    pl.semaphore_wait(bar, 3 + as_int(low_z) + as_int(high_z))

    weights = [remote(ref, ref, r.w_send.at[i], r.w_recv.at[i], partner) for i, ref in enumerate(
        (r.vec.at[c], r.wqkv.at[mine, :], r.wproj.at[mine, :], r.wroute.at[mine, :]))]
    for copy in weights:
        copy.start()
    gathers = [Gather(zs, m == 0, (r.n_all, r.c_all)[m],
                      (r.g_send.at[m], r.g_recv.at[m], r.g_csend.at[m], r.g_crecv.at[m])) for m in range(2)]
    ga, gb = gathers
    gb.begin()

    lane, row = iota((ROWS, 128), 1), iota((ROWS, 128), 0)
    r.routes[...] = jnp.full_like(r.routes, -1.0)
    r.routes[0:tokens, 0:2] = r.routes_in[...].astype(F32)
    experts = [r.routes[:, k:k + 1] for k in range(2)]
    onehot = [jnp.where(lane.astype(F32) == experts[k], 1.0, 0.0) for k in range(2)]
    count = jnp.broadcast_to(column_sum(onehot[0] + onehot[1]), (8, 128))

    def count_copy(i, slot, target):
        return remote(r.count_out.at[i], r.count_in.at[slot], r.count_send.at[i], r.count_recv.at[slot], target)

    r.count_out[0] = count
    count_copy(0, 0, partner).start()

    places = iota((ROWS, r.prio.shape[1]), 1) - 2 * iota((ROWS, r.prio.shape[1]), 0)
    ranks = r.prio[...].astype(F32)
    codes = [experts[k] * 1024.0 + jnp.sum(jnp.where(places == k, ranks, 0.0), axis=1, keepdims=True) for k in range(2)]
    codes = [jnp.where(row[:, 0:1] < tokens, code, -1.0) for code in codes]
    code_rows = jnp.where(lane == 0, codes[0], jnp.where(lane == 1, codes[1], 0.0)).T
    before = []
    for k in range(2):
        floor = experts[k] * 1024.0
        seen = 0.0
        for j in range(2):
            others = code_rows[j:j + 1, :]
            seen = seen + jnp.where((others < codes[k]) & (others >= floor), 1.0, 0.0)
        before.append(jnp.sum(seen, axis=1, keepdims=True))

    count_copy(0, 0, partner).wait_recv()
    ahead = jnp.where(c == 1, 1.0, 0.0) * r.count_in[0]
    count = count + r.count_in[0]
    r.count_out[1] = count
    count_copy(1, 1, xn).start()

    weights[0].wait_send()
    remote(r.vec.at[1 - c], r.vec.at[1 - c], r.w_send.at[0], r.w_recv.at[0], partner).wait_recv()
    vec = jnp.concatenate([r.vec[0], r.vec[1]], axis=1)
    gain1, bias1, bias_q, bias_v, bias_p, gain2, bias2 = [vec[i:i + 1, :] for i in range(7)]
    r.xs[0:tokens, :] = r.x[...].astype(F32)
    xhat, spread1 = normalize(r.xs[...])
    r.xhat1[...] = xhat
    r.n1[...] = half(xhat * gain1 + bias1)

    count_copy(1, 1, xn).wait_recv()
    ahead = ahead + jnp.where(x == 1, 1.0, 0.0) * r.count_in[1]
    count = count + r.count_in[1]
    r.count_out[2] = count
    count_copy(2, 2, yn).start()

    for i, ref in ((1, r.wqkv), (2, r.wproj), (3, r.wroute)):
        weights[i].wait_send()
        ref = ref.at[other, :]
        remote(ref, ref, r.w_send.at[i], r.w_recv.at[i], partner).wait_recv()
    for i, bias in enumerate((bias_q, None, bias_v)):
        part = dot(r.n1[...], r.wqkv[:, 512 * i:512 * (i + 1)])
        r.mixed[:, 512 * i:512 * (i + 1)] = half(part if bias is None else part + bias)

    gb.turn(1)
    gb.side_turn(0)
    count_copy(2, 2, yn).wait_recv()
    ahead = ahead + jnp.where(y == 1, 1.0, 0.0) * r.count_in[2]
    count = count + r.count_in[2]

    low_lane = lane < HEAD_DIM
    key_kept = iota((ROWS, ROWS), 1) < tokens

    def heads_forward(i, _):
        q, k, v = [r.mixed[:, many(base + 128 * i, 128, 128)] for base in (0, 512, 1024)]
        q = q * BF16(HEAD_DIM ** -0.5)
        parts = []
        for h in range(2):
            s = dot_nt(jnp.where(low_lane == (h == 0), q, jnp.zeros_like(q)), k)
            s = jnp.where(key_kept, s, -1e30)
            e = jnp.exp(s - jnp.max(s, axis=-1, keepdims=True))
            p = e / jnp.sum(e, axis=-1, keepdims=True)
            r.probs[2 * i + h] = p
            parts.append(dot(half(p), v))
        r.ctx[:, many(128 * i, 128, 128)] = half(jnp.where(low_lane, parts[0], parts[1]))
        return 0

    lax.fori_loop(0, 4, heads_forward, 0)

    gb.turn(2)
    gb.side_turn(1)

    def pass_up(extra):
        r.count_out[3] = count + extra
        pl.when(high_z)(lambda: count_copy(3, 3, up).start())

    pl.when(z == 0)(lambda: pass_up(0.0))

    @pl.when(low_z)
    def _():
        count_copy(3, 3, up).wait_recv()
        pass_up(r.count_in[3])

    below = jnp.where(low_z, r.count_in[3], 0.0)
    offsets = (ahead + below)[0:1, :]
    chosen = 0.0
    for k in range(2):
        slot = before[k] + jnp.sum(onehot[k] * offsets, axis=1, keepdims=True)
        chosen = chosen + onehot[k] * jnp.where(slot < float(capacity), 1.0, 0.0)
    r.chosen[...] = chosen

    middle = r.xs[...] + (dot(r.ctx[...], r.wproj[...]) + bias_p)
    r.mid[...] = middle
    xhat, spread2 = normalize(middle)
    r.xhat2[...] = xhat
    n2 = half(xhat * gain2 + bias2)
    r.noise[...] = jnp.zeros_like(r.noise)
    r.noise[0:tokens, 0:4] = r.noise_in[...]
    logits = jnp.where(lane < 4, dot(n2, r.wroute[...]) + r.noise[...], -1e30)
    e = jnp.exp(logits - jnp.max(logits, axis=-1, keepdims=True))
    rprobs = e / jnp.sum(e, axis=-1, keepdims=True)
    r.rprobs[...] = rprobs
    gates = rprobs * chosen
    gates_high = half(gates).astype(F32)
    packed = jnp.where(lane < 4, gates_high, pltpu.roll(gates - gates_high, 4, 1)).T
    packed = jnp.concatenate([packed[0:8, :], jnp.zeros((8, 256), F32)], axis=1)
    r.n_all[own_rows, :] = jnp.concatenate([n2[0:192, :], half(jnp.concatenate(
        [n2[192:200, :].astype(F32), packed], axis=0))], axis=0)
    ga.begin()

    gb.turn(3)
    gb.side_turn(2)

    pair = many(me * 2 * BLOCK, 2 * BLOCK, 16)
    gb.finish_partner()
    ga.finish_partner()
    own_gate = [rowwise for rowwise in range(2)]
    for j in range(2):
        g8 = r.n_all[many((me * 2 + j) * BLOCK + 192, 16, 16), 0:256].astype(F32)[8:16, :]
        g8 = g8 + pltpu.roll(g8, 4, 0)
        g8 = jnp.where(c == 0, g8, pltpu.roll(g8, 6, 0))
        r.gcol[j * BLOCK:(j + 1) * BLOCK, :] = jnp.concatenate([g8, jnp.zeros((120, 256), F32)], axis=0).T[0:BLOCK, :]
    for copy in loads:
        copy.wait()
    r.running[...] = jnp.zeros_like(r.running)
    r.drows[...] = jnp.zeros_like(r.drows)
    r.dgate[...] = jnp.zeros_like(r.dgate)
    r.extra[...] = jnp.zeros_like(r.extra)
    pair_lane = iota((2 * BLOCK, 128), 1)
    for e in range(2):
        gate = r.gcol[:, e:e + 1]
        r.res[...] = jnp.zeros_like(r.res)
        d_result = gate * r.c_all[pair, :].astype(F32)
        r.dres[...] = half(d_result)
        r.extra[0, 2 + e:3 + e, 0:512] = column_sum(r.dres[...].astype(F32))

        def hidden_step(j, _, e=e):
            hs = many(j * STEP, STEP, STEP)
            n = r.n_all[pair, :]
            pre = dot(n, r.win[e, :, hs]) + r.bin[e:e + 1, hs].astype(F32)
            hid, slope = gelu_parts(pre)
            r.res[...] += dot(half(hid), r.wout[e, hs, :])
            d_pre = half(slope * dot_nt(r.dres[...], r.wout[e, hs, :]))
            r.extra[0, e:e + 1, hs] = column_sum(d_pre.astype(F32))
            r.drows[...] += dot_nt(d_pre, r.win[e, :, hs])
            return 0

        lax.fori_loop(0, 2, hidden_step, 0)
        if e == 0:
            ga.turn(1)
            ga.side_turn(0)
        else:
            ga.turn(3)
            ga.side_turn(2)
        lax.fori_loop(2, 4, hidden_step, 0)
        if e == 0:
            gb.side_turn(3)
            ga.turn(2)
            ga.side_turn(1)
        else:
            ga.side_turn(3)
        result = r.res[...] + r.bout[e:e + 1, :].astype(F32)
        r.running[...] += gate * result
        d_gate = jnp.sum(r.c_all[pair, :].astype(F32) * result, axis=1, keepdims=True)
        r.dgate[...] = jnp.where(pair_lane == 2 * c + e, d_gate, r.dgate[...])

    theirs, ours = many((1 - c) * BLOCK, BLOCK, 8), many(c * BLOCK, BLOCK, 8)
    partials = [remote(src.at[theirs, :], dst, r.p_send.at[i], r.p_recv.at[i], partner) for i, (src, dst) in enumerate(
        ((r.running, r.got_running), (r.drows, r.got_drows), (r.dgate, r.got_dgate)))]
    for copy in partials:
        copy.start()
    for zz in range(zs):
        gb.far(zz)
    for copy in partials:
        copy.wait()

    r.out[...] = half(r.mid[0:BLOCK, :] + (r.running[ours, :] + r.got_running[...]))[0:tokens, :]
    zeros = jnp.zeros((ROWS - BLOCK, 128), F32)
    d_gates = jnp.concatenate([r.dgate[ours, :] + r.got_dgate[...], zeros], axis=0)
    rprobs, chosen = r.rprobs[...], r.chosen[...]
    d_probs = d_gates * chosen
    d_logits = half(rprobs * (d_probs - jnp.sum(rprobs * d_probs, axis=-1, keepdims=True)))
    r.dn[0:BLOCK, :] = r.drows[ours, :] + r.got_drows[...]
    r.dn[BLOCK:ROWS, :] = jnp.zeros((ROWS - BLOCK, 512), F32)
    dn = r.dn[...] + dot_nt(d_logits, r.wroute[...])
    xhat = r.xhat2[...]
    n2 = half(xhat * gain2 + bias2)
    route_rows = dot(half(d_logits.astype(F32).T), n2)
    vector_rows = {5: column_sum(dn * xhat), 6: column_sum(dn)}
    r.xs[...] = jnp.zeros_like(r.xs)
    r.xs[0:tokens, :] = r.cot[...].astype(F32)
    d_middle = r.xs[...] + norm_back(dn, xhat, spread2, gain2)
    r.mid[...] = d_middle
    r.db[...] = half(d_middle)
    db = r.db[...]
    vector_rows[4] = column_sum(db.astype(F32))
    r.dense[:, 1536:2048] = half(dot(half(r.ctx[...].astype(F32).T), db))
    r.dctx[...] = half(dot_nt(db, r.wproj[...]))

    def heads_back(i, _):
        q, k, v = [r.mixed[:, many(base + 128 * i, 128, 128)] for base in (0, 512, 1024)]
        q = q * BF16(HEAD_DIM ** -0.5)
        do = r.dctx[:, many(128 * i, 128, 128)]
        parts = []
        for h in range(2):
            p = r.probs[2 * i + h]
            dp = dot_nt(jnp.where(low_lane == (h == 0), do, jnp.zeros_like(do)), v)
            ds = p * (dp - jnp.sum(p * dp, axis=-1, keepdims=True))
            parts.append((dot(half(ds), k) * HEAD_DIM ** -0.5, dot(half(ds.T), q), dot(half(p.T), do)))
        for j, base in enumerate((0, 512, 1024)):
            r.dmixed[:, many(base + 128 * i, 128, 128)] = half(jnp.where(low_lane, parts[0][j], parts[1][j]))
        return 0

    lax.fori_loop(0, 4, heads_back, 0)
    n1_t = half(r.n1[...].astype(F32).T)
    dn = 0.0
    for i in range(3):
        part = r.dmixed[:, 512 * i:512 * (i + 1)]
        if i != 1:
            vector_rows[2 + i // 2] = column_sum(part.astype(F32))
        r.dense[:, 512 * i:512 * (i + 1)] = half(dot(n1_t, part))
        dn = dn + dot_nt(part, r.wqkv[:, 512 * i:512 * (i + 1)])
    xhat = r.xhat1[...]
    vector_rows[0] = column_sum(dn * xhat)
    vector_rows[1] = column_sum(dn)
    r.igrad[...] = (r.mid[...] + norm_back(dn, xhat, spread1, gain1))[0:tokens, :]

    vectors = jnp.concatenate([route_rows[0:4, :]] + [vector_rows[i] for i in range(7)] + [jnp.zeros((5, 512), F32)], axis=0)
    r.dn[0:16, :] = vectors
    low_half, high_half = r.dn[0:16, 0:256], r.dn[0:16, 256:512]
    r.extra[1, :, 0:256] = jnp.where(c == 0, high_half, low_half)
    own_half = jnp.where(c == 0, low_half, high_half)
    swaps = [remote(r.dense.at[other, :], r.dense_in, r.d_send.at[0], r.d_recv.at[0], partner),
             remote(r.extra.at[1], r.extra.at[2], r.d_send.at[1], r.d_recv.at[1], partner)]
    for copy in swaps:
        copy.start()
    for zz in range(zs):
        ga.far(zz)
    for copy in swaps:
        copy.wait()
    r.total[0:256, :] = half(r.dense[mine, :].astype(F32) + r.dense_in[...].astype(F32))
    sums = own_half + r.extra[2, :, 0:256]
    small = jnp.concatenate([r.extra[0, 0:4, :], jnp.zeros((12, 2048), F32)], axis=0)
    shifted = jnp.concatenate([jnp.zeros((4, 256), F32), sums[0:12, :]], axis=0)
    r.total[256:272, :] = half(small + jnp.concatenate([shifted, jnp.zeros((16, 1792), F32)], axis=1))

    far_half = (1 - x, 1 - y)
    near_half = (x, y)
    quarter = (x * 2 + y, 4 + y * 2 + x)
    near, next_near = (xn, yn), (yn, xn)

    def cols(j, n):
        return many(j * 256, 256 * n, 256)

    def ar(i, src, dst, target):
        return remote(src, dst, r.ar_send.at[i], r.ar_recv.at[i], target)

    def ar_one(s):
        return ar(s, r.total.at[:, cols(4 * s + 2 * far_half[s], 2)], r.part_in.at[s], near[s])

    def ar_two(s):
        give = 4 * s + 2 * near_half[s] + (1 - near_half[1 - s])
        return ar(2 + s, r.total.at[:, cols(give, 1)], r.part_in.at[2 + s, :, 0:256], next_near[s])

    def ar_up(s):
        return ar(4 + s, r.z_out.at[s], r.z_in.at[s], up)

    def ar_down(s):
        return ar(6 + s, r.z_out.at[2 + s], r.z_in.at[2 + s], down)

    def ar_four(s):
        piece = r.final.at[:, cols(quarter[s], 1)]
        return ar(8 + s, piece, piece, next_near[s])

    def ar_four_got(s):
        piece = r.final.at[:, cols(4 * s + 2 * near_half[s] + (1 - near_half[1 - s]), 1)]
        return ar(8 + s, piece, piece, next_near[s])

    def ar_five(s):
        piece = r.final.at[:, cols(4 * s + 2 * near_half[s], 2)]
        return ar(10 + s, piece, piece, near[s])

    def ar_five_got(s):
        piece = r.final.at[:, cols(4 * s + 2 * far_half[s], 2)]
        return ar(10 + s, piece, piece, near[s])

    def add_into(ref, other_part):
        ref[...] = half(ref[...].astype(F32) + other_part.astype(F32))

    def ar_stage1():
        for s in range(2):
            ar_one(s).start()

    def ar_stage2():
        for s in range(2):
            ar_one(s).wait()
            add_into(r.total.at[:, cols(4 * s + 2 * near_half[s], 2)], r.part_in[s])
            ar_two(s).start()

    def ar_stage3():
        for s in range(2):
            ar_two(s).wait()
            add_into(r.total.at[:, cols(quarter[s], 1)], r.part_in[2 + s, :, 0:256])

            @pl.when(z == 0)
            def _():
                r.z_out[s] = r.total[:, cols(quarter[s], 1)]
                ar_up(s).start()

            @pl.when(z == zs - 1)
            def _():
                r.z_out[2 + s] = r.total[:, cols(quarter[s], 1)]
                ar_down(s).start()

    def ar_stage_z(k):
        for s in range(2):
            @pl.when(z == k)
            def _():
                ar_up(s).wait_recv()
                if k < zs - 1:
                    r.z_out[s] = half(r.total[:, cols(quarter[s], 1)].astype(F32) + r.z_in[s].astype(F32))
                    ar_up(s).start()

            @pl.when(z == zs - 1 - k)
            def _():
                ar_down(s).wait_recv()
                if k < zs - 1:
                    r.z_out[2 + s] = half(r.total[:, cols(quarter[s], 1)].astype(F32) + r.z_in[2 + s].astype(F32))
                    ar_down(s).start()

    def ar_stage4():
        for s in range(2):
            lower = jnp.where(low_z, r.z_in[s].astype(F32), 0.0)
            upper = jnp.where(high_z, r.z_in[2 + s].astype(F32), 0.0)
            own = r.total[:, cols(quarter[s], 1)].astype(F32)
            r.final[:, cols(quarter[s], 1)] = half(own + lower + upper)
            ar_four(s).start()

    def ar_stage5():
        for s in range(2):
            ar_four_got(s).wait_recv()
            ar_five(s).start()

    def ar_stage6():
        for s in range(2):
            ar_five_got(s).wait_recv()
            ar_four(s).wait_send()
            ar_five(s).wait_send()
            pl.when(high_z)(lambda s=s: ar_up(s).wait_send())
            pl.when(low_z)(lambda s=s: ar_down(s).wait_send())

    ar_stage1()
    for g in (gb, ga):
        g.finish()

    r.g_all[...] = jnp.zeros_like(r.g_all)
    for d in range(devices):
        g8 = r.n_all[d * BLOCK + 192:(d + 1) * BLOCK, 0:256].astype(F32)[8:16, :]
        g8 = g8 + pltpu.roll(g8, 4, 0)
        g8 = jnp.where(c == 0, g8, pltpu.roll(g8, 6, 0))
        start, shift = d * BLOCK // 128 * 128, d * BLOCK % 128
        width = min(384, devices * BLOCK - start)
        g8 = jnp.concatenate([g8, jnp.zeros((8, 128), F32)], axis=1)
        if shift:
            g8 = pltpu.roll(g8, shift, 1)
        r.g_all[:, start:start + width] += g8[:, 0:width]

    zn = (jnp.where(z % 2 == 0, rep(z + 1, y, x), rep(z - 1, y, x)), c)
    targets = (xn, yn, zn)
    qx, qy = (x + z) % 2, (y + z) % 2
    quarters = ((1 - qx) * 2 + qy, qx * 2 + 1 - qy, (1 - qx) * 2 + 1 - qy)
    own_quarter = qx * 2 + qy

    def piece(e, kind, q):
        where = many(q * STEP, STEP, STEP)
        return r.gin.at[e, :, where] if kind == 0 else r.gout.at[e, where, :]

    def source(e, kind):
        return (r.st_in if kind == 0 else r.st_out).at[e]

    def give(e, kind, i, q):
        return remote(source(e, kind), piece(e, kind, q), r.s_send.at[e, kind, i], r.s_recv.at[e, kind, i], targets[i])

    ar_stage2()
    hs = many(own_quarter * STEP, STEP, STEP)
    blocks = devices * BLOCK // STEP
    for e in range(2):
        r.acc_in[...] = jnp.zeros_like(r.acc_in)
        r.acc_out[...] = jnp.zeros_like(r.acc_out)
        wi = half(r.win[e, :, hs].astype(F32).T)
        wo = r.wout[e, hs, :]
        bias = jnp.broadcast_to(r.bin[e:e + 1, hs].astype(F32), (128, STEP)).T[:, 0:1]

        def token_step(i, _, e=e, wi=wi, wo=wo, bias=bias):
            ts = many(i * STEP, STEP, STEP)
            n, co, g = r.n_all[ts, :], r.c_all[ts, :], r.g_all[e:e + 1, ts]
            hid, slope = gelu_parts(dot_nt(wi, n) + bias)
            dh = dot_nt(wo, co)
            r.acc_out[...] += dot(half(hid * g), co)
            r.acc_in[...] += dot(half(slope * (dh * g)), n)
            return 0

        lax.fori_loop(0, blocks // 2, token_step, 0)
        if e == 0:
            ar_stage3()
        else:
            ar_stage_z(2)
            ar_stage_z(3)
            ar_stage4()
        lax.fori_loop(blocks // 2, blocks, token_step, 0)
        if e == 0:
            ar_stage_z(1)
        else:
            ar_stage5()
        r.st_in[e] = half(r.acc_in[...].T)
        r.st_out[e] = half(r.acc_out[...])
        for kind in range(2):
            for i in range(3):
                give(e, kind, i, own_quarter).start()
            pltpu.make_async_copy(source(e, kind), piece(e, kind, own_quarter), r.s_own.at[e, kind]).start()

    ar_stage6()
    r.summed[...] = r.final[...].astype(F32)
    for g in (gb, ga):
        g.drain()
    for i in range(3):
        count_copy(i, i, partner).wait_send()
    pl.when(high_z)(lambda: count_copy(3, 3, up).wait_send())
    for e in range(2):
        for kind in range(2):
            pltpu.make_async_copy(source(e, kind), piece(e, kind, own_quarter), r.s_own.at[e, kind]).wait()
            for i in range(3):
                give(e, kind, i, own_quarter).wait_send()
                give(e, kind, i, quarters[i]).wait_recv()


def block_call(zs, *args):
    devices = 8 * zs
    tokens, width = args[0].shape
    flat = devices * BLOCK
    vm, hbm = pl.BlockSpec(memory_space=pltpu.VMEM), pl.BlockSpec(memory_space=pl.ANY)
    shape = jax.ShapeDtypeStruct
    in_specs = [hbm if name in ("win_in", "wout_in") else vm for name in INPUTS]
    scratch = [pltpu.VMEM(tuple(flat if d is None else d for d in dims), dtype) for _, dims, dtype in SCRATCH]
    scratch += [pltpu.SemaphoreType.DMA(tuple(4 * zs if d is None else d for d in dims)) for _, dims in SEMS]
    return pl.pallas_call(
        functools.partial(block_kernel, zs),
        out_shape=(shape((tokens, width), BF16), shape((tokens, width), F32), shape((2, 512, 2048), BF16),
                   shape((2, 2048, 512), BF16), shape((272, 2048), F32)),
        in_specs=in_specs,
        out_specs=(vm, vm, hbm, hbm, vm),
        scratch_shapes=scratch,
        compiler_params=pltpu.CompilerParams(collective_id=0, has_side_effects=True, vmem_limit_bytes=60 << 20),
        name="encoder_block",
    )(*args)


def swap(v):
    return lax.ppermute(v, "shard", [(0, 1), (1, 0)])


def fused(inputs, norm1_gain, norm1_bias, qkv_weight, query_bias, value_bias, out_weight, out_bias, norm2_gain, norm2_bias,
          router_weight, noise, expert_in, expert_in_bias, expert_out, expert_out_bias, routes, priority, cotangent):
    vectors = (norm1_gain, norm1_bias, query_bias, value_bias, out_bias, norm2_gain, norm2_bias)
    vec = jnp.concatenate(vectors + (jnp.zeros_like(norm1_gain),)).astype(F32).reshape(8, -1)
    out, igrad, gin, gout, summed = block_call(
        lax.axis_size("replica") // 4, inputs, cotangent, noise, routes, priority, vec, qkv_weight, out_weight,
        jnp.pad(router_weight, ((0, 0), (0, 124))), expert_in, expert_out, expert_in_bias, expert_out_bias)
    rows = summed[256:272]
    columns = [rows[8 + i, 0:256] for i in range(7)]
    return (
        out, igrad, columns[0], columns[1], summed[0:256, 0:1536], columns[2], columns[3], summed[0:256, 1536:2048],
        columns[4], columns[5], columns[6], rows[4:8, 0:256].T, gin.astype(F32), rows[0:2], gout.astype(F32),
        rows[2:4, 0:512],
    )


def layer_norm(values, gain_vector, bias_vector):
    centered = values - jnp.mean(values, axis=-1, keepdims=True)
    spread = lax.rsqrt(jnp.mean(centered * centered, axis=-1, keepdims=True) + LN_EPS)
    return centered * spread * gain_vector + bias_vector


def kept_gates(pair_expert, ranks, offsets, capacity, expert_count):
    same = pair_expert[:, None] == pair_expert[None, :]
    earlier = ranks[None, :] < ranks[:, None]
    before = jnp.sum(jnp.where(same & earlier, 1, 0).astype(jnp.int32), axis=1)
    onehot = pair_expert[:, None] == jnp.arange(expert_count, dtype=jnp.int32)[None, :]
    first_slot = jnp.sum(jnp.where(onehot, offsets[None, :], 0).astype(jnp.int32), axis=1)
    keep = before + first_slot < capacity
    picked = jnp.where(onehot & keep[:, None], 1.0, 0.0).astype(jnp.float32)
    return jnp.sum(picked.reshape(-1, 2, expert_count), axis=1)


def general(
    inputs, norm1_gain, norm1_bias, qkv_weight, query_bias, value_bias, out_weight, out_bias, norm2_gain, norm2_bias,
    router_weight, noise, expert_in, expert_in_bias, expert_out, expert_out_bias, routes, priority, cotangent,
):
    tok_count, width = inputs.shape
    replicas, cores = lax.axis_size("replica"), lax.axis_size("shard")
    shard = lax.axis_index("shard")
    images = tok_count // PATCHES
    heads = width // HEAD_DIM
    owned, _, hidden_count = expert_in.shape
    expert_count = owned * cores
    score_scale = HEAD_DIM ** (-0.5)
    f32 = jnp.float32

    vectors = (norm1_gain, norm1_bias, query_bias, value_bias, out_bias, norm2_gain, norm2_bias)
    packed = jnp.concatenate(
        [qkv_weight, out_weight, jnp.stack(vectors, axis=1), router_weight], axis=1)
    packed = lax.all_gather(packed, "shard", axis=0, tiled=True)
    weight_qkv = packed[:, :3 * width]
    weight_proj = packed[:, 3 * width:4 * width]
    small = packed[:, 4 * width:]
    gain_one, bias_one, bias_query, bias_value, bias_proj, gain_two, bias_two = [
        small[:, i].astype(f32) for i in range(len(vectors))]
    weight_route = small[:, len(vectors):]

    pair_expert = routes.reshape(-1)
    onehot_pairs = (pair_expert[:, None] == jnp.arange(expert_count, dtype=jnp.int32)[None, :]).astype(jnp.int32)
    load = jnp.sum(onehot_pairs, axis=0)
    loads = lax.all_gather(load, ("replica", "shard"))
    position = lax.axis_index("replica") * cores + shard
    ahead = jnp.arange(replicas * cores)[:, None] < position
    offsets = jnp.sum(jnp.where(ahead, loads, 0), axis=0)
    capacity = 2 * tok_count * replicas * cores // expert_count
    chosen = kept_gates(pair_expert, priority.reshape(-1), offsets, capacity, expert_count)

    residual_in = inputs.astype(f32)
    normed_one, norm_one_back = jax.vjp(layer_norm, residual_in, gain_one, bias_one)
    normed_one_half = half(normed_one)
    qkv_bias = jnp.concatenate([bias_query, jnp.zeros_like(bias_query), bias_value])
    mixed = half(dot(normed_one_half, weight_qkv) + qkv_bias)
    shaped = mixed.reshape(images, PATCHES, 3, heads, HEAD_DIM)
    query, keys, values = (shaped[:, :, 0], shaped[:, :, 1], shaped[:, :, 2])
    scores = jnp.einsum("bqhd,bkhd->bhqk", query, keys, preferred_element_type=f32) * score_scale
    row_max = jnp.max(scores, axis=-1, keepdims=True)
    log_total = row_max + jnp.log(jnp.sum(jnp.exp(scores - row_max), axis=-1, keepdims=True))
    context = jnp.einsum(
        "bhqk,bkhd->bqhd", half(jnp.exp(scores - log_total)), values, preferred_element_type=f32)
    context_half = half(context.reshape(tok_count, width))
    middle = residual_in + (dot(context_half, weight_proj) + bias_proj)
    normed_two, norm_two_back = jax.vjp(layer_norm, middle, gain_two, bias_two)
    normed_two_half = half(normed_two)
    logits = dot(normed_two_half, weight_route) + noise
    route_probs = jax.nn.softmax(logits, axis=-1)
    gate_weights = route_probs * chosen
    upstream = cotangent.astype(f32)

    pair_n = jnp.concatenate([normed_two_half, swap(normed_two_half)], axis=0)
    pair_c = jnp.concatenate([cotangent, swap(cotangent)], axis=0)
    own_gates = lax.dynamic_slice_in_dim(gate_weights, shard * owned, owned, 1)
    other_gates = swap(lax.dynamic_slice_in_dim(gate_weights, (1 - shard) * owned, owned, 1))
    pair_g = jnp.concatenate([own_gates, other_gates], axis=0)
    pair_up = pair_c.astype(f32)
    running = jnp.zeros((2 * tok_count, width), f32)
    d_rows = jnp.zeros((2 * tok_count, width), f32)
    gate_columns, bias_in_grads, bias_out_grads, in_grads, out_grads = [], [], [], [], []
    for e in range(owned):
        gate = pair_g[:, e:e + 1]
        pre = dot(pair_n, expert_in[e]) + expert_in_bias[e].astype(f32)
        act, slope = gelu_parts(pre)
        hid = half(act)
        result = dot(hid, expert_out[e]) + expert_out_bias[e].astype(f32)
        running = running + gate * result
        gate_columns.append(jnp.sum(pair_up * result, axis=1))
        d_result = half(gate * pair_up)
        d_pre = half(slope * dot_nt(d_result, expert_out[e]))
        d_rows = d_rows + dot_nt(d_pre, expert_in[e])
        bias_in_grads.append(jnp.sum(d_pre.astype(f32), axis=0))
        bias_out_grads.append(jnp.sum(d_result.astype(f32), axis=0))
        in_grads.append(jnp.einsum("td,th->dh", pair_n, d_pre, preferred_element_type=f32))
        out_grads.append(jnp.einsum("th,td->hd", hid, d_result, preferred_element_type=f32))
    d_gate_part = jnp.stack(gate_columns, axis=1)
    running = running[:tok_count] + swap(running[tok_count:])
    d_normed = d_rows[:tok_count] + swap(d_rows[tok_count:])
    d_gate_other = swap(d_gate_part[tok_count:])
    d_gate_own = d_gate_part[:tok_count]
    d_gates = jnp.where(shard == 0, jnp.concatenate([d_gate_own, d_gate_other], axis=1),
                        jnp.concatenate([d_gate_other, d_gate_own], axis=1))

    grad_in = lax.psum(half(jnp.stack(in_grads, axis=0)), "replica")
    grad_out = lax.psum(half(jnp.stack(out_grads, axis=0)), "replica")

    output = half(middle + running)
    d_probs = d_gates * chosen
    d_logits = half(route_probs * (d_probs - jnp.sum(route_probs * d_probs, axis=-1, keepdims=True)))
    grad_route = jnp.einsum("td,te->de", normed_two_half, d_logits, preferred_element_type=f32)
    d_normed = d_normed + dot_nt(d_logits, weight_route)
    d_middle, grad_gain_two, grad_bias_two = norm_two_back(d_normed)
    d_middle = d_middle + upstream
    d_branch = half(d_middle)
    grad_proj = jnp.einsum("tc,td->cd", context_half, d_branch, preferred_element_type=f32)
    grad_proj_bias = jnp.sum(d_branch.astype(f32), axis=0)
    d_context = half(dot_nt(d_branch, weight_proj)).reshape(images, PATCHES, heads, HEAD_DIM)
    attn_probs = jnp.exp(scores - log_total)
    d_attn = jnp.einsum("bqhd,bkhd->bhqk", d_context, values, preferred_element_type=f32)
    d_values = jnp.einsum("bhqk,bqhd->bkhd", half(attn_probs), d_context, preferred_element_type=f32)
    d_scores = half(attn_probs * (d_attn - jnp.sum(attn_probs * d_attn, axis=-1, keepdims=True)))
    d_query = jnp.einsum("bhqk,bkhd->bqhd", d_scores, keys, preferred_element_type=f32) * score_scale
    d_keys = jnp.einsum("bhqk,bqhd->bkhd", d_scores, query, preferred_element_type=f32) * score_scale
    d_mixed = half(jnp.stack([d_query, d_keys, d_values], axis=2).reshape(tok_count, 3 * width))
    grad_qkv = jnp.einsum("td,tf->df", normed_one_half, d_mixed, preferred_element_type=f32)
    mixed_sums = jnp.sum(d_mixed.astype(f32), axis=0)
    d_normed_one = dot_nt(d_mixed, weight_qkv)
    d_input, grad_gain_one, grad_bias_one = norm_one_back(d_normed_one)
    input_grad = d_input + d_middle

    columns = jnp.stack((grad_gain_one, grad_bias_one, mixed_sums[:width], mixed_sums[2 * width:], grad_proj_bias,
                         grad_gain_two, grad_bias_two), axis=1)
    dense = half(jnp.concatenate([grad_qkv, grad_proj, columns, grad_route], axis=1))
    mine = width // 2
    keep = lax.dynamic_slice_in_dim(dense, shard * mine, mine, 0)
    give = lax.dynamic_slice_in_dim(dense, (1 - shard) * mine, mine, 0)
    dense = keep.astype(f32) + swap(give).astype(f32)
    bias_row = jnp.concatenate(bias_in_grads + bias_out_grads)
    summed, bias_row = lax.psum((half(dense), bias_row), "replica")
    summed = summed.astype(f32)
    columns = [summed[:, 4 * width + i] for i in range(len(vectors))]
    grad_in_bias = bias_row[:owned * hidden_count].reshape(owned, hidden_count)
    grad_out_bias = bias_row[owned * hidden_count:].reshape(owned, width)
    return (
        output, input_grad, columns[0], columns[1], summed[:, :3 * width], columns[2], columns[3],
        summed[:, 3 * width:4 * width], columns[4], columns[5], columns[6], summed[:, 4 * width + len(vectors):],
        grad_in.astype(f32), grad_in_bias, grad_out.astype(f32), grad_out_bias,
    )


def on_device(*args):
    expert_in, inputs = args[12], args[0]
    planes = lax.axis_size("replica") == 16 and lax.axis_size("shard") == 2
    if planes and inputs.shape == (PATCHES, 512) and expert_in.shape == (2, 512, 2048):
        return fused(*args)
    return general(*args)


def solution(mesh):
    both, split = ("replica", "shard"), "shard"
    return jax.shard_map(
        on_device,
        mesh=mesh,
        in_specs=(
            P(both, None), P(split), P(split), P(split, None), P(split), P(split), P(split, None), P(split), P(split),
            P(split), P(split, None), P(both, None), P(split, None, None), P(split, None), P(split, None, None),
            P(split, None), P(both, None), P(both, None), P(both, None),
        ),
        out_specs=(
            P(both, None), P(both, None), P(split), P(split), P(split, None), P(split), P(split), P(split, None),
            P(split), P(split), P(split), P(split, None), P(split, None, None), P(split, None), P(split, None, None),
            P(split, None),
        ),
        check_vma=False,
    )
```

time: 440 us -> 216 us (0.49)
  blocking collectives: 158 us -> 0 us
  matrix products: 32 us -> 0 us
  local copies, waits for them, and re-layouts: 49.2 us -> 22.7 us
  Pallas kernels: 157 us -> 183 us
  other arithmetic: 24.5 us -> 9.05 us
  between operations: 14.7 us -> 0.68 us
    psum x1 -> x0, blocking collectives: 75.7 us -> none  [on_device(): summed, bias_row = lax.psum((half(dense), bias_row), 'replica')]
    unnamed x1 -> x0, blocking collectives: 41.5 us -> none
    all_gather x1 -> x0, blocking collectives: 40.8 us -> none  [on_device(): gates_all = lax.all_gather(gates_pad, ('replica', 'shard'), axis=0)]
    dot_general x23 -> x0, matrix products: 32 us -> none  [the longest x7 14.3 us: dot_nt(): return lax.dot_general(a, b, NT, preferred_element_type=jnp.float32)]
    pallas_call x2 -> x1, Pallas kernels: 157 us -> 183 us  [block_call(): pl.pallas_call(functools.partial(block_kernel, zs), out_shape=(shape((tok...]
    another operation x15 -> x0, local copies, waits for them, and re-layouts: 12 us -> none  [the longest x7 5.74 us: on_device(): jnp.stack((grad_gain_one, grad_bias_one, mixed_sums[:width], mixed_sums[2...]
    convert_element_type x7 -> x2, other arithmetic: 18.4 us -> 9.05 us  [the longest x1 4.6 us: fused(): gout.astype(F32)]
    dynamic_slice x5 -> x0, local copies, waits for them, and re-layouts: 7.89 us -> none  [the longest x2 3.36 us: on_device(): give = lax.dynamic_slice_in_dim(dense, (1 - shard) * mine, mine, 0)]
  transfers between devices with their start and end apart: 9 -> 0, of which waited for: 2 -> 0; matrix products, arithmetic and copies ran while one was open for 10% -> 0% of each run, Pallas kernels for 36% -> 0%
where the time goes in v2:
time: 216 us
  Pallas kernels  183 us (85%)
  local copies, waits for them, and re-layouts  22.7 us (11%)
  other arithmetic  9.05 us (4%)
    pallas_call x1, Pallas kernels, block_call(): pl.pallas_call(functools.partial(block_kernel, zs), out_shape=(shape((tok...  183 us
    unnamed x20, local copies, waits for them, and re-layouts  11 us
    convert_element_type x1, other arithmetic, fused(): gout.astype(F32)  4.6 us
    convert_element_type x1, other arithmetic, fused(): gin.astype(F32)  4.45 us

profile of v2, /device:TPU:0, one launch (start us, length us, event | category | flops | bytes accessed | tf_op | source)
XLA Modules:
  0.0 215.8 jit_solution(8688723938735825847)
XLA Ops:
  0.7 0.9 dynamic-update-slice
  1.5 0.8 dynamic-update-slice.1
  2.3 0.8 dynamic-update-slice.2
  3.2 0.8 dynamic-update-slice.3
  4.0 0.8 dynamic-update-slice.4
  4.8 0.8 dynamic-update-slice.5
  5.7 0.8 dynamic-update-slice.6
  6.5 0.2 dynamic-update-slice.7
  6.7 0.6 reshape.36.refs_5_
  7.3 0.8 copy.35
  8.1 0.6 pad.4.refs_8_
  8.8 1.5 copy.36.refs_2_
  10.2 1.4 copy.37.refs_3_
  11.7 183.3 %encoder_block.1 = (bf16[197,512]{1,0:T(8,128)(2,1)}, f32[197,512]{1,0:T(8,128)}, bf16[2,512,2048]{2,1,0:T(8,128)(2,1)}, bf16[2,2048,512]{2,1,0:T(8,128)(2,1)}, f32[272,2048]{1,0:T(8,128)}) custom-call(bf16[197,512]{1,0:T(8,128)(2,1)} %refs_0_.1, bf16[197,512]{1,0:T(8,128)(2,1)} %refs_1_.1, f32[197,4]{1,0:T(8,128)} %copy.36.refs_2_, s32[197,2]{1,0:T(8,128)} %copy.37.refs_3_, ...), custom_call_target="tpu_custom_call" | custom-call | tf_op jit(solution)/shard_map/encoder_block/pallas_call | solution.py:710
  195.0 1.4 slice_bitcast_fusion
  196.5 1.3 slice.58
  197.8 1.5 fusion
  199.3 1.4 slice.57
  200.8 1.9 slice.52
  202.6 2.7 %slice.49 = f32[256,1536]{1,0:T(8,128)} slice(f32[272,2048]{1,0:T(8,128)} %get-tuple-element.23), slice={[0:256], [0:1536]} | slice | bytes 3145728 | tf_op jit(solution)/shard_map/slice | solution.py:736
  205.3 4.4 %convert_element_type.17 = f32[2,512,2048]{2,1,0:T(8,128)} convert(bf16[2,512,2048]{2,1,0:T(8,128)(2,1)S(1)} %copy-done.1) | non-fusion elementwise | flops 2097152 | bytes 12582912 | tf_op jit(solution)/shard_map/convert_element_type | solution.py:737
  209.8 4.6 %convert_element_type.18 = f32[2,2048,512]{2,1,0:T(8,128)} convert(bf16[2,2048,512]{2,1,0:T(8,128)(2,1)S(1)} %copy-done) | non-fusion elementwise | flops 2097152 | bytes 12582912 | tf_op jit(solution)/shard_map/convert_element_type | solution.py:737
  214.4 0.7 copy.48
  215.0 0.8 copy.49
  (10 shorter events, 0.0 us)
Async XLA Ops:
  195.0 10.3 %copy-start.1 = (bf16[2,512,2048]{2,1,0:T(8,128)(2,1)S(1)}, bf16[2,512,2048]{2,1,0:T(8,128)(2,1)}, u32[]{:S(2)}) copy-start(bf16[2,512,2048]{2,1,0:T(8,128)(2,1)} %get-tuple-element.24) | copy-start | bytes 12582916
  205.3 4.5 %copy-start = (bf16[2,2048,512]{2,1,0:T(8,128)(2,1)S(1)}, bf16[2,2048,512]{2,1,0:T(8,128)(2,1)}, u32[]{:S(2)}) copy-start(bf16[2,2048,512]{2,1,0:T(8,128)(2,1)} %get-tuple-element.25) | copy-start | bytes 12582916
  209.8 4.6 %copy-start.3 = (bf16[197,512]{1,0:T(8,128)(2,1)S(1)}, bf16[197,512]{1,0:T(8,128)(2,1)}, u32[]{:S(2)}) copy-start(bf16[197,512]{1,0:T(8,128)(2,1)} %get-tuple-element.49) | copy-start | bytes 605188
  209.8 5.3 %copy-start.2 = (f32[197,512]{1,0:T(8,128)S(1)}, f32[197,512]{1,0:T(8,128)}, u32[]{:S(2)}) copy-start(f32[197,512]{1,0:T(8,128)} %get-tuple-element.50) | copy-start | bytes 1210372

commit v3 on v2

v3 whole, which is shorter than its diff:
```python
import functools
from types import SimpleNamespace

import jax
import jax.numpy as jnp
from jax import lax
from jax.experimental import pallas as pl
from jax.experimental.pallas import tpu as pltpu
from jax.sharding import PartitionSpec as P

HEAD_DIM = 64
PATCHES = 197
LN_EPS = 1e-06
MESH = pl.DeviceIdType.MESH
NT = (((1,), (1,)), ((), ()))
GELU_K = 0.7978845608028654
GELU_A = 0.044715
F32 = jnp.float32
BF16 = jnp.bfloat16
ROWS = 256
BLOCK = 208
STEP = 512
SLICE = 256
PIECE = 64
STEPS = 6
PIECES = STEPS * 2 * SLICE // PIECE
SETS = 2 * 2 * SLICE // PIECE
HOP = 3
TICKS = 3
PASS = 8


def half(values):
    return values.astype(BF16)


def dot(a, b):
    return jnp.dot(a, b, preferred_element_type=F32)


def dot_nt(a, b):
    return lax.dot_general(a, b, NT, preferred_element_type=F32)


def gelu_parts(x):
    x2 = x * x
    q = 0.5 + 0.5 * jnp.tanh(x * (GELU_K + (GELU_K * GELU_A) * x2))
    h = x * q
    return h, q + (h * (1.0 - q)) * (2 * GELU_K + (6 * GELU_K * GELU_A) * x2)


def iota(shape, dim):
    return lax.broadcasted_iota(jnp.int32, shape, dim)


def many(start, size, unit):
    return pl.ds(pl.multiple_of(start, unit), size)


def normalize(v):
    centered = v - jnp.mean(v, axis=-1, keepdims=True)
    spread = lax.rsqrt(jnp.mean(centered * centered, axis=-1, keepdims=True) + LN_EPS)
    return centered * spread, spread


def norm_back(d, xhat, spread, gain):
    dx = d * gain
    return spread * (dx - jnp.mean(dx, axis=-1, keepdims=True) - xhat * jnp.mean(dx * xhat, axis=-1, keepdims=True))


def column_sum(v):
    return jnp.sum(v, axis=0, keepdims=True)


def place():
    r = lax.axis_index("replica")
    return r // 4, (r // 2) % 2, r % 2, lax.axis_index("shard")


def rep(z, y, x):
    return (z * 2 + y) * 2 + x


class PlaneGather:
    def __init__(self, x_first, rows, sems):
        self.rows = rows
        self.send, self.recv, self.core_send, self.core_recv = sems
        z, y, x, c = place()
        near = ((rep(z, y, 1 - x), c), (rep(z, 1 - y, x), c))
        spots = (y * 2 + 1 - x, (1 - y) * 2 + x)
        self.targets = near if x_first else near[::-1]
        self.first, self.second = spots if x_first else spots[::-1]
        self.me, self.diagonal = y * 2 + x, (1 - y) * 2 + 1 - x
        self.core, self.partner = c, (rep(z, y, x), 1 - c)

    def ref(self, spot, core):
        return self.rows.at[many((spot * 2 + core) * BLOCK, BLOCK, 16), :]

    def link(self, kind, spot):
        ref = self.ref(spot, self.core)
        return remote(ref, ref, self.send.at[kind, spot], self.recv.at[spot], self.targets[kind])

    def across(self, spot, core=None):
        ref = self.ref(spot, self.core if core is None else core)
        return remote(ref, ref, self.core_send.at[spot], self.core_recv.at[spot], self.partner)

    def begin(self):
        self.link(0, self.me).start()
        self.link(1, self.me).start()
        self.across(self.me).start()

    def turn(self):
        self.link(0, self.first).wait_recv()
        self.link(1, self.first).start()
        self.across(self.first).start()

    def far(self):
        for spot in (self.second, self.diagonal):
            self.link(0, spot).wait_recv()
            self.across(spot).start()

    def from_core(self, spot):
        self.across(spot, 1 - self.core).wait_recv()

    def drain(self):
        for kind, spot in ((0, self.me), (1, self.me), (1, self.first)):
            self.link(kind, spot).wait_send()
        for spot in range(4):
            self.across(spot).wait_send()


SCRATCH = (
    ("n_all", (8 * BLOCK, 512), BF16), ("c_all", (8 * BLOCK, 512), BF16), ("g_all", (8, 8 * BLOCK), F32),
    ("wqkv", (512, 1536), BF16), ("wproj", (512, 512), BF16), ("vec", (2, 16, 256), F32), ("binf", (2, 2048), F32),
    ("win", (2, 512, 2048), BF16), ("wout", (2, 2048, 512), BF16),
    ("count_out", (3, 8, 128), F32), ("count_in", (9, 8, 128), F32),
    ("xs", (ROWS, 512), F32), ("pairs", (16, ROWS), F32),
    ("xhat1", (ROWS, 512), F32), ("n1", (ROWS, 512), BF16), ("mixed", (ROWS, 1536), BF16),
    ("probs", (8, ROWS, ROWS), F32), ("ctx", (ROWS, 512), BF16), ("mid", (ROWS, 512), F32), ("xhat2", (ROWS, 512), F32),
    ("chosen", (ROWS, 128), F32), ("rprobs", (ROWS, 128), F32),
    ("res", (2 * BLOCK, 512), F32), ("running", (2 * BLOCK, 512), F32), ("drows", (2 * BLOCK, 512), F32),
    ("dgate", (2 * BLOCK, 128), F32), ("dres", (2 * BLOCK, 512), BF16), ("gcol", (2 * BLOCK, 128), F32),
    ("got_running", (BLOCK, 512), F32), ("got_drows", (BLOCK, 512), F32), ("got_dgate", (BLOCK, 128), F32),
    ("db", (ROWS, 512), BF16), ("dctx", (ROWS, 512), BF16), ("dmixed", (ROWS, 1536), BF16), ("dn", (ROWS, 512), F32),
    ("dense", (512, 2048), BF16), ("dense_in", (256, 2048), BF16), ("extra", (3, 16, 2048), F32),
    ("total", (272, 2048), BF16), ("part_in", (4, 272, 512), BF16), ("z_out", (4, 272, 256), BF16), ("z_in", (4, 272, 256), BF16),
    ("own", (PIECES, PIECE, 512), BF16), ("up_in", (PIECES, PIECE, 512), BF16), ("up_out", (PIECES, PIECE, 512), BF16),
    ("down_in", (PIECES, PIECE, 512), BF16), ("down_out", (PIECES, PIECE, 512), BF16), ("fin", (PIECES, PIECE, 512), BF16),
)
SEMS = (
    ("g_send", (2, 2, 4)), ("g_recv", (2, 4)), ("g_csend", (2, 4)), ("g_crecv", (2, 4)),
    ("load", (2,)), ("w_send", (3,)), ("w_recv", (3,)), ("count_send", (7,)), ("count_recv", (9,)),
    ("p_send", (3,)), ("p_recv", (3,)), ("d_send", (2,)), ("d_recv", (2,)),
    ("ar_send", (12,)), ("ar_recv", (12,)), ("up_recv", (PIECES,)), ("down_recv", (PIECES,)), ("bulk", (9,)),
    ("x_recv", (SETS,)), ("y_recv", (SETS,)),
)
INPUTS = ("x", "cot", "noise_in", "routes_in", "prio", "v0", "v1", "v2", "v3", "v4", "v5", "v6", "route_in", "wqkv_in",
          "wproj_in", "win_in", "wout_in", "bin", "bout")
OUTPUTS = ("out", "igrad", "grads", "final")


def remote(src, dst, send, recv, target):
    return pltpu.make_async_remote_copy(
        src_ref=src, dst_ref=dst, send_sem=send, recv_sem=recv, device_id=target, device_id_type=MESH)


def block_kernel(zs, *refs):
    names = INPUTS + OUTPUTS + tuple(n for n, _, _ in SCRATCH) + tuple(n for n, _ in SEMS)
    r = SimpleNamespace(**dict(zip(names, refs, strict=True)))
    z, y, x, c = place()
    me = rep(z, y, x)
    partner = (me, 1 - c)
    xn, yn = (rep(z, y, 1 - x), c), (rep(z, 1 - y, x), c)
    up, down = (rep(z + 1, y, x), c), (rep(z - 1, y, x), c)
    low_z, high_z = z > 0, z < zs - 1
    tokens = r.x.shape[0]
    devices = 8 * zs
    capacity = 2 * tokens * devices // 4

    bar = pltpu.get_barrier_semaphore()
    for d in range(1, zs):
        peer = (rep(lax.rem(z + d, zs), y, x), c)
        pl.semaphore_signal(bar, inc=1, device_id=peer, device_id_type=MESH)
    for peer in (xn, yn, (rep(z, 1 - y, 1 - x), c), partner):
        pl.semaphore_signal(bar, inc=1, device_id=peer, device_id_type=MESH)

    loads = [pltpu.make_async_copy(r.win_in, r.win, r.load.at[0]), pltpu.make_async_copy(r.wout_in, r.wout, r.load.at[1])]
    for copy in loads:
        copy.start()

    r.xs[...] = jnp.zeros_like(r.xs)
    r.xs[0:tokens, :] = r.cot[...].astype(F32)
    own_rows = many(((y * 2 + x) * 2 + c) * BLOCK, BLOCK, 16)
    r.c_all[own_rows, :] = half(r.xs[0:BLOCK, :])
    mine, other = many(c * 256, 256, 16), many((1 - c) * 256, 256, 16)
    r.wqkv[mine, :] = r.wqkv_in[...]
    r.wproj[mine, :] = r.wproj_in[...]
    rows = [ref[...].astype(F32).reshape(1, 256) for ref in (r.v0, r.v1, r.v2, r.v3, r.v4, r.v5, r.v6)]
    rows += [jnp.zeros((1, 256), F32), r.route_in[...].astype(F32), jnp.zeros((4, 256), F32)]
    r.vec[c] = jnp.concatenate(rows, axis=0)
    r.binf[...] = r.bin[...].astype(F32)

    pl.semaphore_wait(bar, zs + 3)

    weights = [remote(ref, ref, r.w_send.at[i], r.w_recv.at[i], partner) for i, ref in enumerate(
        (r.vec.at[c], r.wqkv.at[mine, :], r.wproj.at[mine, :]))]
    for copy in weights:
        copy.start()
    gathers = [PlaneGather(m == 0, (r.n_all, r.c_all)[m],
                           (r.g_send.at[m], r.g_recv.at[m], r.g_csend.at[m], r.g_crecv.at[m])) for m in range(2)]
    ga, gb = gathers
    gb.begin()

    lane, row = iota((ROWS, 128), 1), iota((ROWS, 128), 0)
    r.pairs[0:8, :] = jnp.full((8, ROWS), -1.0, F32)
    r.pairs[8:16, :] = jnp.zeros((8, ROWS), F32)
    r.pairs[0:2, 0:tokens] = r.routes_in[...].astype(F32)
    r.pairs[8:12, 0:tokens] = r.noise_in[...]
    by_token = jnp.concatenate([r.pairs[...], jnp.zeros((112, ROWS), F32)], axis=0).T
    experts = [by_token[:, k:k + 1] for k in range(2)]
    noise = pltpu.roll(by_token, 120, 1)
    onehot = [jnp.where(lane.astype(F32) == experts[k], 1.0, 0.0) for k in range(2)]
    count = jnp.broadcast_to(column_sum(onehot[0] + onehot[1]), (8, 128))

    def count_copy(stage, i, slot, target):
        return remote(r.count_out.at[stage], r.count_in.at[slot], r.count_send.at[i], r.count_recv.at[slot], target)

    spot = y * 2 + x
    column = [(rep(k, y, x), c) for k in range(zs)]

    def counts_to_plane():
        for d in range(1, 4):
            q = lax.rem(spot + d, 4)
            count_copy(1, d, 1 + spot, (rep(z, q // 2, lax.rem(q, 2)), c)).start()

    def counts_up():
        for k in range(1, zs):
            pl.when(z < k)(lambda k=k: count_copy(2, 3 + k, 5 + z, column[k]).start())

    r.count_out[0] = count
    count_copy(0, 0, 0, partner).start()

    places = iota((ROWS, r.prio.shape[1]), 1) - 2 * iota((ROWS, r.prio.shape[1]), 0)
    ranks = r.prio[...].astype(F32)
    codes = [experts[k] * 1024.0 + jnp.sum(jnp.where(places == k, ranks, 0.0), axis=1, keepdims=True) for k in range(2)]
    codes = [jnp.where(row[:, 0:1] < tokens, code, -1.0) for code in codes]
    code_rows = jnp.where(lane == 0, codes[0], jnp.where(lane == 1, codes[1], 0.0)).T
    before = []
    for k in range(2):
        floor = experts[k] * 1024.0
        seen = 0.0
        for j in range(2):
            others = code_rows[j:j + 1, :]
            seen = seen + jnp.where((others < codes[k]) & (others >= floor), 1.0, 0.0)
        before.append(jnp.sum(seen, axis=1, keepdims=True))

    count_copy(0, 0, 0, partner).wait_recv()
    ahead = jnp.where(c == 1, 1.0, 0.0) * r.count_in[0]
    count = count + r.count_in[0]
    r.count_out[1] = count
    counts_to_plane()

    weights[0].wait_send()
    remote(r.vec.at[1 - c], r.vec.at[1 - c], r.w_send.at[0], r.w_recv.at[0], partner).wait_recv()
    vec = jnp.concatenate([r.vec[0], r.vec[1]], axis=1)
    gain1, bias1, bias_q, bias_v, bias_p, gain2, bias2 = [vec[i:i + 1, :] for i in range(7)]
    route_rows = jnp.concatenate([vec[8:16, :], jnp.zeros((120, 512), F32)], axis=0)
    route_t, route = half(route_rows), half(route_rows.T)
    r.xs[0:tokens, :] = r.x[...].astype(F32)
    xhat, spread1 = normalize(r.xs[...])
    r.xhat1[...] = xhat
    r.n1[...] = half(xhat * gain1 + bias1)

    for q in range(4):
        pl.when(spot != q)(lambda q=q: count_copy(1, 1, 1 + q, partner).wait_recv())
    for q in range(4):
        ahead = ahead + jnp.where(spot > q, r.count_in[1 + q], 0.0)
        count = count + jnp.where(spot != q, r.count_in[1 + q], 0.0)
    r.count_out[2] = count
    counts_up()

    for i, ref in ((1, r.wqkv), (2, r.wproj)):
        weights[i].wait_send()
        ref = ref.at[other, :]
        remote(ref, ref, r.w_send.at[i], r.w_recv.at[i], partner).wait_recv()
    for i, bias in enumerate((bias_q, None, bias_v)):
        part = dot(r.n1[...], r.wqkv[:, 512 * i:512 * (i + 1)])
        r.mixed[:, 512 * i:512 * (i + 1)] = half(part if bias is None else part + bias)

    low_lane = lane < HEAD_DIM
    key_kept = iota((ROWS, ROWS), 1) < tokens

    def heads_forward(i, _):
        q, k, v = [r.mixed[:, many(base + 128 * i, 128, 128)] for base in (0, 512, 1024)]
        q = q * BF16(HEAD_DIM ** -0.5)
        parts = []
        for h in range(2):
            s = dot_nt(jnp.where(low_lane == (h == 0), q, jnp.zeros_like(q)), k)
            s = jnp.where(key_kept, s, -1e30)
            e = jnp.exp(s - jnp.max(s, axis=-1, keepdims=True))
            p = e / jnp.sum(e, axis=-1, keepdims=True)
            r.probs[2 * i + h] = p
            parts.append(dot(half(p), v))
        r.ctx[:, many(128 * i, 128, 128)] = half(jnp.where(low_lane, parts[0], parts[1]))
        return 0

    lax.fori_loop(0, 4, heads_forward, 0)

    gb.turn()

    for k in range(zs - 1):
        pl.when(z > k)(lambda k=k: count_copy(2, 4, 5 + k, partner).wait_recv())
    for k in range(zs - 1):
        ahead = ahead + jnp.where(z > k, r.count_in[5 + k], 0.0)
    offsets = ahead[0:1, :]
    chosen = 0.0
    for k in range(2):
        slot = before[k] + jnp.sum(onehot[k] * offsets, axis=1, keepdims=True)
        chosen = chosen + onehot[k] * jnp.where(slot < float(capacity), 1.0, 0.0)
    r.chosen[...] = chosen

    middle = r.xs[...] + (dot(r.ctx[...], r.wproj[...]) + bias_p)
    r.mid[...] = middle
    xhat, spread2 = normalize(middle)
    r.xhat2[...] = xhat
    n2 = half(xhat * gain2 + bias2)
    logits = jnp.where(lane < 4, dot(n2, route) + noise, -1e30)
    e = jnp.exp(logits - jnp.max(logits, axis=-1, keepdims=True))
    rprobs = e / jnp.sum(e, axis=-1, keepdims=True)
    r.rprobs[...] = rprobs
    gates = rprobs * chosen
    gates_high = half(gates).astype(F32)
    packed = jnp.where(lane < 4, gates_high, pltpu.roll(gates - gates_high, 4, 1)).T
    packed = jnp.concatenate([packed[0:8, :], jnp.zeros((8, 256), F32)], axis=1)
    r.n_all[own_rows, :] = jnp.concatenate([n2[0:192, :], half(jnp.concatenate(
        [n2[192:200, :].astype(F32), packed], axis=0))], axis=0)
    ga.begin()
    gb.far()

    pair = many(spot * 2 * BLOCK, 2 * BLOCK, 16)
    for g in gathers:
        g.from_core(spot)
    for j in range(2):
        g8 = r.n_all[many((spot * 2 + j) * BLOCK + 192, 16, 16), 0:256].astype(F32)[8:16, :]
        g8 = g8 + pltpu.roll(g8, 4, 0)
        g8 = jnp.where(c == 0, g8, pltpu.roll(g8, 6, 0))
        r.gcol[j * BLOCK:(j + 1) * BLOCK, :] = jnp.concatenate([g8, jnp.zeros((120, 256), F32)], axis=0).T[0:BLOCK, :]
    for copy in loads:
        copy.wait()
    r.running[...] = jnp.zeros_like(r.running)
    r.drows[...] = jnp.zeros_like(r.drows)
    r.dgate[...] = jnp.zeros_like(r.dgate)
    r.extra[...] = jnp.zeros_like(r.extra)
    pair_lane = iota((2 * BLOCK, 128), 1)
    for e in range(2):
        gate = r.gcol[:, e:e + 1]
        r.res[...] = jnp.zeros_like(r.res)
        d_result = gate * r.c_all[pair, :].astype(F32)
        r.dres[...] = half(d_result)
        r.extra[0, 2 + e:3 + e, 0:512] = column_sum(r.dres[...].astype(F32))

        def hidden_step(j, _, e=e):
            hs = many(j * STEP, STEP, STEP)
            n = r.n_all[pair, :]
            pre = dot(n, r.win[e, :, hs]) + r.bin[e:e + 1, hs].astype(F32)
            hid, slope = gelu_parts(pre)
            r.res[...] += dot(half(hid), r.wout[e, hs, :])
            d_pre = half(slope * dot_nt(r.dres[...], r.wout[e, hs, :]))
            r.extra[0, e:e + 1, hs] = column_sum(d_pre.astype(F32))
            r.drows[...] += dot_nt(d_pre, r.win[e, :, hs])
            return 0

        lax.fori_loop(0, 2, hidden_step, 0)
        if e == 0:
            ga.turn()
        lax.fori_loop(2, 4, hidden_step, 0)
        if e == 0:
            ga.far()
        result = r.res[...] + r.bout[e:e + 1, :].astype(F32)
        r.running[...] += gate * result
        d_gate = jnp.sum(r.c_all[pair, :].astype(F32) * result, axis=1, keepdims=True)
        r.dgate[...] = jnp.where(pair_lane == 2 * c + e, d_gate, r.dgate[...])

    theirs, ours = many((1 - c) * BLOCK, BLOCK, 8), many(c * BLOCK, BLOCK, 8)
    partials = [remote(src.at[theirs, :], dst, r.p_send.at[i], r.p_recv.at[i], partner) for i, (src, dst) in enumerate(
        ((r.running, r.got_running), (r.drows, r.got_drows), (r.dgate, r.got_dgate)))]
    for copy in partials:
        copy.start()

    for g in gathers:
        for other_spot in (g.first, g.second, g.diagonal):
            g.from_core(other_spot)
    span = 8 * BLOCK
    row = jnp.zeros((8, span), F32)
    for d in range(8):
        g8 = r.n_all[d * BLOCK + 192:(d + 1) * BLOCK, 0:256].astype(F32)[8:16, :]
        g8 = g8 + pltpu.roll(g8, 4, 0)
        g8 = jnp.where(c == 0, g8, pltpu.roll(g8, 6, 0))
        at, shift = d * BLOCK // 128 * 128, d * BLOCK % 128
        width = min(384, span - at)
        g8 = jnp.concatenate([g8, jnp.zeros((8, 128), F32)], axis=1)
        g8 = pltpu.roll(g8, shift, 1) if shift else g8
        pieces = [jnp.zeros((8, at), F32)] if at else []
        pieces += [g8[:, 0:width]] + ([jnp.zeros((8, span - at - width), F32)] if span > at + width else [])
        row = row + jnp.concatenate(pieces, axis=1)
    r.g_all[...] = row

    slot = lax.rem(x + y, 2)

    def where_from(f, slice_of, x_of):
        s, i, kind = f // 8, lax.rem(f, 8) // 2, lax.rem(f, 2)
        t = jnp.maximum(s - 2, 0)
        e = jnp.where(s < 2, s, t // 2)
        start = slice_of * 1024 + jnp.where(s < 2, 512 + x_of * SLICE, lax.rem(t, 2) * SLICE)
        return e, start, i, kind

    def landing(f, slice_of=slot, x_of=x):
        e, start, i, kind = where_from(f, slice_of, x_of)
        return r.grads.at[kind * 2 + e, many(start + i * PIECE, PIECE, PIECE), :]

    def up_copy(src, f):
        return remote(src, r.up_in.at[f], r.bulk.at[0], r.up_recv.at[f], up)

    def down_copy(src, f):
        return remote(src, r.down_in.at[f], r.bulk.at[1], r.down_recv.at[f], down)

    def keep_copy(f):
        return pltpu.make_async_copy(r.fin.at[f], landing(f), r.bulk.at[2])

    def give_x(f, recv, ref=None):
        return remote(r.fin.at[f], landing(f) if ref is None else ref, r.bulk.at[3], recv, xn)

    def give_y(f, recv, ref=None):
        return remote(r.fin.at[f], landing(f) if ref is None else ref, r.bulk.at[4], recv, yn)

    def pass_x(f):
        ref = landing(f, 1 - slot, x)
        return remote(ref, ref, r.bulk.at[5], r.bulk.at[7], xn)

    def pass_y(f):
        ref = landing(f, 1 - slot, 1 - x)
        return remote(ref, ref, r.bulk.at[6], r.bulk.at[8], yn)

    def goes(f):
        late = lax.rem(f // 8, 2)
        return (f < SETS) | (late == 0), (f < SETS) | (late == 1), lax.rem(f, 8) < 4

    def inside(f, count=PIECES):
        return (f >= 0) & (f < count)

    def tick(t):
        u, d, f, w = t - HOP * z, t - HOP * (zs - 1 - z), t - HOP * (zs - 1), t - HOP * (zs - 1) - PASS

        @pl.when(inside(u))
        def _():
            pl.when(z == 0)(lambda: up_copy(r.own.at[u], u).start())

            @pl.when(low_z)
            def _():
                up_copy(r.up_out.at[u], u).wait_recv()

                @pl.when(high_z)
                def _():
                    r.up_out[u] = half(r.own[u].astype(F32) + r.up_in[u].astype(F32))
                    up_copy(r.up_out.at[u], u).start()

        @pl.when(inside(d))
        def _():
            pl.when(z == zs - 1)(lambda: down_copy(r.own.at[d], d).start())

            @pl.when(high_z)
            def _():
                down_copy(r.down_out.at[d], d).wait_recv()

                @pl.when(low_z)
                def _():
                    r.down_out[d] = half(r.own[d].astype(F32) + r.down_in[d].astype(F32))
                    down_copy(r.down_out.at[d], d).start()

        @pl.when(inside(f))
        def _():
            lower = jnp.where(low_z, r.up_in[f].astype(F32), 0.0)
            upper = jnp.where(high_z, r.down_in[f].astype(F32), 0.0)
            r.fin[f] = half(r.own[f].astype(F32) + lower + upper)
            keep_copy(f).start()
            to_x, to_y, by_x = goes(f)
            single = f < SETS
            pl.when(to_x & single & jnp.logical_not(by_x))(lambda: give_x(f, r.x_recv.at[jnp.minimum(f, SETS - 1)]).start())
            pl.when(to_x & jnp.logical_not(single & jnp.logical_not(by_x)))(lambda: give_x(f, r.bulk.at[7]).start())
            pl.when(to_y & single & by_x)(lambda: give_y(f, r.y_recv.at[jnp.minimum(f, SETS - 1)]).start())
            pl.when(to_y & jnp.logical_not(single & by_x))(lambda: give_y(f, r.bulk.at[8]).start())

        @pl.when(inside(w, SETS))
        def _():
            _, _, by_x = goes(w)

            @pl.when(by_x)
            def _():
                give_y(w, r.y_recv.at[w], landing(w, 1 - slot, x)).wait_recv()
                pass_x(w).start()

            @pl.when(jnp.logical_not(by_x))
            def _():
                give_x(w, r.x_recv.at[w], landing(w, 1 - slot, 1 - x)).wait_recv()
                pass_y(w).start()

    def finish_pieces():
        both = PIECES - SETS
        some = SETS + both // 2
        got = both // 2 + SETS
        pl.when(high_z)(lambda: remote(r.own, r.up_in, r.bulk.at[0], r.bulk.at[0], up).wait_send())
        pl.when(low_z)(lambda: remote(r.own, r.down_in, r.bulk.at[1], r.bulk.at[1], down).wait_send())
        pltpu.make_async_copy(r.fin, r.own, r.bulk.at[2]).wait()
        for i, count in ((3, some), (4, some), (5, SETS // 2), (6, SETS // 2)):
            remote(r.fin.at[0:count], r.own.at[0:count], r.bulk.at[i], r.bulk.at[i], xn).wait_send()
        for i in (7, 8):
            remote(r.fin.at[0:got], r.own.at[0:got], r.bulk.at[i], r.bulk.at[i], xn).wait_recv()

    far_half = (1 - x, 1 - y)
    near_half = (x, y)
    quarter = (x * 2 + y, 4 + y * 2 + x)
    near, next_near = (xn, yn), (yn, xn)

    def cols(j, n):
        return many(j * 256, 256 * n, 256)

    def ar(i, src, dst, target):
        return remote(src, dst, r.ar_send.at[i], r.ar_recv.at[i], target)

    def ar_one(s):
        return ar(s, r.total.at[:, cols(4 * s + 2 * far_half[s], 2)], r.part_in.at[s], near[s])

    def ar_two(s):
        give = 4 * s + 2 * near_half[s] + (1 - near_half[1 - s])
        return ar(2 + s, r.total.at[:, cols(give, 1)], r.part_in.at[2 + s, :, 0:256], next_near[s])

    def ar_up(s):
        return ar(4 + s, r.z_out.at[s], r.z_in.at[s], up)

    def ar_down(s):
        return ar(6 + s, r.z_out.at[2 + s], r.z_in.at[2 + s], down)

    def ar_four(s):
        piece = r.final.at[:, cols(quarter[s], 1)]
        return ar(8 + s, piece, piece, next_near[s])

    def ar_four_got(s):
        piece = r.final.at[:, cols(4 * s + 2 * near_half[s] + (1 - near_half[1 - s]), 1)]
        return ar(8 + s, piece, piece, next_near[s])

    def ar_five(s):
        piece = r.final.at[:, cols(4 * s + 2 * near_half[s], 2)]
        return ar(10 + s, piece, piece, near[s])

    def ar_five_got(s):
        piece = r.final.at[:, cols(4 * s + 2 * far_half[s], 2)]
        return ar(10 + s, piece, piece, near[s])

    def add_into(ref, other_part):
        ref[...] = half(ref[...].astype(F32) + other_part.astype(F32))

    def ar_stage1():
        for s in range(2):
            ar_one(s).start()

    def ar_stage2():
        for s in range(2):
            ar_one(s).wait()
            add_into(r.total.at[:, cols(4 * s + 2 * near_half[s], 2)], r.part_in[s])
            ar_two(s).start()

    def ar_stage3():
        for s in range(2):
            ar_two(s).wait()
            add_into(r.total.at[:, cols(quarter[s], 1)], r.part_in[2 + s, :, 0:256])

            @pl.when(z == 0)
            def _():
                r.z_out[s] = r.total[:, cols(quarter[s], 1)]
                ar_up(s).start()

            @pl.when(z == zs - 1)
            def _():
                r.z_out[2 + s] = r.total[:, cols(quarter[s], 1)]
                ar_down(s).start()

    def ar_stage_z(k):
        for s in range(2):
            @pl.when(z == k)
            def _():
                ar_up(s).wait_recv()
                if k < zs - 1:
                    r.z_out[s] = half(r.total[:, cols(quarter[s], 1)].astype(F32) + r.z_in[s].astype(F32))
                    ar_up(s).start()

            @pl.when(z == zs - 1 - k)
            def _():
                ar_down(s).wait_recv()
                if k < zs - 1:
                    r.z_out[2 + s] = half(r.total[:, cols(quarter[s], 1)].astype(F32) + r.z_in[2 + s].astype(F32))
                    ar_down(s).start()

    def ar_stage4():
        for s in range(2):
            lower = jnp.where(low_z, r.z_in[s].astype(F32), 0.0)
            upper = jnp.where(high_z, r.z_in[2 + s].astype(F32), 0.0)
            own = r.total[:, cols(quarter[s], 1)].astype(F32)
            r.final[:, cols(quarter[s], 1)] = half(own + lower + upper)
            ar_four(s).start()

    def ar_stage5():
        for s in range(2):
            ar_four_got(s).wait_recv()
            ar_five(s).start()

    def ar_stage6():
        for s in range(2):
            ar_five_got(s).wait_recv()
            ar_four(s).wait_send()
            ar_five(s).wait_send()
            pl.when(high_z)(lambda s=s: ar_up(s).wait_send())
            pl.when(low_z)(lambda s=s: ar_down(s).wait_send())

    stages_at = {3: ar_stage2, 4: ar_stage3, 5: lambda: ar_stage_z(1)}

    def slice_step(s, _):
        e, start, _, _ = where_from(s * 8, slot, x)
        hs = many(start, SLICE, SLICE)
        wi = half(r.win[e, :, hs].astype(F32).T)
        wo = r.wout[e, hs, :]
        bias = jnp.broadcast_to(r.binf[pl.ds(e, 1), hs], (128, SLICE)).T[:, 0:1]
        n, co, g = r.n_all[...], r.c_all[...], r.g_all[pl.ds(e, 1), :]
        hid, slope = gelu_parts(dot_nt(wi, n) + bias)
        dh = dot_nt(wo, co)
        for kind, grad in ((0, dot(half(slope * (dh * g)), n)), (1, dot(half(hid * g), co))):
            for i in range(SLICE // PIECE):
                r.own[s * 8 + i * 2 + kind] = half(grad[i * PIECE:(i + 1) * PIECE, :])
        for at, todo in stages_at.items():
            pl.when(s == at)(todo)
        first = jnp.where(s < 2, s * TICKS, SETS + (s - 2) * TICKS)
        for k in range(TICKS):
            tick(first + k)
        return 0

    lax.fori_loop(0, 2, slice_step, 0)
    clock = iter(range(2 * TICKS, SETS))

    for copy in partials:
        copy.wait()

    r.out[...] = half(r.mid[0:BLOCK, :] + (r.running[ours, :] + r.got_running[...]))[0:tokens, :]
    zeros = jnp.zeros((ROWS - BLOCK, 128), F32)
    d_gates = jnp.concatenate([r.dgate[ours, :] + r.got_dgate[...], zeros], axis=0)
    rprobs, chosen = r.rprobs[...], r.chosen[...]
    d_probs = d_gates * chosen
    d_logits = half(rprobs * (d_probs - jnp.sum(rprobs * d_probs, axis=-1, keepdims=True)))
    r.dn[0:BLOCK, :] = r.drows[ours, :] + r.got_drows[...]
    r.dn[BLOCK:ROWS, :] = jnp.zeros((ROWS - BLOCK, 512), F32)
    tick(next(clock))
    dn = r.dn[...] + dot(d_logits, route_t)
    xhat = r.xhat2[...]
    n2 = half(xhat * gain2 + bias2)
    grad_route = dot(half(d_logits.astype(F32).T), n2)
    vector_rows = {5: column_sum(dn * xhat), 6: column_sum(dn)}
    r.xs[...] = jnp.zeros_like(r.xs)
    r.xs[0:tokens, :] = r.cot[...].astype(F32)
    d_middle = r.xs[...] + norm_back(dn, xhat, spread2, gain2)
    r.mid[...] = d_middle
    r.db[...] = half(d_middle)
    db = r.db[...]
    vector_rows[4] = column_sum(db.astype(F32))
    r.dense[:, 1536:2048] = half(dot(half(r.ctx[...].astype(F32).T), db))
    r.dctx[...] = half(dot_nt(db, r.wproj[...]))
    tick(next(clock))

    def heads_back(i, _):
        q, k, v = [r.mixed[:, many(base + 128 * i, 128, 128)] for base in (0, 512, 1024)]
        q = q * BF16(HEAD_DIM ** -0.5)
        do = r.dctx[:, many(128 * i, 128, 128)]
        parts = []
        for h in range(2):
            p = r.probs[2 * i + h]
            dp = dot_nt(jnp.where(low_lane == (h == 0), do, jnp.zeros_like(do)), v)
            ds = p * (dp - jnp.sum(p * dp, axis=-1, keepdims=True))
            parts.append((dot(half(ds), k) * HEAD_DIM ** -0.5, dot(half(ds.T), q), dot(half(p.T), do)))
        for j, base in enumerate((0, 512, 1024)):
            r.dmixed[:, many(base + 128 * i, 128, 128)] = half(jnp.where(low_lane, parts[0][j], parts[1][j]))
        return 0

    tick(next(clock))
    tick(next(clock))
    lax.fori_loop(0, 4, heads_back, 0)
    tick(next(clock))
    tick(next(clock))
    tick(next(clock))
    n1_t = half(r.n1[...].astype(F32).T)
    dn = 0.0
    for i in range(3):
        part = r.dmixed[:, 512 * i:512 * (i + 1)]
        if i != 1:
            vector_rows[2 + i // 2] = column_sum(part.astype(F32))
        r.dense[:, 512 * i:512 * (i + 1)] = half(dot(n1_t, part))
        dn = dn + dot_nt(part, r.wqkv[:, 512 * i:512 * (i + 1)])
        tick(next(clock))
    xhat = r.xhat1[...]
    vector_rows[0] = column_sum(dn * xhat)
    vector_rows[1] = column_sum(dn)
    r.igrad[...] = (r.mid[...] + norm_back(dn, xhat, spread1, gain1))[0:tokens, :]

    vectors = jnp.concatenate([grad_route[0:4, :]] + [vector_rows[i] for i in range(7)] + [jnp.zeros((5, 512), F32)], axis=0)
    r.dn[0:16, :] = vectors
    low_half, high_half = r.dn[0:16, 0:256], r.dn[0:16, 256:512]
    r.extra[1, :, 0:256] = jnp.where(c == 0, high_half, low_half)
    own_half = jnp.where(c == 0, low_half, high_half)
    swaps = [remote(r.dense.at[other, :], r.dense_in, r.d_send.at[0], r.d_recv.at[0], partner),
             remote(r.extra.at[1], r.extra.at[2], r.d_send.at[1], r.d_recv.at[1], partner)]
    for copy in swaps:
        copy.start()
    for copy in swaps:
        copy.wait()
    r.total[0:256, :] = half(r.dense[mine, :].astype(F32) + r.dense_in[...].astype(F32))
    sums = own_half + r.extra[2, :, 0:256]
    small = jnp.concatenate([r.extra[0, 0:4, :], jnp.zeros((12, 2048), F32)], axis=0)
    shifted = jnp.concatenate([jnp.zeros((4, 256), F32), sums[0:12, :]], axis=0)
    r.total[256:272, :] = half(small + jnp.concatenate([shifted, jnp.zeros((16, 1792), F32)], axis=1))

    ar_stage1()

    for t in clock:
        tick(t)
    lax.fori_loop(2, STEPS, slice_step, 0)
    start, ends = SETS + (STEPS - 2) * TICKS, PIECES + HOP * (zs - 1)
    stages = {2: lambda: ar_stage_z(2), 5: lambda: ar_stage_z(3), 8: ar_stage4, 13: ar_stage5}

    def last_ticks(t, _):
        for at, stage in stages.items():
            pl.when(t == start + at)(stage)
        tick(t)
        return 0

    lax.fori_loop(start, ends, last_ticks, 0)
    ar_stage6()
    finish_pieces()
    for g in gathers:
        g.drain()
    for i in range(4):
        count_copy(min(i, 1), i, 0, partner).wait_send()
    for k in range(1, zs):
        pl.when(z < k)(lambda k=k: count_copy(2, 3 + k, 0, partner).wait_send())


def block_call(zs, *args):
    tokens, width = args[0].shape
    vm, hbm = pl.BlockSpec(memory_space=pltpu.VMEM), pl.BlockSpec(memory_space=pl.ANY)
    shape = jax.ShapeDtypeStruct
    in_specs = [hbm if name in ("win_in", "wout_in") else vm for name in INPUTS]
    scratch = [pltpu.VMEM(dims, dtype) for _, dims, dtype in SCRATCH]
    scratch += [pltpu.SemaphoreType.DMA(dims) for _, dims in SEMS]
    return pl.pallas_call(
        functools.partial(block_kernel, zs),
        out_shape=(shape((tokens, width), BF16), shape((tokens, width), F32), shape((4, 2048, 512), BF16), shape((272, 2048), BF16)),
        in_specs=in_specs,
        out_specs=(vm, vm, hbm, vm),
        scratch_shapes=scratch,
        compiler_params=pltpu.CompilerParams(collective_id=0, has_side_effects=True, vmem_limit_bytes=63 << 20),
        name="encoder_block",
    )(*args)


def finish_kernel(grads_in, grads_out, summed, out_in, igrad_in, grad_in, grad_out, qkv, proj, route, bias_in, bias_out, out, igrad,
                  *vectors):
    grad_in[0] = grads_in[0].astype(F32).T
    grad_out[...] = grads_out[...].astype(F32)

    @pl.when(pl.program_id(0) == 0)
    def _():
        qkv[...] = summed[0:256, 0:1536].astype(F32)
        proj[...] = summed[0:256, 1536:2048].astype(F32)
        rows = summed[256:272, :].astype(F32)
        bias_in[...] = rows[0:2, :]
        bias_out[...] = rows[2:4, 0:512]
        route[...] = rows[4:8, 0:256]
        for i, ref in enumerate(vectors):
            ref[...] = rows[8 + i, 0:256]
        out[...] = out_in[...]
        igrad[...] = igrad_in[...]


def finish(grads, summed, out, igrad):
    shape = jax.ShapeDtypeStruct
    steps = 8

    def whole(ref):
        return pl.BlockSpec(ref.shape, lambda i: (0,) * len(ref.shape))

    got_in = pl.BlockSpec((1, 512, 512), lambda i: (i // 4, i % 4, 0))
    got_out = pl.BlockSpec((1, 512, 512), lambda i: (2 + i // 4, i % 4, 0))
    block_in = pl.BlockSpec((1, 512, 512), lambda i: (i // 4, 0, i % 4))
    block_out = pl.BlockSpec((1, 512, 512), lambda i: (i // 4, i % 4, 0))
    small = [shape((256, 1536), F32), shape((256, 512), F32), shape((4, 256), F32), shape((2, 2048), F32), shape((2, 512), F32),
             shape(out.shape, out.dtype), shape(igrad.shape, igrad.dtype)] + [shape((256,), F32)] * 7
    return pl.pallas_call(
        finish_kernel,
        grid=(steps,),
        out_shape=[shape((2, 512, 2048), F32), shape((2, 2048, 512), F32)] + small,
        in_specs=[got_in, got_out, whole(summed), whole(out), whole(igrad)],
        out_specs=[block_in, block_out] + [whole(v) for v in small],
        compiler_params=pltpu.CompilerParams(vmem_limit_bytes=60 << 20),
        name="finish",
    )(grads, grads, summed, out, igrad)


def swap(v):
    return lax.ppermute(v, "shard", [(0, 1), (1, 0)])


def fused(inputs, norm1_gain, norm1_bias, qkv_weight, query_bias, value_bias, out_weight, out_bias, norm2_gain, norm2_bias,
          router_weight, noise, expert_in, expert_in_bias, expert_out, expert_out_bias, routes, priority, cotangent):
    out, igrad, grads, summed = block_call(
        lax.axis_size("replica") // 4, inputs, cotangent, noise.T, routes.T, priority, norm1_gain, norm1_bias, query_bias,
        value_bias, out_bias, norm2_gain, norm2_bias, router_weight.T, qkv_weight, out_weight, expert_in, expert_out,
        expert_in_bias, expert_out_bias)
    grad_in, grad_out, qkv, proj, route, bias_in, bias_out, out, igrad, *cols = finish(grads, summed, out, igrad)
    return (out, igrad, cols[0], cols[1], qkv, cols[2], cols[3], proj, cols[4], cols[5], cols[6], route.T,
            grad_in, bias_in, grad_out, bias_out)


def layer_norm(values, gain_vector, bias_vector):
    centered = values - jnp.mean(values, axis=-1, keepdims=True)
    spread = lax.rsqrt(jnp.mean(centered * centered, axis=-1, keepdims=True) + LN_EPS)
    return centered * spread * gain_vector + bias_vector


def kept_gates(pair_expert, ranks, offsets, capacity, expert_count):
    same = pair_expert[:, None] == pair_expert[None, :]
    earlier = ranks[None, :] < ranks[:, None]
    before = jnp.sum(jnp.where(same & earlier, 1, 0).astype(jnp.int32), axis=1)
    onehot = pair_expert[:, None] == jnp.arange(expert_count, dtype=jnp.int32)[None, :]
    first_slot = jnp.sum(jnp.where(onehot, offsets[None, :], 0).astype(jnp.int32), axis=1)
    keep = before + first_slot < capacity
    picked = jnp.where(onehot & keep[:, None], 1.0, 0.0).astype(jnp.float32)
    return jnp.sum(picked.reshape(-1, 2, expert_count), axis=1)


def general(
    inputs, norm1_gain, norm1_bias, qkv_weight, query_bias, value_bias, out_weight, out_bias, norm2_gain, norm2_bias,
    router_weight, noise, expert_in, expert_in_bias, expert_out, expert_out_bias, routes, priority, cotangent,
):
    tok_count, width = inputs.shape
    replicas, cores = lax.axis_size("replica"), lax.axis_size("shard")
    shard = lax.axis_index("shard")
    images = tok_count // PATCHES
    heads = width // HEAD_DIM
    owned, _, hidden_count = expert_in.shape
    expert_count = owned * cores
    score_scale = HEAD_DIM ** (-0.5)
    f32 = jnp.float32

    vectors = (norm1_gain, norm1_bias, query_bias, value_bias, out_bias, norm2_gain, norm2_bias)
    packed = jnp.concatenate(
        [qkv_weight, out_weight, jnp.stack(vectors, axis=1), router_weight], axis=1)
    packed = lax.all_gather(packed, "shard", axis=0, tiled=True)
    weight_qkv = packed[:, :3 * width]
    weight_proj = packed[:, 3 * width:4 * width]
    small = packed[:, 4 * width:]
    gain_one, bias_one, bias_query, bias_value, bias_proj, gain_two, bias_two = [
        small[:, i].astype(f32) for i in range(len(vectors))]
    weight_route = small[:, len(vectors):]

    pair_expert = routes.reshape(-1)
    onehot_pairs = (pair_expert[:, None] == jnp.arange(expert_count, dtype=jnp.int32)[None, :]).astype(jnp.int32)
    load = jnp.sum(onehot_pairs, axis=0)
    loads = lax.all_gather(load, ("replica", "shard"))
    position = lax.axis_index("replica") * cores + shard
    ahead = jnp.arange(replicas * cores)[:, None] < position
    offsets = jnp.sum(jnp.where(ahead, loads, 0), axis=0)
    capacity = 2 * tok_count * replicas * cores // expert_count
    chosen = kept_gates(pair_expert, priority.reshape(-1), offsets, capacity, expert_count)

    residual_in = inputs.astype(f32)
    normed_one, norm_one_back = jax.vjp(layer_norm, residual_in, gain_one, bias_one)
    normed_one_half = half(normed_one)
    qkv_bias = jnp.concatenate([bias_query, jnp.zeros_like(bias_query), bias_value])
    mixed = half(dot(normed_one_half, weight_qkv) + qkv_bias)
    shaped = mixed.reshape(images, PATCHES, 3, heads, HEAD_DIM)
    query, keys, values = (shaped[:, :, 0], shaped[:, :, 1], shaped[:, :, 2])
    scores = jnp.einsum("bqhd,bkhd->bhqk", query, keys, preferred_element_type=f32) * score_scale
    row_max = jnp.max(scores, axis=-1, keepdims=True)
    log_total = row_max + jnp.log(jnp.sum(jnp.exp(scores - row_max), axis=-1, keepdims=True))
    context = jnp.einsum(
        "bhqk,bkhd->bqhd", half(jnp.exp(scores - log_total)), values, preferred_element_type=f32)
    context_half = half(context.reshape(tok_count, width))
    middle = residual_in + (dot(context_half, weight_proj) + bias_proj)
    normed_two, norm_two_back = jax.vjp(layer_norm, middle, gain_two, bias_two)
    normed_two_half = half(normed_two)
    logits = dot(normed_two_half, weight_route) + noise
    route_probs = jax.nn.softmax(logits, axis=-1)
    gate_weights = route_probs * chosen
    upstream = cotangent.astype(f32)

    pair_n = jnp.concatenate([normed_two_half, swap(normed_two_half)], axis=0)
    pair_c = jnp.concatenate([cotangent, swap(cotangent)], axis=0)
    own_gates = lax.dynamic_slice_in_dim(gate_weights, shard * owned, owned, 1)
    other_gates = swap(lax.dynamic_slice_in_dim(gate_weights, (1 - shard) * owned, owned, 1))
    pair_g = jnp.concatenate([own_gates, other_gates], axis=0)
    pair_up = pair_c.astype(f32)
    running = jnp.zeros((2 * tok_count, width), f32)
    d_rows = jnp.zeros((2 * tok_count, width), f32)
    gate_columns, bias_in_grads, bias_out_grads, in_grads, out_grads = [], [], [], [], []
    for e in range(owned):
        gate = pair_g[:, e:e + 1]
        pre = dot(pair_n, expert_in[e]) + expert_in_bias[e].astype(f32)
        act, slope = gelu_parts(pre)
        hid = half(act)
        result = dot(hid, expert_out[e]) + expert_out_bias[e].astype(f32)
        running = running + gate * result
        gate_columns.append(jnp.sum(pair_up * result, axis=1))
        d_result = half(gate * pair_up)
        d_pre = half(slope * dot_nt(d_result, expert_out[e]))
        d_rows = d_rows + dot_nt(d_pre, expert_in[e])
        bias_in_grads.append(jnp.sum(d_pre.astype(f32), axis=0))
        bias_out_grads.append(jnp.sum(d_result.astype(f32), axis=0))
        in_grads.append(jnp.einsum("td,th->dh", pair_n, d_pre, preferred_element_type=f32))
        out_grads.append(jnp.einsum("th,td->hd", hid, d_result, preferred_element_type=f32))
    d_gate_part = jnp.stack(gate_columns, axis=1)
    running = running[:tok_count] + swap(running[tok_count:])
    d_normed = d_rows[:tok_count] + swap(d_rows[tok_count:])
    d_gate_other = swap(d_gate_part[tok_count:])
    d_gate_own = d_gate_part[:tok_count]
    d_gates = jnp.where(shard == 0, jnp.concatenate([d_gate_own, d_gate_other], axis=1),
                        jnp.concatenate([d_gate_other, d_gate_own], axis=1))

    grad_in = lax.psum(half(jnp.stack(in_grads, axis=0)), "replica")
    grad_out = lax.psum(half(jnp.stack(out_grads, axis=0)), "replica")

    output = half(middle + running)
    d_probs = d_gates * chosen
    d_logits = half(route_probs * (d_probs - jnp.sum(route_probs * d_probs, axis=-1, keepdims=True)))
    grad_route = jnp.einsum("td,te->de", normed_two_half, d_logits, preferred_element_type=f32)
    d_normed = d_normed + dot_nt(d_logits, weight_route)
    d_middle, grad_gain_two, grad_bias_two = norm_two_back(d_normed)
    d_middle = d_middle + upstream
    d_branch = half(d_middle)
    grad_proj = jnp.einsum("tc,td->cd", context_half, d_branch, preferred_element_type=f32)
    grad_proj_bias = jnp.sum(d_branch.astype(f32), axis=0)
    d_context = half(dot_nt(d_branch, weight_proj)).reshape(images, PATCHES, heads, HEAD_DIM)
    attn_probs = jnp.exp(scores - log_total)
    d_attn = jnp.einsum("bqhd,bkhd->bhqk", d_context, values, preferred_element_type=f32)
    d_values = jnp.einsum("bhqk,bqhd->bkhd", half(attn_probs), d_context, preferred_element_type=f32)
    d_scores = half(attn_probs * (d_attn - jnp.sum(attn_probs * d_attn, axis=-1, keepdims=True)))
    d_query = jnp.einsum("bhqk,bkhd->bqhd", d_scores, keys, preferred_element_type=f32) * score_scale
    d_keys = jnp.einsum("bhqk,bqhd->bkhd", d_scores, query, preferred_element_type=f32) * score_scale
    d_mixed = half(jnp.stack([d_query, d_keys, d_values], axis=2).reshape(tok_count, 3 * width))
    grad_qkv = jnp.einsum("td,tf->df", normed_one_half, d_mixed, preferred_element_type=f32)
    mixed_sums = jnp.sum(d_mixed.astype(f32), axis=0)
    d_normed_one = dot_nt(d_mixed, weight_qkv)
    d_input, grad_gain_one, grad_bias_one = norm_one_back(d_normed_one)
    input_grad = d_input + d_middle

    columns = jnp.stack((grad_gain_one, grad_bias_one, mixed_sums[:width], mixed_sums[2 * width:], grad_proj_bias,
                         grad_gain_two, grad_bias_two), axis=1)
    dense = half(jnp.concatenate([grad_qkv, grad_proj, columns, grad_route], axis=1))
    mine = width // 2
    keep = lax.dynamic_slice_in_dim(dense, shard * mine, mine, 0)
    give = lax.dynamic_slice_in_dim(dense, (1 - shard) * mine, mine, 0)
    dense = keep.astype(f32) + swap(give).astype(f32)
    bias_row = jnp.concatenate(bias_in_grads + bias_out_grads)
    summed, bias_row = lax.psum((half(dense), bias_row), "replica")
    summed = summed.astype(f32)
    columns = [summed[:, 4 * width + i] for i in range(len(vectors))]
    grad_in_bias = bias_row[:owned * hidden_count].reshape(owned, hidden_count)
    grad_out_bias = bias_row[owned * hidden_count:].reshape(owned, width)
    return (
        output, input_grad, columns[0], columns[1], summed[:, :3 * width], columns[2], columns[3],
        summed[:, 3 * width:4 * width], columns[4], columns[5], columns[6], summed[:, 4 * width + len(vectors):],
        grad_in.astype(f32), grad_in_bias, grad_out.astype(f32), grad_out_bias,
    )


def on_device(*args):
    expert_in, inputs = args[12], args[0]
    planes = lax.axis_size("replica") == 16 and lax.axis_size("shard") == 2
    if planes and inputs.shape == (PATCHES, 512) and expert_in.shape == (2, 512, 2048):
        return fused(*args)
    return general(*args)


def solution(mesh):
    both, split = ("replica", "shard"), "shard"
    return jax.shard_map(
        on_device,
        mesh=mesh,
        in_specs=(
            P(both, None), P(split), P(split), P(split, None), P(split), P(split), P(split, None), P(split), P(split),
            P(split), P(split, None), P(both, None), P(split, None, None), P(split, None), P(split, None, None),
            P(split, None), P(both, None), P(both, None), P(both, None),
        ),
        out_specs=(
            P(both, None), P(both, None), P(split), P(split), P(split, None), P(split), P(split), P(split, None),
            P(split), P(split), P(split), P(split, None), P(split, None, None), P(split, None), P(split, None, None),
            P(split, None),
        ),
        check_vma=False,
    )
```

time: 216 us -> 162 us (0.75)
  local copies, waits for them, and re-layouts: 22.7 us -> 0 us
  Pallas kernels: 183 us -> 161 us
  other arithmetic: 9.05 us -> 0 us
    pallas_call x1, Pallas kernels: 183 us -> 149 us  [block_call(): pl.pallas_call(functools.partial(block_kernel, zs), out_shape=(shape((tok...]
    pallas_call x0 -> x1, Pallas kernels: none -> 12.5 us  [finish(): pl.pallas_call(finish_kernel, grid=(steps,), out_shape=[shape((2, 512, 20...]
    unnamed x20 -> x0, local copies, waits for them, and re-layouts: 11 us -> none
    convert_element_type x2 -> x0, other arithmetic: 9.05 us -> none  [the longest x1 4.6 us: fused(): gout.astype(F32)]
    slice x5 -> x0, local copies, waits for them, and re-layouts: 8.83 us -> none  [the longest x1 2.66 us: fused(): summed[0:256, 0:1536]]
where the time goes in v3:
time: 162 us
  Pallas kernels  161 us (99%)
    pallas_call x1, Pallas kernels, block_call(): pl.pallas_call(functools.partial(block_kernel, zs), out_shape=(shape((tok...  149 us
    pallas_call x1, Pallas kernels, finish(): pl.pallas_call(finish_kernel, grid=(steps,), out_shape=[shape((2, 512, 20...  12.5 us

profile of v3, /device:TPU:0, one launch (start us, length us, event | category | flops | bytes accessed | tf_op | source)
XLA Modules:
  0.0 162.0 jit_solution(3235870506782293979)
XLA Ops:
  0.7 148.7 %encoder_block.1 = (bf16[197,512]{1,0:T(8,128)(2,1)}, f32[197,512]{1,0:T(8,128)}, bf16[4,2048,512]{2,1,0:T(8,128)(2,1)}, bf16[272,2048]{1,0:T(8,128)(2,1)}) custom-call(bf16[197,512]{1,0:T(8,128)(2,1)} %refs_0_.1, bf16[197,512]{1,0:T(8,128)(2,1)} %refs_1_.1, f32[4,197]{1,0:T(4,128)} %bitcast.4, s32[2,197]{1,0:T(2,128)} %bitcast.5, s32[1,394]{1,0:T(1,128)} %refs_4_.1, ...), custom_call_target="tpu_custom_call" | custom-call | tf_op jit(solution)/shard_map/encoder_block/pallas_call | solution.py:759
  149.3 12.5 %finish.1 = (f32[2,512,2048]{2,1,0:T(8,128)}, f32[2,2048,512]{2,1,0:T(8,128)}, f32[256,1536]{1,0:T(8,128)}, f32[256,512]{1,0:T(8,128)}, f32[4,256]{1,0:T(4,128)}...) custom-call(bf16[4,2048,512]{2,1,0:T(8,128)(2,1)} %get-tuple-element, ...), custom_call_target="tpu_custom_call" | custom-call | tf_op jit(solution)/shard_map/finish/pallas_call | solution.py:802

commit v4 on v3

--- a/solution.py
+++ b/solution.py
@@ -21,13 +21,16 @@
 BLOCK = 208
 STEP = 512
 SLICE = 256
-PIECE = 64
+PIECE = 128
 STEPS = 6
-PIECES = STEPS * 2 * SLICE // PIECE
-SETS = 2 * 2 * SLICE // PIECE
+PER = 2 * SLICE // PIECE
+PIECES = STEPS * PER
+SETS = 2 * PER
 HOP = 3
-TICKS = 3
-PASS = 8
+TICKS, LATER = 1, 2
+EARLY = 3
+BEATS = (1, 1, 1, 1, 1, 0, 1, 1, 0, 1)
+PASS = 4
 
 
 def half(values):
@@ -82,8 +85,8 @@
 
 
 class PlaneGather:
-    def __init__(self, x_first, rows, sems):
-        self.rows = rows
+    def __init__(self, x_first, rows, at, sems):
+        self.rows, self.at = rows, at
         self.send, self.recv, self.core_send, self.core_recv = sems
         z, y, x, c = place()
         near = ((rep(z, y, 1 - x), c), (rep(z, 1 - y, x), c))
@@ -94,7 +97,8 @@
         self.core, self.partner = c, (rep(z, y, x), 1 - c)
 
     def ref(self, spot, core):
-        return self.rows.at[many((spot * 2 + core) * BLOCK, BLOCK, 16), :]
+        first, size = self.at
+        return self.rows.at[many((spot * 2 + core) * BLOCK + first, size, 16), :]
 
     def link(self, kind, spot):
         ref = self.ref(spot, self.core)
@@ -104,9 +108,10 @@
         ref = self.ref(spot, self.core if core is None else core)
         return remote(ref, ref, self.core_send.at[spot], self.core_recv.at[spot], self.partner)
 
-    def begin(self):
-        self.link(0, self.me).start()
-        self.link(1, self.me).start()
+    def begin(self, kind):
+        self.link(kind, self.me).start()
+
+    def hand(self):
         self.across(self.me).start()
 
     def turn(self):
@@ -127,6 +132,40 @@
             self.link(kind, spot).wait_send()
         for spot in range(4):
             self.across(spot).wait_send()
+
+
+class Halves:
+    def __init__(self, rows, sems):
+        cuts = ((0, 112), (112, BLOCK - 112))
+        self.parts = [PlaneGather(m == 0, rows, cuts[m], [ref.at[m] for ref in sems]) for m in range(2)]
+
+    def begin(self):
+        for part in self.parts:
+            part.begin(0)
+        for part in self.parts:
+            part.hand()
+        for part in self.parts:
+            part.begin(1)
+
+    def turn(self):
+        for part in self.parts:
+            part.turn()
+
+    def far(self):
+        for part in self.parts:
+            part.far()
+
+    def from_core(self, spot):
+        for part in self.parts:
+            part.from_core(spot)
+
+    def others(self):
+        part = self.parts[0]
+        return part.first, part.second, part.diagonal
+
+    def drain(self):
+        for part in self.parts:
+            part.drain()
 
 
 SCRATCH = (
@@ -148,7 +187,7 @@
     ("down_in", (PIECES, PIECE, 512), BF16), ("down_out", (PIECES, PIECE, 512), BF16), ("fin", (PIECES, PIECE, 512), BF16),
 )
 SEMS = (
-    ("g_send", (2, 2, 4)), ("g_recv", (2, 4)), ("g_csend", (2, 4)), ("g_crecv", (2, 4)),
+    ("g_send", (2, 2, 2, 4)), ("g_recv", (2, 2, 4)), ("g_csend", (2, 2, 4)), ("g_crecv", (2, 2, 4)),
     ("load", (2,)), ("w_send", (3,)), ("w_recv", (3,)), ("count_send", (7,)), ("count_recv", (9,)),
     ("p_send", (3,)), ("p_recv", (3,)), ("d_send", (2,)), ("d_recv", (2,)),
     ("ar_send", (12,)), ("ar_recv", (12,)), ("up_recv", (PIECES,)), ("down_recv", (PIECES,)), ("bulk", (9,)),
@@ -200,17 +239,6 @@
     r.vec[c] = jnp.concatenate(rows, axis=0)
     r.binf[...] = r.bin[...].astype(F32)
 
-    pl.semaphore_wait(bar, zs + 3)
-
-    weights = [remote(ref, ref, r.w_send.at[i], r.w_recv.at[i], partner) for i, ref in enumerate(
-        (r.vec.at[c], r.wqkv.at[mine, :], r.wproj.at[mine, :]))]
-    for copy in weights:
-        copy.start()
-    gathers = [PlaneGather(m == 0, (r.n_all, r.c_all)[m],
-                           (r.g_send.at[m], r.g_recv.at[m], r.g_csend.at[m], r.g_crecv.at[m])) for m in range(2)]
-    ga, gb = gathers
-    gb.begin()
-
     lane, row = iota((ROWS, 128), 1), iota((ROWS, 128), 0)
     r.pairs[0:8, :] = jnp.full((8, ROWS), -1.0, F32)
     r.pairs[8:16, :] = jnp.zeros((8, ROWS), F32)
@@ -222,23 +250,7 @@
     onehot = [jnp.where(lane.astype(F32) == experts[k], 1.0, 0.0) for k in range(2)]
     count = jnp.broadcast_to(column_sum(onehot[0] + onehot[1]), (8, 128))
 
-    def count_copy(stage, i, slot, target):
-        return remote(r.count_out.at[stage], r.count_in.at[slot], r.count_send.at[i], r.count_recv.at[slot], target)
-
-    spot = y * 2 + x
-    column = [(rep(k, y, x), c) for k in range(zs)]
-
-    def counts_to_plane():
-        for d in range(1, 4):
-            q = lax.rem(spot + d, 4)
-            count_copy(1, d, 1 + spot, (rep(z, q // 2, lax.rem(q, 2)), c)).start()
-
-    def counts_up():
-        for k in range(1, zs):
-            pl.when(z < k)(lambda k=k: count_copy(2, 3 + k, 5 + z, column[k]).start())
-
     r.count_out[0] = count
-    count_copy(0, 0, 0, partner).start()
 
     places = iota((ROWS, r.prio.shape[1]), 1) - 2 * iota((ROWS, r.prio.shape[1]), 0)
     ranks = r.prio[...].astype(F32)
@@ -254,6 +266,37 @@
             seen = seen + jnp.where((others < codes[k]) & (others >= floor), 1.0, 0.0)
         before.append(jnp.sum(seen, axis=1, keepdims=True))
 
+    def count_copy(stage, i, slot, target):
+        return remote(r.count_out.at[stage], r.count_in.at[slot], r.count_send.at[i], r.count_recv.at[slot], target)
+
+    spot = y * 2 + x
+    column = [(rep(k, y, x), c) for k in range(zs)]
+
+    def counts_to_plane():
+        for d in range(1, 4):
+            q = lax.rem(spot + d, 4)
+            count_copy(1, d, 1 + spot, (rep(z, q // 2, lax.rem(q, 2)), c)).start()
+
+    def counts_up():
+        for k in range(1, zs):
+            pl.when(z < k)(lambda k=k: count_copy(2, 3 + k, 5 + z, column[k]).start())
+
+    pl.semaphore_wait(bar, zs + 3)
+
+    weights = [remote(ref, ref, r.w_send.at[i], r.w_recv.at[i], partner) for i, ref in enumerate(
+        (r.vec.at[c], r.wqkv.at[mine, :], r.wproj.at[mine, :]))]
+    for copy in weights:
+        copy.start()
+    gathers = [Halves((r.n_all, r.c_all)[m], (r.g_send.at[m], r.g_recv.at[m], r.g_csend.at[m], r.g_crecv.at[m]))
+               for m in range(2)]
+    ga, gb = gathers
+    gb.begin()
+    count_copy(0, 0, 0, partner).start()
+
+    r.xs[0:tokens, :] = r.x[...].astype(F32)
+    xhat, spread1 = normalize(r.xs[...])
+    r.xhat1[...] = xhat
+
     count_copy(0, 0, 0, partner).wait_recv()
     ahead = jnp.where(c == 1, 1.0, 0.0) * r.count_in[0]
     count = count + r.count_in[0]
@@ -266,10 +309,15 @@
     gain1, bias1, bias_q, bias_v, bias_p, gain2, bias2 = [vec[i:i + 1, :] for i in range(7)]
     route_rows = jnp.concatenate([vec[8:16, :], jnp.zeros((120, 512), F32)], axis=0)
     route_t, route = half(route_rows), half(route_rows.T)
-    r.xs[0:tokens, :] = r.x[...].astype(F32)
-    xhat, spread1 = normalize(r.xs[...])
-    r.xhat1[...] = xhat
     r.n1[...] = half(xhat * gain1 + bias1)
+
+    for i, ref in ((1, r.wqkv), (2, r.wproj)):
+        weights[i].wait_send()
+        ref = ref.at[other, :]
+        remote(ref, ref, r.w_send.at[i], r.w_recv.at[i], partner).wait_recv()
+    for i, bias in enumerate((bias_q, None, bias_v)):
+        part = dot(r.n1[...], r.wqkv[:, 512 * i:512 * (i + 1)])
+        r.mixed[:, 512 * i:512 * (i + 1)] = half(part if bias is None else part + bias)
 
     for q in range(4):
         pl.when(spot != q)(lambda q=q: count_copy(1, 1, 1 + q, partner).wait_recv())
@@ -279,13 +327,7 @@
     r.count_out[2] = count
     counts_up()
 
-    for i, ref in ((1, r.wqkv), (2, r.wproj)):
-        weights[i].wait_send()
-        ref = ref.at[other, :]
-        remote(ref, ref, r.w_send.at[i], r.w_recv.at[i], partner).wait_recv()
-    for i, bias in enumerate((bias_q, None, bias_v)):
-        part = dot(r.n1[...], r.wqkv[:, 512 * i:512 * (i + 1)])
-        r.mixed[:, 512 * i:512 * (i + 1)] = half(part if bias is None else part + bias)
+    gb.turn()
 
     low_lane = lane < HEAD_DIM
     key_kept = iota((ROWS, ROWS), 1) < tokens
@@ -306,8 +348,7 @@
 
     lax.fori_loop(0, 4, heads_forward, 0)
 
-    gb.turn()
-
+    gb.far()
     for k in range(zs - 1):
         pl.when(z > k)(lambda k=k: count_copy(2, 4, 5 + k, partner).wait_recv())
     for k in range(zs - 1):
@@ -335,7 +376,6 @@
     r.n_all[own_rows, :] = jnp.concatenate([n2[0:192, :], half(jnp.concatenate(
         [n2[192:200, :].astype(F32), packed], axis=0))], axis=0)
     ga.begin()
-    gb.far()
 
     pair = many(spot * 2 * BLOCK, 2 * BLOCK, 16)
     for g in gathers:
@@ -352,14 +392,14 @@
     r.dgate[...] = jnp.zeros_like(r.dgate)
     r.extra[...] = jnp.zeros_like(r.extra)
     pair_lane = iota((2 * BLOCK, 128), 1)
-    for e in range(2):
+    def expert_pass(e, between):
         gate = r.gcol[:, e:e + 1]
         r.res[...] = jnp.zeros_like(r.res)
         d_result = gate * r.c_all[pair, :].astype(F32)
         r.dres[...] = half(d_result)
         r.extra[0, 2 + e:3 + e, 0:512] = column_sum(r.dres[...].astype(F32))
 
-        def hidden_step(j, _, e=e):
+        def hidden_step(j, _):
             hs = many(j * STEP, STEP, STEP)
             n = r.n_all[pair, :]
             pre = dot(n, r.win[e, :, hs]) + r.bin[e:e + 1, hs].astype(F32)
@@ -371,24 +411,19 @@
             return 0
 
         lax.fori_loop(0, 2, hidden_step, 0)
-        if e == 0:
-            ga.turn()
+        between()
         lax.fori_loop(2, 4, hidden_step, 0)
-        if e == 0:
-            ga.far()
         result = r.res[...] + r.bout[e:e + 1, :].astype(F32)
         r.running[...] += gate * result
         d_gate = jnp.sum(r.c_all[pair, :].astype(F32) * result, axis=1, keepdims=True)
         r.dgate[...] = jnp.where(pair_lane == 2 * c + e, d_gate, r.dgate[...])
 
-    theirs, ours = many((1 - c) * BLOCK, BLOCK, 8), many(c * BLOCK, BLOCK, 8)
-    partials = [remote(src.at[theirs, :], dst, r.p_send.at[i], r.p_recv.at[i], partner) for i, (src, dst) in enumerate(
-        ((r.running, r.got_running), (r.drows, r.got_drows), (r.dgate, r.got_dgate)))]
-    for copy in partials:
-        copy.start()
+    expert_pass(0, lambda: None)
+    ga.turn()
+    ga.far()
 
     for g in gathers:
-        for other_spot in (g.first, g.second, g.diagonal):
+        for other_spot in g.others():
             g.from_core(other_spot)
     span = 8 * BLOCK
     row = jnp.zeros((8, span), F32)
@@ -408,7 +443,7 @@
     slot = lax.rem(x + y, 2)
 
     def where_from(f, slice_of, x_of):
-        s, i, kind = f // 8, lax.rem(f, 8) // 2, lax.rem(f, 2)
+        s, i, kind = f // PER, lax.rem(f, PER) // 2, lax.rem(f, 2)
         t = jnp.maximum(s - 2, 0)
         e = jnp.where(s < 2, s, t // 2)
         start = slice_of * 1024 + jnp.where(s < 2, 512 + x_of * SLICE, lax.rem(t, 2) * SLICE)
@@ -442,8 +477,8 @@
         return remote(ref, ref, r.bulk.at[6], r.bulk.at[8], yn)
 
     def goes(f):
-        late = lax.rem(f // 8, 2)
-        return (f < SETS) | (late == 0), (f < SETS) | (late == 1), lax.rem(f, 8) < 4
+        late = lax.rem(f // PER, 2)
+        return (f < SETS) | (late == 0), (f < SETS) | (late == 1), lax.rem(f, PER) < PER // 2
 
     def inside(f, count=PIECES):
         return (f >= 0) & (f < count)
@@ -621,10 +656,10 @@
             pl.when(high_z)(lambda s=s: ar_up(s).wait_send())
             pl.when(low_z)(lambda s=s: ar_down(s).wait_send())
 
-    stages_at = {3: ar_stage2, 4: ar_stage3, 5: lambda: ar_stage_z(1)}
+    stages_at = {4: ar_stage2, 5: ar_stage3}
 
     def slice_step(s, _):
-        e, start, _, _ = where_from(s * 8, slot, x)
+        e, start, _, _ = where_from(s * PER, slot, x)
         hs = many(start, SLICE, SLICE)
         wi = half(r.win[e, :, hs].astype(F32).T)
         wo = r.wout[e, hs, :]
@@ -634,17 +669,34 @@
         dh = dot_nt(wo, co)
         for kind, grad in ((0, dot(half(slope * (dh * g)), n)), (1, dot(half(hid * g), co))):
             for i in range(SLICE // PIECE):
-                r.own[s * 8 + i * 2 + kind] = half(grad[i * PIECE:(i + 1) * PIECE, :])
+                r.own[s * PER + i * 2 + kind] = half(grad[i * PIECE:(i + 1) * PIECE, :])
         for at, todo in stages_at.items():
             pl.when(s == at)(todo)
-        first = jnp.where(s < 2, s * TICKS, SETS + (s - 2) * TICKS)
         for k in range(TICKS):
-            tick(first + k)
+            pl.when(s < EARLY)(lambda k=k: tick(s * TICKS + k))
+        for k in range(LATER):
+            pl.when(s >= EARLY)(lambda k=k: tick(middle + (s - EARLY) * LATER + k))
         return 0
 
-    lax.fori_loop(0, 2, slice_step, 0)
-    clock = iter(range(2 * TICKS, SETS))
-
+    middle = EARLY * TICKS + sum(BEATS)
+    assert middle <= EARLY * PER
+
+    lax.fori_loop(0, EARLY, slice_step, 0)
+    clock, beats = iter(range(EARLY * TICKS, middle)), iter(BEATS)
+
+    def beat():
+        for _ in range(next(beats)):
+            tick(next(clock))
+
+
+    expert_pass(1, beat)
+    beat()
+    theirs, ours = many((1 - c) * BLOCK, BLOCK, 8), many(c * BLOCK, BLOCK, 8)
+    partials = [remote(src.at[theirs, :], dst, r.p_send.at[i], r.p_recv.at[i], partner) for i, (src, dst) in enumerate(
+        ((r.running, r.got_running), (r.drows, r.got_drows), (r.dgate, r.got_dgate)))]
+    for copy in partials:
+        copy.start()
+    beat()
     for copy in partials:
         copy.wait()
 
@@ -656,7 +708,7 @@
     d_logits = half(rprobs * (d_probs - jnp.sum(rprobs * d_probs, axis=-1, keepdims=True)))
     r.dn[0:BLOCK, :] = r.drows[ours, :] + r.got_drows[...]
     r.dn[BLOCK:ROWS, :] = jnp.zeros((ROWS - BLOCK, 512), F32)
-    tick(next(clock))
+    beat()
     dn = r.dn[...] + dot(d_logits, route_t)
     xhat = r.xhat2[...]
     n2 = half(xhat * gain2 + bias2)
@@ -671,7 +723,7 @@
     vector_rows[4] = column_sum(db.astype(F32))
     r.dense[:, 1536:2048] = half(dot(half(r.ctx[...].astype(F32).T), db))
     r.dctx[...] = half(dot_nt(db, r.wproj[...]))
-    tick(next(clock))
+    beat()
 
     def heads_back(i, _):
         q, k, v = [r.mixed[:, many(base + 128 * i, 128, 128)] for base in (0, 512, 1024)]
@@ -687,12 +739,9 @@
             r.dmixed[:, many(base + 128 * i, 128, 128)] = half(jnp.where(low_lane, parts[0][j], parts[1][j]))
         return 0
 
-    tick(next(clock))
-    tick(next(clock))
+    beat()
     lax.fori_loop(0, 4, heads_back, 0)
-    tick(next(clock))
-    tick(next(clock))
-    tick(next(clock))
+    beat()
     n1_t = half(r.n1[...].astype(F32).T)
     dn = 0.0
     for i in range(3):
@@ -701,7 +750,7 @@
             vector_rows[2 + i // 2] = column_sum(part.astype(F32))
         r.dense[:, 512 * i:512 * (i + 1)] = half(dot(n1_t, part))
         dn = dn + dot_nt(part, r.wqkv[:, 512 * i:512 * (i + 1)])
-        tick(next(clock))
+        beat()
     xhat = r.xhat1[...]
     vector_rows[0] = column_sum(dn * xhat)
     vector_rows[1] = column_sum(dn)
@@ -726,11 +775,9 @@
 
     ar_stage1()
 
-    for t in clock:
-        tick(t)
-    lax.fori_loop(2, STEPS, slice_step, 0)
-    start, ends = SETS + (STEPS - 2) * TICKS, PIECES + HOP * (zs - 1)
-    stages = {2: lambda: ar_stage_z(2), 5: lambda: ar_stage_z(3), 8: ar_stage4, 13: ar_stage5}
+    lax.fori_loop(EARLY, STEPS, slice_step, 0)
+    start, ends = middle + (STEPS - EARLY) * LATER, PIECES + HOP * (zs - 1)
+    stages = {0: lambda: ar_stage_z(1), 3: lambda: ar_stage_z(2), 6: lambda: ar_stage_z(3), 8: ar_stage4, 11: ar_stage5}
 
     def last_ticks(t, _):
         for at, stage in stages.items():
@@ -767,47 +814,74 @@
     )(*args)
 
 
-def finish_kernel(grads_in, grads_out, summed, out_in, igrad_in, grad_in, grad_out, qkv, proj, route, bias_in, bias_out, out, igrad,
-                  *vectors):
-    grad_in[0] = grads_in[0].astype(F32).T
-    grad_out[...] = grads_out[...].astype(F32)
-
-    @pl.when(pl.program_id(0) == 0)
-    def _():
-        qkv[...] = summed[0:256, 0:1536].astype(F32)
-        proj[...] = summed[0:256, 1536:2048].astype(F32)
-        rows = summed[256:272, :].astype(F32)
-        bias_in[...] = rows[0:2, :]
-        bias_out[...] = rows[2:4, 0:512]
-        route[...] = rows[4:8, 0:256]
-        for i, ref in enumerate(vectors):
-            ref[...] = rows[8 + i, 0:256]
-        out[...] = out_in[...]
-        igrad[...] = igrad_in[...]
+def finish_kernel(grads, summed, out_in, igrad_in, grad_in, grad_out, qkv, proj, route, bias_in, bias_out, out, igrad, *rest):
+    vectors, (got, done_in, done_out, got_sem, done_sem) = rest[:7], rest[7:]
+    n = done_in.shape[0]
+
+    def source(k, i):
+        return pltpu.make_async_copy(
+            grads.at[2 * k + i // 4, many(lax.rem(i, 4) * STEP, STEP, STEP), :], got.at[k * n + i], got_sem.at[k * n + i])
+
+    def results(i):
+        where = many(lax.rem(i, 4) * STEP, STEP, STEP)
+        return (pltpu.make_async_copy(done_in.at[i], grad_in.at[i // 4, :, where], done_sem.at[i]),
+                pltpu.make_async_copy(done_out.at[i], grad_out.at[i // 4, where, :], done_sem.at[n + i]))
+
+    def fetch(i, _):
+        source(1, i).start()
+        source(0, i).start()
+        return 0
+
+    lax.fori_loop(0, n, fetch, 0)
+    qkv[...] = summed[0:256, 0:1536].astype(F32)
+    proj[...] = summed[0:256, 1536:2048].astype(F32)
+    rows = summed[256:272, :].astype(F32)
+    bias_in[...] = rows[0:2, :]
+    bias_out[...] = rows[2:4, 0:512]
+    route[...] = rows[4:8, 0:256]
+    for i, ref in enumerate(vectors):
+        ref[...] = rows[8 + i, 0:256]
+    out[...] = out_in[...]
+    igrad[...] = igrad_in[...]
+
+    def convert(i, _):
+        to_in, to_out = results(i)
+        source(1, i).wait()
+        done_out[i] = got[n + i].astype(F32)
+        to_out.start()
+        source(0, i).wait()
+        done_in[i] = got[i].astype(F32).T
+        to_in.start()
+        return 0
+
+    lax.fori_loop(0, n, convert, 0)
+
+    def settle(i, _):
+        for copy in results(i):
+            copy.wait()
+        return 0
+
+    lax.fori_loop(0, n, settle, 0)
 
 
 def finish(grads, summed, out, igrad):
     shape = jax.ShapeDtypeStruct
-    steps = 8
-
-    def whole(ref):
-        return pl.BlockSpec(ref.shape, lambda i: (0,) * len(ref.shape))
-
-    got_in = pl.BlockSpec((1, 512, 512), lambda i: (i // 4, i % 4, 0))
-    got_out = pl.BlockSpec((1, 512, 512), lambda i: (2 + i // 4, i % 4, 0))
-    block_in = pl.BlockSpec((1, 512, 512), lambda i: (i // 4, 0, i % 4))
-    block_out = pl.BlockSpec((1, 512, 512), lambda i: (i // 4, i % 4, 0))
+    vm, hbm = pl.BlockSpec(memory_space=pltpu.VMEM), pl.BlockSpec(memory_space=pl.ANY)
     small = [shape((256, 1536), F32), shape((256, 512), F32), shape((4, 256), F32), shape((2, 2048), F32), shape((2, 512), F32),
              shape(out.shape, out.dtype), shape(igrad.shape, igrad.dtype)] + [shape((256,), F32)] * 7
+    n = 8
     return pl.pallas_call(
         finish_kernel,
-        grid=(steps,),
         out_shape=[shape((2, 512, 2048), F32), shape((2, 2048, 512), F32)] + small,
-        in_specs=[got_in, got_out, whole(summed), whole(out), whole(igrad)],
-        out_specs=[block_in, block_out] + [whole(v) for v in small],
+        in_specs=[hbm, vm, vm, vm],
+        out_specs=[hbm, hbm] + [vm] * len(small),
+        scratch_shapes=[
+            pltpu.VMEM((2 * n, STEP, 512), BF16), pltpu.VMEM((n, 512, STEP), F32), pltpu.VMEM((n, STEP, 512), F32),
+            pltpu.SemaphoreType.DMA((2 * n,)), pltpu.SemaphoreType.DMA((2 * n,)),
+        ],
         compiler_params=pltpu.CompilerParams(vmem_limit_bytes=60 << 20),
         name="finish",
-    )(grads, grads, summed, out, igrad)
+    )(grads, summed, out, igrad)
 
 
 def swap(v):

time: 162 us -> 149 us (0.920)
  Pallas kernels: 161 us -> 148 us
    pallas_call x1, Pallas kernels: 149 us -> 136 us  [block_call(): pl.pallas_call(functools.partial(block_kernel, zs), out_shape=(shape((tok...]
where the time goes in v4:
time: 149 us; the launch traced here: 148 us
  Pallas kernels  148 us (99%)
    pallas_call x1, Pallas kernels, block_call(): pl.pallas_call(functools.partial(block_kernel, zs), out_shape=(shape((tok...  136 us
    pallas_call x1, Pallas kernels, finish(): pl.pallas_call(finish_kernel, out_shape=[shape((2, 512, 2048), F32), shap...  11.2 us

profile of v4, /device:TPU:0, one launch (start us, length us, event | category | flops | bytes accessed | tf_op | source)
XLA Modules:
  0.0 148.4 jit_solution(9143658354614700164)
XLA Ops:
  0.7 136.3 %encoder_block.1 = (bf16[197,512]{1,0:T(8,128)(2,1)}, f32[197,512]{1,0:T(8,128)}, bf16[4,2048,512]{2,1,0:T(8,128)(2,1)}, bf16[272,2048]{1,0:T(8,128)(2,1)}) custom-call(bf16[197,512]{1,0:T(8,128)(2,1)} %refs_0_.1, bf16[197,512]{1,0:T(8,128)(2,1)} %refs_1_.1, f32[4,197]{1,0:T(4,128)} %bitcast.4, s32[2,197]{1,0:T(2,128)} %bitcast.5, s32[1,394]{1,0:T(1,128)} %refs_4_.1, ...), custom_call_target="tpu_custom_call" | custom-call | tf_op jit(solution)/shard_map/encoder_block/pallas_call | solution.py:806
  137.0 11.2 %finish.1 = (f32[2,512,2048]{2,1,0:T(8,128)}, f32[2,2048,512]{2,1,0:T(8,128)}, f32[256,1536]{1,0:T(8,128)}, f32[256,512]{1,0:T(8,128)}, f32[4,256]{1,0:T(4,128)}...) custom-call(bf16[4,2048,512]{2,1,0:T(8,128)(2,1)} %get-tuple-element, ...), custom_call_target="tpu_custom_call" | custom-call | tf_op jit(solution)/shard_map/finish/pallas_call | solution.py:873

commit v5 on v4

--- a/solution.py
+++ b/solution.py
@@ -18,6 +18,7 @@
 F32 = jnp.float32
 BF16 = jnp.bfloat16
 ROWS = 256
+LATE = 192
 BLOCK = 208
 STEP = 512
 SLICE = 256
@@ -136,19 +137,19 @@
 
 class Halves:
     def __init__(self, rows, sems):
-        cuts = ((0, 112), (112, BLOCK - 112))
-        self.parts = [PlaneGather(m == 0, rows, cuts[m], [ref.at[m] for ref in sems]) for m in range(2)]
-
-    def begin(self):
-        for part in self.parts:
+        cuts = ((0, 96), (96, LATE - 96), (LATE, BLOCK - LATE))
+        self.parts = [PlaneGather(m == 0, rows, cuts[m], [ref.at[m] for ref in sems]) for m in range(3)]
+
+    def begin(self, parts=slice(0, 3)):
+        for part in self.parts[parts]:
             part.begin(0)
-        for part in self.parts:
+        for part in self.parts[parts]:
             part.hand()
-        for part in self.parts:
+        for part in self.parts[parts]:
             part.begin(1)
 
-    def turn(self):
-        for part in self.parts:
+    def turn(self, parts=slice(0, 3)):
+        for part in self.parts[parts]:
             part.turn()
 
     def far(self):
@@ -187,8 +188,8 @@
     ("down_in", (PIECES, PIECE, 512), BF16), ("down_out", (PIECES, PIECE, 512), BF16), ("fin", (PIECES, PIECE, 512), BF16),
 )
 SEMS = (
-    ("g_send", (2, 2, 2, 4)), ("g_recv", (2, 2, 4)), ("g_csend", (2, 2, 4)), ("g_crecv", (2, 2, 4)),
-    ("load", (2,)), ("w_send", (3,)), ("w_recv", (3,)), ("count_send", (7,)), ("count_recv", (9,)),
+    ("g_send", (2, 3, 2, 4)), ("g_recv", (2, 3, 4)), ("g_csend", (2, 3, 4)), ("g_crecv", (2, 3, 4)),
+    ("load", (4,)), ("w_send", (3,)), ("w_recv", (3,)), ("count_send", (7,)), ("count_recv", (9,)),
     ("p_send", (3,)), ("p_recv", (3,)), ("d_send", (2,)), ("d_recv", (2,)),
     ("ar_send", (12,)), ("ar_recv", (12,)), ("up_recv", (PIECES,)), ("down_recv", (PIECES,)), ("bulk", (9,)),
     ("x_recv", (SETS,)), ("y_recv", (SETS,)),
@@ -223,17 +224,17 @@
     for peer in (xn, yn, (rep(z, 1 - y, 1 - x), c), partner):
         pl.semaphore_signal(bar, inc=1, device_id=peer, device_id_type=MESH)
 
+    mine, other = many(c * 256, 256, 16), many((1 - c) * 256, 256, 16)
+    halves = [pltpu.make_async_copy(r.wqkv_in, r.wqkv.at[mine, :], r.load.at[2]),
+              pltpu.make_async_copy(r.wproj_in, r.wproj.at[mine, :], r.load.at[3])]
     loads = [pltpu.make_async_copy(r.win_in, r.win, r.load.at[0]), pltpu.make_async_copy(r.wout_in, r.wout, r.load.at[1])]
-    for copy in loads:
+    for copy in halves + loads:
         copy.start()
 
     r.xs[...] = jnp.zeros_like(r.xs)
     r.xs[0:tokens, :] = r.cot[...].astype(F32)
     own_rows = many(((y * 2 + x) * 2 + c) * BLOCK, BLOCK, 16)
     r.c_all[own_rows, :] = half(r.xs[0:BLOCK, :])
-    mine, other = many(c * 256, 256, 16), many((1 - c) * 256, 256, 16)
-    r.wqkv[mine, :] = r.wqkv_in[...]
-    r.wproj[mine, :] = r.wproj_in[...]
     rows = [ref[...].astype(F32).reshape(1, 256) for ref in (r.v0, r.v1, r.v2, r.v3, r.v4, r.v5, r.v6)]
     rows += [jnp.zeros((1, 256), F32), r.route_in[...].astype(F32), jnp.zeros((4, 256), F32)]
     r.vec[c] = jnp.concatenate(rows, axis=0)
@@ -281,6 +282,8 @@
         for k in range(1, zs):
             pl.when(z < k)(lambda k=k: count_copy(2, 3 + k, 5 + z, column[k]).start())
 
+    for copy in halves:
+        copy.wait()
     pl.semaphore_wait(bar, zs + 3)
 
     weights = [remote(ref, ref, r.w_send.at[i], r.w_recv.at[i], partner) for i, ref in enumerate(
@@ -349,6 +352,14 @@
     lax.fori_loop(0, 4, heads_forward, 0)
 
     gb.far()
+    middle = r.xs[...] + (dot(r.ctx[...], r.wproj[...]) + bias_p)
+    r.mid[...] = middle
+    xhat, spread2 = normalize(middle)
+    r.xhat2[...] = xhat
+    n2 = half(xhat * gain2 + bias2)
+    own_first = ((y * 2 + x) * 2 + c) * BLOCK
+    r.n_all[many(own_first, LATE, 16), :] = n2[0:LATE, :]
+    ga.begin(slice(0, 2))
     for k in range(zs - 1):
         pl.when(z > k)(lambda k=k: count_copy(2, 4, 5 + k, partner).wait_recv())
     for k in range(zs - 1):
@@ -359,12 +370,6 @@
         slot = before[k] + jnp.sum(onehot[k] * offsets, axis=1, keepdims=True)
         chosen = chosen + onehot[k] * jnp.where(slot < float(capacity), 1.0, 0.0)
     r.chosen[...] = chosen
-
-    middle = r.xs[...] + (dot(r.ctx[...], r.wproj[...]) + bias_p)
-    r.mid[...] = middle
-    xhat, spread2 = normalize(middle)
-    r.xhat2[...] = xhat
-    n2 = half(xhat * gain2 + bias2)
     logits = jnp.where(lane < 4, dot(n2, route) + noise, -1e30)
     e = jnp.exp(logits - jnp.max(logits, axis=-1, keepdims=True))
     rprobs = e / jnp.sum(e, axis=-1, keepdims=True)
@@ -373,9 +378,9 @@
     gates_high = half(gates).astype(F32)
     packed = jnp.where(lane < 4, gates_high, pltpu.roll(gates - gates_high, 4, 1)).T
     packed = jnp.concatenate([packed[0:8, :], jnp.zeros((8, 256), F32)], axis=1)
-    r.n_all[own_rows, :] = jnp.concatenate([n2[0:192, :], half(jnp.concatenate(
-        [n2[192:200, :].astype(F32), packed], axis=0))], axis=0)
-    ga.begin()
+    r.n_all[many(own_first + LATE, BLOCK - LATE, 16), :] = half(jnp.concatenate(
+        [n2[LATE:LATE + 8, :].astype(F32), packed], axis=0))
+    ga.begin(slice(2, 3))
 
     pair = many(spot * 2 * BLOCK, 2 * BLOCK, 16)
     for g in gathers:
@@ -418,8 +423,7 @@
         d_gate = jnp.sum(r.c_all[pair, :].astype(F32) * result, axis=1, keepdims=True)
         r.dgate[...] = jnp.where(pair_lane == 2 * c + e, d_gate, r.dgate[...])
 
-    expert_pass(0, lambda: None)
-    ga.turn()
+    expert_pass(0, ga.turn)
     ga.far()
 
     for g in gathers:
@@ -800,7 +804,7 @@
     tokens, width = args[0].shape
     vm, hbm = pl.BlockSpec(memory_space=pltpu.VMEM), pl.BlockSpec(memory_space=pl.ANY)
     shape = jax.ShapeDtypeStruct
-    in_specs = [hbm if name in ("win_in", "wout_in") else vm for name in INPUTS]
+    in_specs = [hbm if name in ("win_in", "wout_in", "wqkv_in", "wproj_in") else vm for name in INPUTS]
     scratch = [pltpu.VMEM(dims, dtype) for _, dims, dtype in SCRATCH]
     scratch += [pltpu.SemaphoreType.DMA(dims) for _, dims in SEMS]
     return pl.pallas_call(
@@ -814,8 +818,8 @@
     )(*args)
 
 
-def finish_kernel(grads, summed, out_in, igrad_in, grad_in, grad_out, qkv, proj, route, bias_in, bias_out, out, igrad, *rest):
-    vectors, (got, done_in, done_out, got_sem, done_sem) = rest[:7], rest[7:]
+def finish_kernel(grads, summed, out_in, igrad_in, grad_in, grad_out, qkv, proj, igrad, out, route, bias_in, bias_out, *rest):
+    vectors, (got, done_in, done_out, sums, wide, narrow, igrad_now, got_sem, done_sem, sem) = rest[:7], rest[7:]
     n = done_in.shape[0]
 
     def source(k, i):
@@ -832,17 +836,13 @@
         source(0, i).start()
         return 0
 
-    lax.fori_loop(0, n, fetch, 0)
-    qkv[...] = summed[0:256, 0:1536].astype(F32)
-    proj[...] = summed[0:256, 1536:2048].astype(F32)
-    rows = summed[256:272, :].astype(F32)
-    bias_in[...] = rows[0:2, :]
-    bias_out[...] = rows[2:4, 0:512]
-    route[...] = rows[4:8, 0:256]
-    for i, ref in enumerate(vectors):
-        ref[...] = rows[8 + i, 0:256]
-    out[...] = out_in[...]
-    igrad[...] = igrad_in[...]
+    arrivals = [pltpu.make_async_copy(summed, sums, sem.at[0]), pltpu.make_async_copy(igrad_in, igrad_now, sem.at[1])]
+    others = [pltpu.make_async_copy(wide, qkv, sem.at[2]), pltpu.make_async_copy(narrow, proj, sem.at[3]),
+              pltpu.make_async_copy(igrad_now, igrad, sem.at[4])]
+    lax.fori_loop(0, 2, fetch, 0)
+    for copy in arrivals:
+        copy.start()
+    lax.fori_loop(2, n, fetch, 0)
 
     def convert(i, _):
         to_in, to_out = results(i)
@@ -854,7 +854,21 @@
         to_in.start()
         return 0
 
-    lax.fori_loop(0, n, convert, 0)
+    lax.fori_loop(0, n - 2, convert, 0)
+    for copy in arrivals:
+        copy.wait()
+    wide[...] = sums[0:256, 0:1536].astype(F32)
+    narrow[...] = sums[0:256, 1536:2048].astype(F32)
+    for copy in others:
+        copy.start()
+    lax.fori_loop(n - 2, n, convert, 0)
+    out[...] = out_in[...]
+    rows = sums[256:272, :].astype(F32)
+    bias_in[...] = rows[0:2, :]
+    bias_out[...] = rows[2:4, 0:512]
+    route[...] = rows[4:8, 0:256]
+    for i, ref in enumerate(vectors):
+        ref[...] = rows[8 + i, 0:256]
 
     def settle(i, _):
         for copy in results(i):
@@ -862,22 +876,27 @@
         return 0
 
     lax.fori_loop(0, n, settle, 0)
+    for copy in others:
+        copy.wait()
 
 
 def finish(grads, summed, out, igrad):
     shape = jax.ShapeDtypeStruct
     vm, hbm = pl.BlockSpec(memory_space=pltpu.VMEM), pl.BlockSpec(memory_space=pl.ANY)
-    small = [shape((256, 1536), F32), shape((256, 512), F32), shape((4, 256), F32), shape((2, 2048), F32), shape((2, 512), F32),
-             shape(out.shape, out.dtype), shape(igrad.shape, igrad.dtype)] + [shape((256,), F32)] * 7
+    large = [shape((2, 512, 2048), F32), shape((2, 2048, 512), F32), shape((256, 1536), F32), shape((256, 512), F32),
+             shape(igrad.shape, igrad.dtype)]
+    small = [shape(out.shape, out.dtype), shape((4, 256), F32), shape((2, 2048), F32), shape((2, 512), F32)] + [shape((256,), F32)] * 7
     n = 8
     return pl.pallas_call(
         finish_kernel,
-        out_shape=[shape((2, 512, 2048), F32), shape((2, 2048, 512), F32)] + small,
-        in_specs=[hbm, vm, vm, vm],
-        out_specs=[hbm, hbm] + [vm] * len(small),
+        out_shape=large + small,
+        in_specs=[hbm, hbm, vm, hbm],
+        out_specs=[hbm] * len(large) + [vm] * len(small),
         scratch_shapes=[
             pltpu.VMEM((2 * n, STEP, 512), BF16), pltpu.VMEM((n, 512, STEP), F32), pltpu.VMEM((n, STEP, 512), F32),
-            pltpu.SemaphoreType.DMA((2 * n,)), pltpu.SemaphoreType.DMA((2 * n,)),
+            pltpu.VMEM(summed.shape, BF16), pltpu.VMEM((256, 1536), F32), pltpu.VMEM((256, 512), F32),
+            pltpu.VMEM(igrad.shape, igrad.dtype),
+            pltpu.SemaphoreType.DMA((2 * n,)), pltpu.SemaphoreType.DMA((2 * n,)), pltpu.SemaphoreType.DMA((5,)),
         ],
         compiler_params=pltpu.CompilerParams(vmem_limit_bytes=60 << 20),
         name="finish",
@@ -894,7 +913,7 @@
         lax.axis_size("replica") // 4, inputs, cotangent, noise.T, routes.T, priority, norm1_gain, norm1_bias, query_bias,
         value_bias, out_bias, norm2_gain, norm2_bias, router_weight.T, qkv_weight, out_weight, expert_in, expert_out,
         expert_in_bias, expert_out_bias)
-    grad_in, grad_out, qkv, proj, route, bias_in, bias_out, out, igrad, *cols = finish(grads, summed, out, igrad)
+    grad_in, grad_out, qkv, proj, igrad, out, route, bias_in, bias_out, *cols = finish(grads, summed, out, igrad)
     return (out, igrad, cols[0], cols[1], qkv, cols[2], cols[3], proj, cols[4], cols[5], cols[6], route.T,
             grad_in, bias_in, grad_out, bias_out)
 

time: 149 us -> 146 us (0.980)
  Pallas kernels: 148 us -> 145 us
    pallas_call x1, Pallas kernels: 136 us -> 134 us  [block_call(): pl.pallas_call(functools.partial(block_kernel, zs), out_shape=(shape((tok...]
where the time goes in v5:
time: 146 us
  Pallas kernels  145 us (99%)
    pallas_call x1, Pallas kernels, block_call(): pl.pallas_call(functools.partial(block_kernel, zs), out_shape=(shape((tok...  134 us
    pallas_call x1, Pallas kernels, finish(): pl.pallas_call(finish_kernel, out_shape=large + small, in_specs=[hbm, hbm...  11.3 us

profile of v5, /device:TPU:0, one launch (start us, length us, event | category | flops | bytes accessed | tf_op | source)
XLA Modules:
  0.0 146.0 jit_solution(5929243326794674194)
XLA Ops:
  0.7 134.0 %encoder_block.1 = (bf16[197,512]{1,0:T(8,128)(2,1)}, f32[197,512]{1,0:T(8,128)}, bf16[4,2048,512]{2,1,0:T(8,128)(2,1)}, bf16[272,2048]{1,0:T(8,128)(2,1)}) custom-call(bf16[197,512]{1,0:T(8,128)(2,1)} %refs_0_.1, bf16[197,512]{1,0:T(8,128)(2,1)} %refs_1_.1, f32[4,197]{1,0:T(4,128)} %bitcast.4, s32[2,197]{1,0:T(2,128)} %bitcast.5, s32[1,394]{1,0:T(1,128)} %refs_4_.1, ...), custom_call_target="tpu_custom_call" | custom-call | tf_op jit(solution)/shard_map/encoder_block/pallas_call | solution.py:810
  134.6 11.3 %finish.1 = (f32[2,512,2048]{2,1,0:T(8,128)}, f32[2,2048,512]{2,1,0:T(8,128)}, f32[256,1536]{1,0:T(8,128)}, f32[256,512]{1,0:T(8,128)}, f32[197,512]{1,0:T(8,128...) custom-call(bf16[4,2048,512]{2,1,0:T(8,128)(2,1)} %get-tuple-element, ...), custom_call_target="tpu_custom_call" | custom-call | tf_op jit(solution)/shard_map/finish/pallas_call | solution.py:890

commit v6 on v5

--- a/solution.py
+++ b/solution.py
@@ -784,9 +784,9 @@
     stages = {0: lambda: ar_stage_z(1), 3: lambda: ar_stage_z(2), 6: lambda: ar_stage_z(3), 8: ar_stage4, 11: ar_stage5}
 
     def last_ticks(t, _):
+        tick(t)
         for at, stage in stages.items():
             pl.when(t == start + at)(stage)
-        tick(t)
         return 0
 
     lax.fori_loop(start, ends, last_ticks, 0)

time: 146 us -> 148 us (1.014)
  Pallas kernels: 145 us -> 147 us
    pallas_call x1, Pallas kernels: 134 us -> 136 us  [block_call(): pl.pallas_call(functools.partial(block_kernel, zs), out_shape=(shape((tok...]
where the time goes in v6:
time: 148 us
  Pallas kernels  147 us (99%)
    pallas_call x1, Pallas kernels, block_call(): pl.pallas_call(functools.partial(block_kernel, zs), out_shape=(shape((tok...  136 us
    pallas_call x1, Pallas kernels, finish(): pl.pallas_call(finish_kernel, out_shape=large + small, in_specs=[hbm, hbm...  11.3 us

profile of v6, /device:TPU:0, one launch (start us, length us, event | category | flops | bytes accessed | tf_op | source)
XLA Modules:
  0.0 147.7 jit_solution(7624346059554759810)
XLA Ops:
  0.7 135.6 %encoder_block.1 = (bf16[197,512]{1,0:T(8,128)(2,1)}, f32[197,512]{1,0:T(8,128)}, bf16[4,2048,512]{2,1,0:T(8,128)(2,1)}, bf16[272,2048]{1,0:T(8,128)(2,1)}) custom-call(bf16[197,512]{1,0:T(8,128)(2,1)} %refs_0_.1, bf16[197,512]{1,0:T(8,128)(2,1)} %refs_1_.1, f32[4,197]{1,0:T(4,128)} %bitcast.4, s32[2,197]{1,0:T(2,128)} %bitcast.5, s32[1,394]{1,0:T(1,128)} %refs_4_.1, ...), custom_call_target="tpu_custom_call" | custom-call | tf_op jit(solution)/shard_map/encoder_block/pallas_call | solution.py:810
  136.3 11.3 %finish.1 = (f32[2,512,2048]{2,1,0:T(8,128)}, f32[2,2048,512]{2,1,0:T(8,128)}, f32[256,1536]{1,0:T(8,128)}, f32[256,512]{1,0:T(8,128)}, f32[197,512]{1,0:T(8,128...) custom-call(bf16[4,2048,512]{2,1,0:T(8,128)(2,1)} %get-tuple-element, ...), custom_call_target="tpu_custom_call" | custom-call | tf_op jit(solution)/shard_map/finish/pallas_call | solution.py:890
